TPU v7x, 32 devices: a whole 2x2x4 slice. The times are simulated.
32 devices in a mesh: dp: 4 (over x, core), row: 2 (over y), col: 4 (over z).
Axes of the slice: x: 2, y: 2, z: 4, core: 2. Of those that a mesh axis runs over, the one named last changes fastest.
Arguments:
- tokens: bfloat16 [16384, 1024], P(('dp', 'col'), 'row'), may hold values from -6 to 6
- segment_ids: int32 [16384], P(('dp', 'row')), may hold values from 0 to 302, as said below
- cotangent: bfloat16 [16384, 1024], P(('dp', 'col'), 'row'), may hold values from -6 to 6
- norm1_gain: bfloat16 [1024], P('row'), may hold values from 0.5 to 1.5
- in_weight: bfloat16 [1024, 3, 1024], P('row', None, 'col'), may hold values from -0.1875 to 0.1875
- conv_weight: bfloat16 [3, 1024], P(None, 'col'), may hold values from -3.5 to 3.5
- out_weight: bfloat16 [1024, 1024], P('col', 'row'), may hold values from -0.1875 to 0.1875
- norm2_gain: bfloat16 [1024], P('row'), may hold values from 0.5 to 1.5
- gate_weight: bfloat16 [1024, 4608], P('row', 'col'), may hold values from -0.1875 to 0.1875
- up_weight: bfloat16 [1024, 4608], P('row', 'col'), may hold values from -0.1875 to 0.1875
- down_weight: bfloat16 [4608, 1024], P('col', 'row'), may hold values from -0.09375 to 0.09375
Outputs:
- output: bfloat16 [16384, 1024], P(('dp', 'col'), 'row')
- input_grad: float32 [16384, 1024], P(('dp', 'col'), 'row')
- norm1_grad: float32 [1024], P('row')
- in_grad: float32 [1024, 3, 1024], P('row', None, 'col')
- conv_grad: float32 [3, 1024], P(None, 'col')
- out_grad: float32 [1024, 1024], P('col', 'row')
- norm2_grad: float32 [1024], P('row')
- gate_grad: float32 [1024, 4608], P('row', 'col')
- up_grad: float32 [1024, 4608], P('row', 'col')
- down_grad: float32 [4608, 1024], P('col', 'row')
Inputs may be any that keep to these rules, and one draw needn't show every extreme that they name: `segment_ids`: segment numbers never fall along the tokens; a run of one number never crosses a boundary between the sequences of 1024 tokens, and every run but a sequence's last has 60 to 800 tokens.
All inputs are finite; a program needn't handle non-finite values.
Results may differ from a plain program's by a relative error of at most 0.012.
Values may be sent and summed in bfloat16 or wider, within the bound.
No kernel may reach another device: no remote copies, remote signals or barrier semaphores. Data moves between devices by JAX's collectives and lax.ppermute only.
A program may use at most 256 MiB of HBM per device.

v0:
```python
import jax
import jax.numpy as jnp
from jax import lax
from jax.sharding import PartitionSpec as P

EPSILON = 1e-05


def token_rows(values):
    return lax.all_gather(values, "col", axis=0, tiled=True)


def block_rows(values):
    return lax.all_gather(values, "row", axis=0, tiled=True)


def row_totals(values):
    return lax.psum(values, "row")


def summed_over_row(left, right):
    return lax.psum_scatter(
        jnp.dot(left, right, preferred_element_type=jnp.float32),
        "row",
        scatter_dimension=0,
        tiled=True,
    )


def summed_over_col(left, right):
    return lax.psum_scatter(
        jnp.dot(left, right, preferred_element_type=jnp.float32),
        "col",
        scatter_dimension=0,
        tiled=True,
    )


def norm_forward(hidden, gain_vector):
    full_width = hidden.shape[1] * lax.axis_size("row")
    squares = row_totals(jnp.sum(hidden * hidden, axis=1, keepdims=True))
    row_scale = lax.rsqrt(squares / full_width + EPSILON)
    return ((hidden * row_scale * gain_vector).astype(jnp.bfloat16), row_scale)


def norm_backward(grad_normed, hidden, row_scale, gain_vector):
    full_width = hidden.shape[1] * lax.axis_size("row")
    inner_sum = row_totals(jnp.sum(grad_normed * gain_vector * hidden, axis=1, keepdims=True))
    cubed = row_scale * row_scale * row_scale
    grad_hidden = grad_normed * gain_vector * row_scale - hidden * (cubed / full_width) * inner_sum
    gain_grad = jnp.sum(grad_normed * hidden * row_scale, axis=0)
    return (grad_hidden, gain_grad)


def same_segment(segments, offset):
    equal = (segments[offset:] == segments[:-offset]).astype(jnp.float32)
    return jnp.concatenate([jnp.zeros((offset,), jnp.float32), equal])[:, None]


def shifted(values, offset):
    filler = jnp.zeros((offset,) + values.shape[1:], values.dtype)
    return jnp.concatenate([filler, values[:-offset]], axis=0)


def advanced(values, offset):
    filler = jnp.zeros((offset,) + values.shape[1:], values.dtype)
    return jnp.concatenate([values[offset:], filler], axis=0)


def body(
    tokens,
    segment_ids,
    cotangent,
    norm1_gain,
    in_weight,
    conv_weight,
    out_weight,
    norm2_gain,
    gate_weight,
    up_weight,
    down_weight,
):
    mid_width = in_weight.shape[2]
    ffn_width = gate_weight.shape[1]
    inputs = tokens.astype(jnp.float32)
    row_width = inputs.shape[1]
    gain_one = norm1_gain.astype(jnp.float32)
    gain_two = norm2_gain.astype(jnp.float32)
    conv_taps = conv_weight.astype(jnp.float32)
    flat_in = in_weight.reshape(in_weight.shape[0], 3 * mid_width)
    normed_one, scale_one = norm_forward(inputs, gain_one)
    rows_one = token_rows(normed_one)
    projected = summed_over_row(rows_one, flat_in)
    input_gate = projected[:, :mid_width]
    output_gate = projected[:, mid_width : 2 * mid_width]
    values_part = projected[:, 2 * mid_width :]
    mix_input = input_gate * values_part
    keep_one = same_segment(segment_ids, 1)
    keep_two = same_segment(segment_ids, 2)
    prior_one = keep_one * shifted(mix_input, 1)
    prior_two = keep_two * shifted(mix_input, 2)
    convolved = conv_taps[2] * mix_input + conv_taps[1] * prior_one + conv_taps[0] * prior_two
    mixed_value = (output_gate * convolved).astype(jnp.bfloat16)
    mixed_rows = block_rows(mixed_value)
    hidden_one = inputs + summed_over_col(mixed_rows, out_weight)
    normed_two, scale_two = norm_forward(hidden_one, gain_two)
    rows_two = token_rows(normed_two)
    paired_weight = jnp.concatenate([gate_weight, up_weight], axis=1)
    paired_value = summed_over_row(rows_two, paired_weight)
    gate_value = paired_value[:, :ffn_width]
    up_value = paired_value[:, ffn_width:]
    sigmoid_gate = jax.nn.sigmoid(gate_value)
    activated = (gate_value * sigmoid_gate * up_value).astype(jnp.bfloat16)
    activated_rows = block_rows(activated)
    result_value = hidden_one + summed_over_col(activated_rows, down_weight)
    cotangent_rows = token_rows(cotangent)
    down_grad = jnp.dot(activated_rows.T, cotangent_rows, preferred_element_type=jnp.float32)
    grad_act = summed_over_row(cotangent_rows, down_weight.T)
    grad_gate = grad_act * up_value * sigmoid_gate * (1.0 + gate_value * (1.0 - sigmoid_gate))
    grad_up = grad_act * gate_value * sigmoid_gate
    grad_paired = jnp.concatenate([grad_gate, grad_up], axis=1).astype(jnp.bfloat16)
    paired_rows = block_rows(grad_paired)
    paired_grad = jnp.dot(rows_two.T, paired_rows, preferred_element_type=jnp.float32)
    grad_normed_two = summed_over_col(paired_rows, paired_weight.T)
    grad_two, gain_grad_two = norm_backward(grad_normed_two, hidden_one, scale_two, gain_two)
    grad_hidden = cotangent.astype(jnp.float32) + grad_two
    grad_rows = token_rows(grad_hidden.astype(jnp.bfloat16))
    out_grad = jnp.dot(mixed_rows.T, grad_rows, preferred_element_type=jnp.float32)
    grad_mixed = summed_over_row(grad_rows, out_weight.T)
    grad_convolved = grad_mixed * output_gate
    grad_output_gate = grad_mixed * convolved
    conv_local = jnp.stack(
        [
            jnp.sum(grad_convolved * prior_two, axis=0),
            jnp.sum(grad_convolved * prior_one, axis=0),
            jnp.sum(grad_convolved * mix_input, axis=0),
        ]
    )
    grad_mix_input = (
        conv_taps[2] * grad_convolved
        + conv_taps[1] * advanced(keep_one * grad_convolved, 1)
        + conv_taps[0] * advanced(keep_two * grad_convolved, 2)
    )
    grad_projected = jnp.concatenate(
        [grad_mix_input * values_part, grad_output_gate, grad_mix_input * input_gate], axis=1
    ).astype(jnp.bfloat16)
    projected_rows = block_rows(grad_projected)
    in_grad = jnp.dot(rows_one.T, projected_rows, preferred_element_type=jnp.float32).reshape(
        in_weight.shape
    )
    grad_normed_one = summed_over_col(projected_rows, flat_in.T)
    grad_one, gain_grad_one = norm_backward(grad_normed_one, inputs, scale_one, gain_one)
    input_grad = grad_hidden + grad_one
    in_total, out_total, paired_total, down_total = (
        lax.psum(in_grad.astype(jnp.bfloat16), "dp").astype(jnp.float32),
        lax.psum(out_grad.astype(jnp.bfloat16), "dp").astype(jnp.float32),
        lax.psum(paired_grad.astype(jnp.bfloat16), "dp").astype(jnp.float32),
        lax.psum(down_grad.astype(jnp.bfloat16), "dp").astype(jnp.float32),
    )
    conv_wide = lax.dynamic_update_slice(
        jnp.zeros((3, mid_width * lax.axis_size("col")), jnp.float32),
        conv_local,
        (0, lax.axis_index("col") * mid_width),
    )
    gain_local = jnp.stack([gain_grad_one, gain_grad_two])
    gain_wide = lax.dynamic_update_slice(
        jnp.zeros((2, row_width * lax.axis_size("row")), jnp.float32),
        gain_local,
        (0, lax.axis_index("row") * row_width),
    )
    conv_sum, gain_sum = lax.psum((conv_wide, gain_wide), ("dp", "row", "col"))
    conv_grad = lax.dynamic_slice_in_dim(conv_sum, lax.axis_index("col") * mid_width, mid_width, 1)
    gain_block = lax.dynamic_slice_in_dim(gain_sum, lax.axis_index("row") * row_width, row_width, 1)
    gate_grad = paired_total[:, :ffn_width]
    up_grad = paired_total[:, ffn_width:]
    return (
        result_value.astype(jnp.bfloat16),
        input_grad,
        gain_block[0],
        in_total,
        conv_grad,
        out_total,
        gain_block[1],
        gate_grad,
        up_grad,
        down_total,
    )


def solution(mesh):
    return jax.shard_map(
        body,
        mesh=mesh,
        in_specs=(
            P(("dp", "col"), "row"),
            P(("dp", "row")),
            P(("dp", "col"), "row"),
            P("row"),
            P("row", None, "col"),
            P(None, "col"),
            P("col", "row"),
            P("row"),
            P("row", "col"),
            P("row", "col"),
            P("col", "row"),
        ),
        out_specs=(
            P(("dp", "col"), "row"),
            P(("dp", "col"), "row"),
            P("row"),
            P("row", None, "col"),
            P(None, "col"),
            P("col", "row"),
            P("row"),
            P("row", "col"),
            P("row", "col"),
            P("col", "row"),
        ),
        check_vma=False,
    )
```

profile of v0, /device:TPU:0, one launch (start us, length us, event | category | flops | bytes accessed | tf_op | source)
XLA Modules:
  0.0 2440.9 jit_solution(6228563064661299590)
XLA Ops:
  19.5 82.3 %all-gather.9.cloned.1.call-done = bf16[4096,512]{1,0:T(8,128)(2,1)} async-done(((bf16[1024,512]{1,0:T(8,128)(2,1)}), bf16[4096,512]{1,0:T(8,128)(2,1)}) %all-gather.9.cloned.1.call-update) | async-done | bytes 4194320 | tf_op jit(solution)/shard_map/all_gather | solution.py:10
  113.0 142.3 %reduce-scatter.9.cloned.1.call-done = f32[2048,768]{1,0:T(8,128)} async-done(((f32[4096,768]{1,0:T(8,128)}), f32[2048,768]{1,0:T(8,128)}) %reduce-scatter.9.cloned.1.call-update) | async-done | bytes 6291472 | tf_op jit(solution)/shard_map/reduce_scatter | solution.py:22
  262.7 33.2 %all-gather.11.cloned.1.call-done = bf16[4096,256]{1,0:T(8,128)(2,1)} async-done(((bf16[2048,256]{1,0:T(8,128)(2,1)}), bf16[4096,256]{1,0:T(8,128)(2,1)}) %all-gather.11.cloned.1.call-update) | async-done | bytes 2097168 | tf_op jit(solution)/shard_map/all_gather | solution.py:14
  303.3 143.4 %reduce-scatter.11.cloned.1.call-done = f32[1024,512]{1,0:T(8,128)} async-done(((f32[4096,512]{1,0:T(8,128)}), f32[1024,512]{1,0:T(8,128)}) %reduce-scatter.11.cloned.1.call-update) | async-done | bytes 2097168 | tf_op jit(solution)/shard_map/reduce_scatter | solution.py:31
  459.0 70.7 %all-gather.17.cloned.1.call-done = bf16[4096,512]{1,0:T(8,128)(2,1)} async-done(((bf16[1024,512]{1,0:T(8,128)(2,1)}), bf16[4096,512]{1,0:T(8,128)(2,1)}) %all-gather.17.cloned.1.call-update) | async-done | bytes 4194320 | tf_op jit(solution)/shard_map/all_gather | solution.py:10
  529.6 12.3 fusion.19
  545.9 65.0 %all-gather.13.cloned.1.call-done = bf16[4096,512]{1,0:T(8,128)(2,1)} async-done(((bf16[1024,512]{1,0:T(8,128)(2,1)}), bf16[4096,512]{1,0:T(8,128)(2,1)}) %all-gather.13.cloned.1.call-update) | async-done | bytes 4194320 | tf_op jit(solution)/shard_map/all_gather | solution.py:10
  611.0 19.8 fusion.17
  630.8 192.7 %reduce-scatter.17.cloned.1.call-done = f32[2048,1152]{1,0:T(8,128)} async-done(((f32[4096,1152]{1,0:T(8,128)}), f32[2048,1152]{1,0:T(8,128)}) %reduce-scatter.17.cloned.1.call-update) | async-done | bytes 9437200 | tf_op jit(solution)/shard_map/reduce_scatter | solution.py:22
  823.5 416.2 %reduce-scatter.13.cloned.1.call-done = f32[2048,2304]{1,0:T(8,128)} async-done(((f32[4096,2304]{1,0:T(8,128)}), f32[2048,2304]{1,0:T(8,128)}) %reduce-scatter.13.cloned.1.call-update) | async-done | bytes 18874384 | tf_op jit(solution)/shard_map/reduce_scatter | solution.py:22
  1239.7 13.5 multiply_convert_fusion.1
  1258.6 223.9 %all-gather.19.cloned.1.call-done = bf16[4096,2304]{1,0:T(8,128)(2,1)} async-done(((bf16[2048,2304]{1,0:T(8,128)(2,1)}), bf16[4096,2304]{1,0:T(8,128)(2,1)}) %all-gather.19.cloned.1.call-update) | async-done | bytes 18874384 | tf_op jit(solution)/shard_map/all_gather | solution.py:14
  1482.4 16.5 fusion.20
  1499.6 102.3 %all-gather.15.cloned.1.call-done = bf16[4096,1152]{1,0:T(8,128)(2,1)} async-done(((bf16[2048,1152]{1,0:T(8,128)(2,1)}), bf16[4096,1152]{1,0:T(8,128)(2,1)}) %all-gather.15.cloned.1.call-update) | async-done | bytes 9437200 | tf_op jit(solution)/shard_map/all_gather | solution.py:14
  1601.9 11.7 fusion.18
  1613.6 135.1 %reduce-scatter.19.cloned.1.call-done = f32[1024,512]{1,0:T(8,128)} async-done(((f32[4096,512]{1,0:T(8,128)}), f32[1024,512]{1,0:T(8,128)}) %reduce-scatter.19.cloned.1.call-update) | async-done | bytes 2097168 | tf_op jit(solution)/shard_map/reduce_scatter | solution.py:31
  1757.2 139.0 %reduce-scatter.15.cloned.1.call-done = f32[1024,512]{1,0:T(8,128)} async-done(((f32[4096,512]{1,0:T(8,128)}), f32[1024,512]{1,0:T(8,128)}) %reduce-scatter.15.cloned.1.call-update) | async-done | bytes 2097168 | tf_op jit(solution)/shard_map/reduce_scatter | solution.py:31
  1900.5 81.6 %all-gather.21.cloned.1.call-done = bf16[4096,512]{1,0:T(8,128)(2,1)} async-done(((bf16[1024,512]{1,0:T(8,128)(2,1)}), bf16[4096,512]{1,0:T(8,128)(2,1)}) %all-gather.21.cloned.1.call-update) | async-done | bytes 4194320 | tf_op jit(solution)/shard_map/all_gather | solution.py:10
  1987.9 52.8 %reduce-scatter.21.cloned.1.call-done = f32[2048,256]{1,0:T(8,128)} async-done(((f32[4096,256]{1,0:T(8,128)}), f32[2048,256]{1,0:T(8,128)}) %reduce-scatter.21.cloned.1.call-update) | async-done | bytes 2097168 | tf_op jit(solution)/shard_map/reduce_scatter | solution.py:22
  2061.9 17.0 convolution_convert_fusion
  2080.9 50.7 %all-gather.23.cloned.1.call-done = bf16[4096,768]{1,0:T(8,128)(2,1)} async-done(((bf16[2048,768]{1,0:T(8,128)(2,1)}), bf16[4096,768]{1,0:T(8,128)(2,1)}) %all-gather.23.cloned.1.call-update) | async-done | bytes 6291472 | tf_op jit(solution)/shard_map/all_gather | solution.py:14
  2150.0 82.9 %all-reduce.9.cloned.1.call-done = (bf16[512,3,256]{0,2,1:T(8,128)(2,1)}, bf16[512,2304]{1,0:T(8,128)(2,1)}, bf16[256,512]{1,0:T(8,128)(2,1)}, bf16[1152,512]{1,0:T(8,128)(2,1)}) async-done(((bf16[512,3,256]{0,2,1:T(8,128)(2,1)}, bf16[512,2304]{1,0:T(8,128)(2,1)}, bf16[256,512]{1,0:T(8,128)(2,1)}, bf16[1152,512]{1,0:T(8,128)(2,1)}), (bf16[512,3,256]{0,2,1:T(8,128)(2,1)}, bf16[512,2304]{1,0:T(8,128)(2,1)}, ...) | async-done | bytes 4587536 | tf_op jit(solution)/shard_map/psum | solution.py:155
  2242.7 137.2 %reduce-scatter.23.cloned.1.call-done = f32[1024,512]{1,0:T(8,128)} async-done(((f32[4096,512]{1,0:T(8,128)}), f32[1024,512]{1,0:T(8,128)}) %reduce-scatter.23.cloned.1.call-update) | async-done | bytes 2097168 | tf_op jit(solution)/shard_map/reduce_scatter | solution.py:31
  2382.4 41.3 %all-reduce.5 = (f32[2,1024]{1,0:T(2,128)S(1)}, f32[3,1024]{1,0:T(4,128)S(1)}) all-reduce(f32[2,1024]{1,0:T(2,128)S(1)} %maximum_dynamic-update-slice_fusion, f32[3,1024]{1,0:T(4,128)S(1)} %maximum_dynamic-update-slice_fusion.1), channel_id=1, replica_groups=mesh['dp'=4,'row'=2,'col'=4] {'dp','row','col'}, use_global_device_ids=true, to_apply=%region_18.0 | all-reduce | flops 5120 | bytes 40960 | tf_op jit(solution)/shard_map/psum | solution.py:171
  (151 shorter events, 143.0 us)
Async XLA Ops:
  7.2 522.5 %copy-start = (bf16[1152,512]{1,0:T(8,128)(2,1)S(1)}, bf16[1152,512]{1,0:T(8,128)(2,1)}, u32[]{:S(2)}) copy-start(bf16[1152,512]{1,0:T(8,128)(2,1)} %param.21) | copy-start | bytes 3538948
  7.2 94.7 %all-gather.9.cloned.1.call-start = ((), (), s32[]{:S(2)}) async-start(), calls=%async_computation.8 | async-start | bytes 5242880 | tf_op jit(solution)/shard_map/all_gather | solution.py:10
  19.2 236.1 %reduce-scatter.9.cloned.1.call-start = ((), (), s32[]{:S(2)}) async-start(), calls=%async_computation.9 | async-start | bytes 18874368 | tf_op jit(solution)/shard_map/reduce_scatter | solution.py:22
  112.1 183.8 %all-gather.11.cloned.1.call-start = ((), (), s32[]{:S(2)}) async-start(), calls=%async_computation.10 | async-start | bytes 3145728 | tf_op jit(solution)/shard_map/all_gather | solution.py:14
  113.0 145.0 %copy-start.20 = (f32[1,256]{1,0:T(1,128)}, f32[1,256]{1,0:T(1,128)S(1)}, u32[]{:S(2)}) copy-start(f32[1,256]{1,0:T(1,128)S(1)} %get-tuple-element.55) | copy-start | bytes 3076
  113.0 145.0 %copy-start.22 = (f32[1,256]{1,0:T(1,128)}, f32[1,256]{1,0:T(1,128)S(1)}, u32[]{:S(2)}) copy-start(f32[1,256]{1,0:T(1,128)S(1)} %get-tuple-element.56) | copy-start | bytes 3076
  113.0 145.0 %copy-start.24 = (f32[1,256]{1,0:T(1,128)}, f32[1,256]{1,0:T(1,128)S(1)}, u32[]{:S(2)}) copy-start(f32[1,256]{1,0:T(1,128)S(1)} %get-tuple-element.57) | copy-start | bytes 3076
  262.6 184.1 %reduce-scatter.11.cloned.1.call-start = ((), (), s32[]{:S(2)}) async-start(), calls=%async_computation.11 | async-start | bytes 10485760 | tf_op jit(solution)/shard_map/reduce_scatter | solution.py:31
  302.0 227.6 %all-gather.17.cloned.1.call-start = ((), (), s32[]{:S(2)}) async-start(), calls=%async_computation.16 | async-start | bytes 5242880 | tf_op jit(solution)/shard_map/all_gather | solution.py:10
  302.6 308.3 %all-gather.13.cloned.1.call-start = ((), (), s32[]{:S(2)}) async-start(), calls=%async_computation.12 | async-start | bytes 5242880 | tf_op jit(solution)/shard_map/all_gather | solution.py:10
  458.9 364.6 %reduce-scatter.17.cloned.1.call-start = ((), (), s32[]{:S(2)}) async-start(), calls=%async_computation.17 | async-start | bytes 28311552 | tf_op jit(solution)/shard_map/reduce_scatter | solution.py:22
  542.0 697.7 %reduce-scatter.13.cloned.1.call-start = ((), (), s32[]{:S(2)}) async-start(), calls=%async_computation.13 | async-start | bytes 56623104 | tf_op jit(solution)/shard_map/reduce_scatter | solution.py:22
  630.8 851.7 %all-gather.19.cloned.1.call-start = ((), (), s32[]{:S(2)}) async-start(), calls=%async_computation.18 | async-start | bytes 28311552 | tf_op jit(solution)/shard_map/all_gather | solution.py:14
  1257.9 344.0 %all-gather.15.cloned.1.call-start = ((), (), s32[]{:S(2)}) async-start(), calls=%async_computation.14 | async-start | bytes 14155776 | tf_op jit(solution)/shard_map/all_gather | solution.py:14
  1258.5 490.2 %reduce-scatter.19.cloned.1.call-start = ((), (), s32[]{:S(2)}) async-start(), calls=%async_computation.19 | async-start | bytes 10485760 | tf_op jit(solution)/shard_map/reduce_scatter | solution.py:31
  1499.0 397.2 %reduce-scatter.15.cloned.1.call-start = ((), (), s32[]{:S(2)}) async-start(), calls=%async_computation.15 | async-start | bytes 10485760 | tf_op jit(solution)/shard_map/reduce_scatter | solution.py:31
  1613.6 368.6 %all-gather.21.cloned.1.call-start = ((), (), s32[]{:S(2)}) async-start(), calls=%async_computation.20 | async-start | bytes 5242880 | tf_op jit(solution)/shard_map/all_gather | solution.py:10
  1900.5 140.2 %reduce-scatter.21.cloned.1.call-start = ((), (), s32[]{:S(2)}) async-start(), calls=%async_computation.21 | async-start | bytes 6291456 | tf_op jit(solution)/shard_map/reduce_scatter | solution.py:22
  1987.7 143.9 %all-gather.23.cloned.1.call-start = ((), (), s32[]{:S(2)}) async-start(), calls=%async_computation.22 | async-start | bytes 9437184 | tf_op jit(solution)/shard_map/all_gather | solution.py:14
  2051.1 181.9 %all-reduce.9.cloned.1.call-start = ((), (), s32[]{:S(2)}) async-start(), calls=%async_computation.24 | async-start | bytes 9175040 | tf_op jit(solution)/shard_map/psum | solution.py:155
  2140.3 239.6 %reduce-scatter.23.cloned.1.call-start = ((), (), s32[]{:S(2)}) async-start(), calls=%async_computation.23 | async-start | bytes 10485760 | tf_op jit(solution)/shard_map/reduce_scatter | solution.py:31
  2238.3 141.6 %copy-start.16 = (f32[1024,1]{0,1:T(1,128)S(1)}, f32[1024,1]{0,1:T(1,128)}, u32[]{:S(2)}) copy-start(f32[1024,1]{0,1:T(1,128)} %copy-done.15) | copy-start | bytes 12292
  2238.3 141.6 %copy-start.18 = (f32[512]{0:T(512)S(1)}, f32[512]{0:T(512)}, u32[]{:S(2)}) copy-start(f32[512]{0:T(512)} %copy-done.17) | copy-start | bytes 6148
  2242.7 187.4 %copy-start.19 = (f32[1024,1]{0,1:T(1,128)S(1)}, f32[1024,1]{0,1:T(1,128)}, u32[]{:S(2)}) copy-start(f32[1024,1]{0,1:T(1,128)} %get-tuple-element.34) | copy-start | bytes 12292
  (25 other events, 565.4 us)
Sparse Core Ops, SparseCore 0:
  19.3 82.5 all-gather.8
  112.2 143.0 reduce-scatter.8
  262.7 33.1 all-gather.10
  302.2 144.4 reduce-scatter.10
  448.1 81.4 all-gather.16
  531.6 79.2 all-gather.12
  613.3 210.2 reduce-scatter.16
  825.8 413.8 reduce-scatter.12
  1258.0 224.3 all-gather.18
  1483.8 117.9 all-gather.14
  1604.2 144.4 reduce-scatter.18
  1751.0 145.1 reduce-scatter.14
  1900.6 81.4 all-gather.20
  1987.9 52.8 reduce-scatter.20
  2051.2 80.3 all-gather.22
  2140.4 92.4 all-reduce.8
  2235.2 144.5 reduce-scatter.22
where the time goes:
time: 2450 us; the launch traced here: 2440 us
  waiting for transfers between devices  2150 us (88%)
  matrix products  128 us (5%)
  blocking collectives  63.6 us (3%)
  other arithmetic  63 us (3%)
    reduce_scatter x4, waiting for transfers between devices, summed_over_row(): lax.psum_scatter(jnp.dot(left, right, preferred_element_type=jnp.float32)...  804 us
    reduce_scatter x4, waiting for transfers between devices, summed_over_col(): lax.psum_scatter(jnp.dot(left, right, preferred_element_type=jnp.float32)...  555 us
    all_gather x4, waiting for transfers between devices, block_rows(): return lax.all_gather(values, 'row', axis=0, tiled=True)  410 us
    all_gather x4, waiting for transfers between devices, token_rows(): return lax.all_gather(values, 'col', axis=0, tiled=True)  300 us
    psum x1, waiting for transfers between devices, body(): lax.psum(in_grad.astype(jnp.bfloat16), 'dp').astype(jnp.float32)  82.9 us
  transfers between devices with their start and end apart: 17, of which 17 were waited for; matrix products, arithmetic and copies ran while one was open for 5% of the time, Pallas kernels for 0%

commit v1 on v0

v1 whole, which is shorter than its diff:
```python
import jax
import jax.numpy as jnp
from jax import lax
from jax.sharding import PartitionSpec as P

EPSILON = 1e-05
TEAM = 4


def dot_nt(left, right):
    return lax.dot_general(left, right, (((1,), (1,)), ((), ())), preferred_element_type=jnp.float32)


def dot_nn(left, right):
    return lax.dot_general(left, right, (((1,), (0,)), ((), ())), preferred_element_type=jnp.float32)


def dot_tn(left, right):
    return lax.dot_general(left, right, (((0,), (0,)), ((), ())), preferred_element_type=jnp.float32)


def over_dp(values, distance):
    size = lax.axis_size("dp")
    return lax.ppermute(values, "dp", [(i, i ^ distance) for i in range(size)])


def over_core(values):
    return over_dp(values, 1)


def over_x(values):
    return over_dp(values, 2)


def over_row(values):
    return lax.ppermute(values, "row", [(0, 1), (1, 0)])


def over_col(values, shift):
    size = lax.axis_size("col")
    return lax.ppermute(values, "col", [(i, (i + shift) % size) for i in range(size)])


def col_swap(values, distance):
    size = lax.axis_size("col")
    return lax.ppermute(values, "col", [(i, i ^ distance) for i in range(size)])


def narrow(values):
    return values.astype(jnp.bfloat16)


def wide(values):
    return values.astype(jnp.float32)


def halves(values):
    size = values.shape[0] // 2
    return values[:size], values[size:]


def other_teams(values):
    distance = TEAM
    while distance < lax.axis_size("dp"):
        values = values + over_dp(values, distance)
        distance *= 2
    return values


def gather_pieces(piece, parts):
    cols = lax.axis_size("col")
    pieces = [piece] + [over_col(piece, shift) for shift in range(1, cols)]
    rows = piece.shape[0] // parts
    stacked = jnp.concatenate(
        [one[part * rows : (part + 1) * rows] for part in range(parts) for one in pieces], axis=0
    )
    return jnp.concatenate([stacked, over_row(stacked)], axis=1)


def scatter_pieces(partial, parts):
    cols = lax.axis_size("col")
    half = partial.shape[1] // 2
    mine = partial[:, :half] + wide(over_row(narrow(partial[:, half:])))
    rows = partial.shape[0] // (parts * cols)
    grid = mine.reshape(parts, cols, rows, half)
    total = grid[:, 0].reshape(parts * rows, half)
    for shift in range(1, cols):
        total = total + wide(over_col(narrow(grid[:, shift].reshape(parts * rows, half)), -shift))
    return total


def team_rows(piece, parts):
    rows, half = piece.shape[0] // parts, piece.shape[1]
    own = narrow(other_teams(piece)).reshape(parts, rows, half)
    far = over_x(own)
    pair = over_core(jnp.stack([own, far]))
    place = lax.axis_index("dp") % TEAM
    blocks = [own, pair[0], far, pair[1]]
    result = jnp.zeros((parts, TEAM * rows, half), jnp.bfloat16)
    for distance, block in enumerate(blocks):
        result = lax.dynamic_update_slice(result, block, (0, (place ^ distance) * rows, 0))
    return result


def norm_scale(hidden):
    return lax.rsqrt(jnp.mean(hidden * hidden, axis=1, keepdims=True) + EPSILON)


def norm_backward(grad_normed, hidden, row_scale, gain_vector):
    inner_sum = jnp.sum(grad_normed * gain_vector * hidden, axis=1, keepdims=True)
    cubed = row_scale * row_scale * row_scale
    return grad_normed * gain_vector * row_scale - hidden * (cubed / hidden.shape[1]) * inner_sum


def to_own_tokens(block):
    size = block.shape[0] // 2
    row = lax.axis_index("row")
    own = lax.dynamic_slice_in_dim(block, row * size, size, 0)
    other = lax.dynamic_slice_in_dim(block, (1 - row) * size, size, 0)
    received = over_row(other)
    far_own, far_received = over_x(own), over_x(received)
    near = jnp.concatenate([own, received], axis=1)
    far = jnp.concatenate([far_own, far_received], axis=1)
    both = over_core(jnp.stack([near, far]))
    return (near, both[0]), (far, both[1])


def to_blocks(values, dtype):
    half = values.shape[1] // 2
    size = values.shape[0]
    row = lax.axis_index("row")
    received = over_row(narrow(values[:, half:])).astype(dtype)
    result = jnp.zeros((2 * size, half), dtype)
    result = lax.dynamic_update_slice(result, values[:, :half].astype(dtype), (row * size, 0))
    return lax.dynamic_update_slice(result, received, ((1 - row) * size, 0))


def body(
    tokens,
    segment_ids,
    cotangent,
    norm1_gain,
    in_weight,
    conv_weight,
    out_weight,
    norm2_gain,
    gate_weight,
    up_weight,
    down_weight,
):
    place = lax.axis_index("dp") % TEAM
    row = lax.axis_index("row")
    col = lax.axis_index("col")
    cols = lax.axis_size("col")
    sequence = tokens.shape[0]
    size = sequence // 2
    half = tokens.shape[1]

    channels = in_weight.shape[2] // TEAM
    hidden = gate_weight.shape[1] // TEAM
    in_part = lax.dynamic_slice_in_dim(in_weight, place * channels, channels, 2)
    in_part = in_part.transpose(1, 2, 0).reshape(3 * channels, half)
    out_part = lax.dynamic_slice_in_dim(out_weight, place * channels, channels, 0)
    gate_part = lax.dynamic_slice_in_dim(gate_weight, place * hidden, hidden, 1).T
    up_part = lax.dynamic_slice_in_dim(up_weight, place * hidden, hidden, 1).T
    down_part = lax.dynamic_slice_in_dim(down_weight, place * hidden, hidden, 0)
    taps_part = lax.dynamic_slice_in_dim(conv_weight, place * channels, channels, 1)

    near_tokens, far_tokens = to_own_tokens(tokens)
    mixer = gather_pieces(jnp.concatenate([in_part, out_part], axis=0), 4)
    in_rows, out_rows = mixer[: 3 * cols * channels], mixer[3 * cols * channels :]
    taps = jnp.concatenate([taps_part] + [over_col(taps_part, shift) for shift in range(1, cols)], axis=1)
    taps = wide(taps)
    gains = jnp.stack([norm1_gain, norm2_gain])
    gains = wide(jnp.concatenate([gains, over_row(gains)], axis=1))
    gain_one, gain_two = gains[0], gains[1]

    ids = jnp.stack([segment_ids, over_row(segment_ids)])
    ids = lax.dynamic_index_in_dim(ids, (col // 2) ^ row, 0, keepdims=False)
    ids = lax.dynamic_slice_in_dim(ids, (col % 2) * sequence, sequence, 0)
    ids_far = over_x(ids)
    ids_pair = over_core(jnp.stack([ids, ids_far]))
    ids = jnp.stack([ids, ids_pair[0], ids_far, ids_pair[1]])
    keeps = []
    for offset in (1, 2):
        equal = (ids[:, offset:] == ids[:, :-offset]).astype(jnp.float32)
        keeps.append(jnp.pad(equal, ((0, 0), (offset, offset))))
    keep_one = lax.dynamic_slice_in_dim(keeps[0], row * size, size, 1)[:, :, None]
    keep_two = lax.dynamic_slice_in_dim(keeps[1], row * size, size, 1)[:, :, None]
    next_one = lax.dynamic_slice_in_dim(keeps[0], row * size + 1, size, 1)[:, :, None]
    next_two = lax.dynamic_slice_in_dim(keeps[1], row * size + 2, size, 1)[:, :, None]
    keep_one, keep_two, next_one, next_two = (
        (flags[:2], flags[2:]) for flags in (keep_one, keep_two, next_one, next_two)
    )

    gate_rows = gather_pieces(gate_part, 1)
    up_rows = gather_pieces(up_part, 1)
    down_rows = gather_pieces(down_part, 1)
    near_grads, far_grads = to_own_tokens(cotangent)

    width = cols * channels
    inputs = [jnp.concatenate(pair, axis=0) for pair in (near_tokens, far_tokens)]
    normed_one, scale_one, mixed, saved = [], [], [], []
    for pair in (0, 1):
        values = wide(inputs[pair])
        scale = norm_scale(values)
        scale_one.append(scale)
        normed_one.append(narrow(values * scale * gain_one))
    for pair in (0, 1):
        projected = dot_nt(normed_one[pair], in_rows).reshape(2, size, 3 * width)
        input_gate, output_gate, values_part = (
            projected[:, :, :width],
            projected[:, :, width : 2 * width],
            projected[:, :, 2 * width :],
        )
        mix_input = input_gate * values_part
        before = over_row(mix_input[:, size - 2 :])
        extended = jnp.concatenate([before, mix_input], axis=1)
        prior_one = keep_one[pair] * extended[:, 1 : size + 1]
        prior_two = keep_two[pair] * extended[:, :size]
        convolved = taps[2] * mix_input + taps[1] * prior_one + taps[0] * prior_two
        mixed.append(narrow(output_gate * convolved).reshape(2 * size, width))
        saved.append((input_gate, output_gate, values_part, mix_input, prior_one, prior_two, convolved))

    far_sum = dot_nn(mixed[1], out_rows)
    far_sum = far_sum[:size] + wide(over_core(narrow(far_sum[size:])))
    from_far = over_x(narrow(far_sum))
    near_sum = dot_nn(mixed[0], out_rows)
    near_sum = near_sum[:size] + wide(over_core(narrow(near_sum[size:])))
    to_far = over_x(narrow(near_sum))
    hidden_near = wide(near_tokens[0]) + (near_sum + wide(from_far))
    hidden_far = wide(far_tokens[0]) + (far_sum + wide(to_far))

    hiddens, scale_two, normed_two = (hidden_near, hidden_far), [], []
    for values in hiddens:
        scale = norm_scale(values)
        scale_two.append(scale)
        normed = narrow(values * scale * gain_two)
        normed_two.append(jnp.concatenate([normed, over_core(normed)], axis=0))

    cotangents = [jnp.concatenate(pair, axis=0) for pair in (near_grads, far_grads)]
    act, grad_gate, grad_up, back = [], [], [], []
    for pair in (0, 1):
        gate_value = dot_nt(normed_two[pair], gate_rows)
        up_value = dot_nt(normed_two[pair], up_rows)
        grad_act = dot_nt(cotangents[pair], down_rows)
        sigmoid_gate = jax.nn.sigmoid(gate_value)
        silu = gate_value * sigmoid_gate
        act.append(narrow(silu * up_value))
        grad_gate.append(narrow(grad_act * up_value * sigmoid_gate * (1.0 + gate_value * (1.0 - sigmoid_gate))))
        grad_up.append(narrow(grad_act * silu))
        back.append(dot_nn(grad_gate[pair], gate_rows) + dot_nn(grad_up[pair], up_rows))
        if pair == 0:
            near_back = back[0][:size] + wide(over_core(narrow(back[0][size:])))
            back_to_far = over_x(narrow(near_back))
    far_back = back[1][:size] + wide(over_core(narrow(back[1][size:])))
    back_from_far = over_x(narrow(far_back))

    down_total = scatter_pieces(dot_tn(act[0], cotangents[0]) + dot_tn(act[1], cotangents[1]), 1)
    gate_total = scatter_pieces(
        dot_tn(grad_gate[0], normed_two[0]) + dot_tn(grad_gate[1], normed_two[1]), 1
    )
    up_total = scatter_pieces(dot_tn(grad_up[0], normed_two[0]) + dot_tn(grad_up[1], normed_two[1]), 1)

    far_out = dot_nn(act[1], down_rows)
    far_out = far_out[:size] + wide(over_core(narrow(far_out[size:])))
    out_from_far = over_x(narrow(far_out))
    near_out = dot_nn(act[0], down_rows)
    near_out = near_out[:size] + wide(over_core(narrow(near_out[size:])))
    result = narrow(hidden_near + (near_out + wide(out_from_far)))

    back_sums = (near_back + wide(back_from_far), far_back + wide(back_to_far))
    grad_hidden, grad_mixed = [], []
    for which, cotangent_rows in ((0, near_grads[0]), (1, far_grads[0])):
        grads = wide(cotangent_rows) + norm_backward(
            back_sums[which], hiddens[which], scale_two[which], gain_two
        )
        grad_hidden.append(grads)
        low = narrow(grads)
        grad_mixed.append(jnp.concatenate([low, over_core(low)], axis=0))
    gain_two_grad = jnp.sum(back_sums[0] * hidden_near * scale_two[0], axis=0)

    grad_projected, conv_local = [None, None], 0.0
    sums = [None, None]
    for pair in (1, 0):
        input_gate, output_gate, values_part, mix_input, prior_one, prior_two, convolved = saved[pair]
        grad_y = dot_nt(grad_mixed[pair], out_rows).reshape(2, size, width)
        grad_conv = grad_y * output_gate
        conv_local = conv_local + jnp.stack(
            [
                jnp.sum(grad_conv * prior_two, axis=(0, 1)),
                jnp.sum(grad_conv * prior_one, axis=(0, 1)),
                jnp.sum(grad_conv * mix_input, axis=(0, 1)),
            ]
        )
        after = over_row(grad_conv[:, :2])
        extended = jnp.concatenate([grad_conv, after], axis=1)
        grad_mix = (
            taps[2] * grad_conv
            + taps[1] * (next_one[pair] * extended[:, 1 : size + 1])
            + taps[0] * (next_two[pair] * extended[:, 2:])
        )
        grad_projected[pair] = narrow(
            jnp.concatenate([grad_mix * values_part, grad_y * convolved, grad_mix * input_gate], axis=2)
        ).reshape(2 * size, 3 * width)
        sums[pair] = dot_nn(grad_projected[pair], in_rows)
        if pair == 1:
            far_one = sums[1][:size] + wide(over_core(narrow(sums[1][size:])))
            one_from_far = over_x(narrow(far_one))
    near_one = sums[0][:size] + wide(over_core(narrow(sums[0][size:])))
    grad_normed_one = near_one + wide(one_from_far)

    mixer_total = scatter_pieces(
        jnp.concatenate(
            [
                dot_tn(grad_projected[0], normed_one[0]) + dot_tn(grad_projected[1], normed_one[1]),
                dot_tn(mixed[0], grad_mixed[0]) + dot_tn(mixed[1], grad_mixed[1]),
            ],
            axis=0,
        ),
        4,
    )

    own_inputs = wide(near_tokens[0])
    own_scale = scale_one[0][:size]
    input_grad = grad_hidden[0] + norm_backward(grad_normed_one, own_inputs, own_scale, gain_one)
    gain_one_grad = jnp.sum(grad_normed_one * own_inputs * own_scale, axis=0)

    gain_local = jnp.stack([gain_one_grad, gain_two_grad])
    conv_flat = conv_local.reshape(3, cols, channels).transpose(1, 0, 2).reshape(cols, 3 * channels)
    conv_flat = jnp.take(conv_flat, (col - jnp.arange(cols)) % cols, axis=0).reshape(-1)
    sent = jnp.concatenate([gain_local[:, half:].reshape(-1), conv_flat])
    small = jnp.concatenate([gain_local[:, :half].reshape(-1), conv_flat]) + over_row(sent)
    for distance in (1, 2):
        small = small + col_swap(small, distance)
    conv_own = lax.dynamic_slice_in_dim(small[2 * half :], col * 3 * channels, 3 * channels, 0)
    conv_wide = lax.dynamic_update_slice(
        jnp.zeros((TEAM * 3 * channels,), jnp.float32), conv_own, (place * 3 * channels,)
    )
    small = jnp.concatenate([small[: 2 * half], conv_wide])
    small = small + over_x(small)
    small = small + over_core(small)
    small = other_teams(small)
    conv_grad = small[2 * half :].reshape(TEAM, 3, channels).transpose(1, 0, 2).reshape(3, TEAM * channels)

    down_grad = wide(team_rows(down_total, 1)[0])
    gate_grad = wide(team_rows(gate_total, 1)[0].T)
    up_grad = wide(team_rows(up_total, 1)[0].T)
    mixer_grads = team_rows(mixer_total, 4)
    in_grad = wide(mixer_grads[:3].transpose(2, 0, 1))
    out_grad = wide(mixer_grads[3])
    return (
        to_blocks(result, jnp.bfloat16),
        to_blocks(input_grad, jnp.float32),
        small[:half],
        in_grad,
        conv_grad,
        out_grad,
        small[half : 2 * half],
        gate_grad,
        up_grad,
        down_grad,
    )


def solution(mesh):
    return jax.shard_map(
        body,
        mesh=mesh,
        in_specs=(
            P(("dp", "col"), "row"),
            P(("dp", "row")),
            P(("dp", "col"), "row"),
            P("row"),
            P("row", None, "col"),
            P(None, "col"),
            P("col", "row"),
            P("row"),
            P("row", "col"),
            P("row", "col"),
            P("col", "row"),
        ),
        out_specs=(
            P(("dp", "col"), "row"),
            P(("dp", "col"), "row"),
            P("row"),
            P("row", None, "col"),
            P(None, "col"),
            P("col", "row"),
            P("row"),
            P("row", "col"),
            P("row", "col"),
            P("col", "row"),
        ),
        check_vma=False,
    )
```

time: 2450 us -> 682 us (0.28)
  waiting for transfers between devices: 2150 us -> 308 us
  starting transfers between devices: 1.9 us -> 120 us
  blocking collectives: 63.6 us -> 0 us
  local copies, waits for them, and re-layouts: 17.4 us -> 66.5 us
    reduce_scatter x8 -> x0, waiting for transfers between devices: 1360 us -> none  [the longest x4 804 us: summed_over_row(): lax.psum_scatter(jnp.dot(left, right, preferred_element_type=jnp.float32)...]
    all_gather x8 -> x0, waiting for transfers between devices: 710 us -> none  [the longest x4 410 us: block_rows(): return lax.all_gather(values, 'row', axis=0, tiled=True)]
    ppermute x0 -> x84, waiting for transfers between devices: none -> 308 us  [the longest x27 126 us: over_col(): lax.ppermute(values, 'col', [(i, (i + shift) % size) for i in range(size)])]
    ppermute x0 -> x84, starting transfers between devices: none -> 120 us  [the longest x27 83.3 us: over_col(): lax.ppermute(values, 'col', [(i, (i + shift) % size) for i in range(size)])]
    psum x1 -> x0, waiting for transfers between devices: 82.9 us -> none  [body(): lax.psum(in_grad.astype(jnp.bfloat16), 'dp').astype(jnp.float32)]
    psum x5 -> x0, blocking collectives: 63.6 us -> none  [the longest x1 41.3 us: body(): conv_sum, gain_sum = lax.psum((conv_wide, gain_wide), ('dp', 'row', 'col'))]
    dot_general x12 -> x30, matrix products: 128 us -> 115 us  [the longest x10 45.4 us: dot_nt(): lax.dot_general(left, right, (((1,), (1,)), ((), ())), preferred_element_...]
  transfers between devices with their start and end apart: 17 -> 84, of which waited for: 17 -> 31; matrix products, arithmetic and copies ran while one was open for 5% -> 30% of each run, Pallas kernels for 0% -> 0%
where the time goes in v1:
time: 682 us; the launch traced here: 671 us
  waiting for transfers between devices  308 us (45%)
  starting transfers between devices  120 us (18%)
  matrix products  115 us (17%)
  local copies, waits for them, and re-layouts  66.5 us (10%)
  other arithmetic  57.7 us (8%)
    ppermute x27, waiting for transfers between devices, over_col(): lax.ppermute(values, 'col', [(i, (i + shift) % size) for i in range(size)])  126 us
    ppermute x36, waiting for transfers between devices, over_dp(): return lax.ppermute(values, 'dp', [(i, i ^ distance) for i in range(size)])  96.3 us
    ppermute x27, starting transfers between devices, over_col(): lax.ppermute(values, 'col', [(i, (i + shift) % size) for i in range(size)])  83.3 us
    ppermute x19, waiting for transfers between devices, over_row(): return lax.ppermute(values, 'row', [(0, 1), (1, 0)])  78 us
    dot_general x10, matrix products, dot_nt(): lax.dot_general(left, right, (((1,), (1,)), ((), ())), preferred_element_...  45.4 us
    dot_general x10, matrix products, dot_nn(): lax.dot_general(left, right, (((1,), (0,)), ((), ())), preferred_element_...  36.7 us
    dot_general x10, matrix products, dot_tn(): lax.dot_general(left, right, (((0,), (0,)), ((), ())), preferred_element_...  33.4 us
    unnamed x245, local copies, waits for them, and re-layouts  27.5 us
  transfers between devices with their start and end apart: 84, of which 31 were waited for; matrix products, arithmetic and copies ran while one was open for 30% of the time, Pallas kernels for 0%

profile of v1, /device:TPU:0, one launch (start us, length us, event | category | flops | bytes accessed | tf_op | source)
XLA Modules:
  0.0 670.7 jit_solution(3631938102290036785)
XLA Ops:
  16.9 9.7 %collective-permute-done.10 = bf16[3,64]{1,0:T(4,128)(2,1)S(1)} collective-permute-done((bf16[3,64]{1,0:T(4,128)(2,1)S(1)}, bf16[3,64]{1,0:T(4,128)(2,1)S(1)}, u32[]{:S(2)}, u32[]{:S(2)}) %collective-permute-start.10) | collective-permute-done | bytes 416 | tf_op jit(solution)/shard_map/ppermute | solution.py:41
  49.2 7.9 %collective-permute-done = bf16[512,512]{1,0:T(8,128)(2,1)S(1)} collective-permute-done((bf16[512,512]{1,0:T(8,128)(2,1)}, bf16[512,512]{1,0:T(8,128)(2,1)S(1)}, u32[]{:S(2)}, u32[]{:S(2)}) %collective-permute-start) | collective-permute-done | bytes 524320 | tf_op jit(solution)/shard_map/ppermute | solution.py:36
  60.5 9.0 %collective-permute-done.2 = bf16[512,512]{1,0:T(8,128)(2,1)S(1)} collective-permute-done((bf16[512,512]{1,0:T(8,128)(2,1)S(1)}, bf16[512,512]{1,0:T(8,128)(2,1)S(1)}, u32[]{:S(2)}, u32[]{:S(2)}) %collective-permute-start.2) | collective-permute-done | bytes 524320 | tf_op jit(solution)/shard_map/ppermute | solution.py:24
  75.1 22.9 %collective-permute-done.8 = bf16[1024,512]{1,0:T(8,128)(2,1)S(1)} collective-permute-done((bf16[1024,512]{1,0:T(8,128)(2,1)S(1)}, bf16[1024,512]{1,0:T(8,128)(2,1)S(1)}, u32[]{:S(2)}, u32[]{:S(2)}) %collective-permute-start.8) | collective-permute-done | bytes 1048608 | tf_op jit(solution)/shard_map/ppermute | solution.py:36
  117.4 12.6 %collective-permute-done.41 = bf16[512,512]{1,0:T(8,128)(2,1)S(1)} collective-permute-done((bf16[512,512]{1,0:T(8,128)(2,1)S(1)}, bf16[512,512]{1,0:T(8,128)(2,1)S(1)}, u32[]{:S(2)}, u32[]{:S(2)}) %collective-permute-start.41) | collective-permute-done | bytes 524320 | tf_op jit(solution)/shard_map/ppermute | solution.py:24
  139.5 11.3 %collective-permute-done.25 = bf16[288,512]{0,1:T(8,128)(2,1)S(1)} collective-permute-done((bf16[288,512]{0,1:T(8,128)(2,1)S(1)}, bf16[288,512]{0,1:T(8,128)(2,1)S(1)}, u32[]{:S(2)}, u32[]{:S(2)}) %collective-permute-start.25) | collective-permute-done | bytes 294944 | tf_op jit(solution)/shard_map/ppermute | solution.py:41
  150.9 16.5 %collective-permute-done.26 = bf16[288,512]{0,1:T(8,128)(2,1)S(1)} collective-permute-done((bf16[288,512]{0,1:T(8,128)(2,1)S(1)}, bf16[288,512]{0,1:T(8,128)(2,1)S(1)}, u32[]{:S(2)}, u32[]{:S(2)}) %collective-permute-start.26) | collective-permute-done | bytes 294944 | tf_op jit(solution)/shard_map/ppermute | solution.py:41
  186.3 10.5 %collective-permute-done.30 = bf16[288,512]{1,0:T(8,128)(2,1)S(1)} collective-permute-done((bf16[288,512]{1,0:T(8,128)(2,1)S(1)}, bf16[288,512]{1,0:T(8,128)(2,1)S(1)}, u32[]{:S(2)}, u32[]{:S(2)}) %collective-permute-start.30) | collective-permute-done | bytes 294944 | tf_op jit(solution)/shard_map/ppermute | solution.py:41
  209.5 18.3 %collective-permute-done.22 = bf16[288,512]{0,1:T(8,128)(2,1)} collective-permute-done((bf16[288,512]{0,1:T(8,128)(2,1)S(1)}, bf16[288,512]{0,1:T(8,128)(2,1)}, u32[]{:S(2)}, u32[]{:S(2)}) %collective-permute-start.22) | collective-permute-done | bytes 294944 | tf_op jit(solution)/shard_map/ppermute | solution.py:41
  228.3 7.8 %collective-permute-done.23 = bf16[288,512]{0,1:T(8,128)(2,1)} collective-permute-done((bf16[288,512]{0,1:T(8,128)(2,1)S(1)}, bf16[288,512]{0,1:T(8,128)(2,1)}, u32[]{:S(2)}, u32[]{:S(2)}) %collective-permute-start.23) | collective-permute-done | bytes 294944 | tf_op jit(solution)/shard_map/ppermute | solution.py:41
  245.5 18.0 %collective-permute-done.32 = bf16[1152,512]{1,0:T(8,128)(2,1)} collective-permute-done((bf16[1152,512]{1,0:T(8,128)(2,1)}, bf16[1152,512]{1,0:T(8,128)(2,1)}, u32[]{:S(2)}, u32[]{:S(2)}) %collective-permute-start.32) | collective-permute-done | bytes 1179680 | tf_op jit(solution)/shard_map/ppermute | solution.py:36
  286.0 9.1 %multiply_convert_fusion.3 = (bf16[1024,1152]{1,0:T(8,128)(2,1)}, bf16[1024,1152]{1,0:T(8,128)(2,1)}, bf16[1024,1152]{1,0:T(8,128)(2,1)}) fusion(f32[1024,1152]{1,0:T(8,128)} %fusion.52, f32[1024,1152]{1,0:T(8,128)S(1)} %fusion.115, bf16[1152,512]{0,1:T(8,128)(2,1)S(1)} %collective-permute-done.24, bf16[1152,512]{0,1:T(8,128)(2,1)S(1)} %copy-done.56, ...), kind=kOutput, calls=%fused_computation.8 | convolution fusion | flops 2442526720 | bytes 20971520 | tf_op jit(solution)/shard_map/dot_general | solution.py:11
  295.1 9.4 %fusion.51 = f32[1152,1024]{1,0:T(8,128)} fusion(bf16[1024,1152]{1,0:T(8,128)(2,1)} %get-tuple-element.75, bf16[512,1024]{1,0:T(8,128)(2,1)S(1)} %get-tuple-element.81, bf16[512,512]{1,0:T(8,128)(2,1)S(1)} %copy-done.49, bf16[512,512]{1,0:T(8,128)(2,1)S(1)} %copy-done.29), kind=kOutput, calls=%fused_computation.174 | convolution fusion | flops 2422210560 | bytes 9175040 | tf_op jit(solution)/shard_map/dot_general | solution.py:19
  309.0 9.1 %multiply_convert_fusion.1 = (bf16[1024,1152]{1,0:T(8,128)(2,1)}, bf16[1024,1152]{1,0:T(8,128)(2,1)}, bf16[1024,1152]{1,0:T(8,128)(2,1)}) fusion(f32[1024,1152]{1,0:T(8,128)} %fusion.27, f32[1024,1152]{1,0:T(8,128)S(1)} %fusion.113, bf16[1152,512]{0,1:T(8,128)(2,1)S(1)} %collective-permute-done.24, bf16[1152,512]{0,1:T(8,128)(2,1)S(1)} %copy-done.56, ...), kind=kOutput, calls=%fused_computation.6 | convolution fusion | flops 2442526720 | bytes 20971520 | tf_op jit(solution)/shard_map/dot_general | solution.py:11
  353.0 7.3 %fusion.120 = f32[1024,1024]{1,0:T(8,128)} fusion(bf16[1024,1152]{1,0:T(8,128)(2,1)} %get-tuple-element.77, bf16[1152,512]{0,1:T(8,128)(2,1)} %collective-permute-done.28, bf16[1152,512]{0,1:T(8,128)(2,1)} %concatenate.131), kind=kOutput, calls=%fused_computation.354 | convolution fusion | flops 2420637696 | bytes 8912896 | tf_op jit(solution)/shard_map/dot_general | solution.py:15
  384.2 18.9 %collective-permute-start.79 = (bf16[288,512]{1,0:T(8,128)(2,1)S(1)}, bf16[288,512]{1,0:T(8,128)(2,1)S(1)}, u32[]{:S(2)}, u32[]{:S(2)}) collective-permute-start(bf16[288,512]{1,0:T(8,128)(2,1)S(1)} %get-tuple-element.85), channel_id=1, source_target_pairs={{0,3},{1,0},{2,1},{3,2},{4,7},{5,4},{6,5},{7,6},{8,11},{9,8},{10,9... | collective-permute-start | bytes 884744 | tf_op jit(solution)/shard_map/ppermute | solution.py:41
  405.7 15.6 %collective-permute-start.81 = (bf16[288,512]{1,0:T(8,128)(2,1)S(1)}, bf16[288,512]{1,0:T(8,128)(2,1)S(1)}, u32[]{:S(2)}, u32[]{:S(2)}) collective-permute-start(bf16[288,512]{1,0:T(8,128)(2,1)S(1)} %get-tuple-element.86), channel_id=1, source_target_pairs={{0,1},{1,2},{2,3},{3,0},{4,5},{5,6},{6,7},{7,4},{8,9},{9,10},{10,1... | collective-permute-start | bytes 884744 | tf_op jit(solution)/shard_map/ppermute | solution.py:41
  425.6 15.8 %collective-permute-done.80 = bf16[288,512]{1,0:T(8,128)(2,1)S(1)} collective-permute-done((bf16[288,512]{1,0:T(8,128)(2,1)S(1)}, bf16[288,512]{1,0:T(8,128)(2,1)S(1)}, u32[]{:S(2)}, u32[]{:S(2)}) %collective-permute-start.80) | collective-permute-done | bytes 294944 | tf_op jit(solution)/shard_map/ppermute | solution.py:41
  447.8 15.8 %collective-permute-done.74 = bf16[288,512]{1,0:T(8,128)(2,1)S(1)} collective-permute-done((bf16[288,512]{1,0:T(8,128)(2,1)S(1)}, bf16[288,512]{1,0:T(8,128)(2,1)S(1)}, u32[]{:S(2)}, u32[]{:S(2)}) %collective-permute-start.74) | collective-permute-done | bytes 294944 | tf_op jit(solution)/shard_map/ppermute | solution.py:41
  466.6 14.8 %collective-permute-done.68 = bf16[288,512]{1,0:T(8,128)(2,1)S(1)} collective-permute-done((bf16[288,512]{1,0:T(8,128)(2,1)S(1)}, bf16[288,512]{1,0:T(8,128)(2,1)S(1)}, u32[]{:S(2)}, u32[]{:S(2)}) %collective-permute-start.68) | collective-permute-done | bytes 294944 | tf_op jit(solution)/shard_map/ppermute | solution.py:41
  484.7 34.5 %collective-permute-done.82 = bf16[1,288,512]{2,1,0:T(8,128)(2,1)S(1)} collective-permute-done((bf16[1,288,512]{2,1,0:T(8,128)(2,1)S(1)}, bf16[1,288,512]{2,1,0:T(8,128)(2,1)S(1)}, u32[]{:S(2)}, u32[]{:S(2)}) %collective-permute-start.82) | collective-permute-done | bytes 294944 | tf_op jit(solution)/shard_map/ppermute | solution.py:24
  536.2 14.8 %collective-permute-done.37 = bf16[512,1024]{1,0:T(8,128)(2,1)} collective-permute-done((bf16[512,1024]{1,0:T(8,128)(2,1)S(1)}, bf16[512,1024]{1,0:T(8,128)(2,1)}, u32[]{:S(2)}, u32[]{:S(2)}) %collective-permute-start.37) | collective-permute-done | bytes 1048608 | tf_op jit(solution)/shard_map/ppermute | solution.py:24
  586.9 16.2 %collective-permute-done.60 = bf16[1024,512]{1,0:T(8,128)(2,1)S(1)} collective-permute-done((bf16[1024,512]{1,0:T(8,128)(2,1)S(1)}, bf16[1024,512]{1,0:T(8,128)(2,1)S(1)}, u32[]{:S(2)}, u32[]{:S(2)}) %collective-permute-start.60) | collective-permute-done | bytes 1048608 | tf_op jit(solution)/shard_map/ppermute | solution.py:36
  636.3 7.7 %collective-permute-done.64 = bf16[4,64,512]{2,1,0:T(8,128)(2,1)S(1)} collective-permute-done((bf16[4,64,512]{2,1,0:T(8,128)(2,1)S(1)}, bf16[4,64,512]{2,1,0:T(8,128)(2,1)S(1)}, u32[]{:S(2)}, u32[]{:S(2)}) %collective-permute-start.64) | collective-permute-done | bytes 262176 | tf_op jit(solution)/shard_map/ppermute | solution.py:24
  (583 shorter events, 334.0 us)
Async XLA Ops:
  3.7 40.0 %collective-permute-start.5 = (bf16[256,512]{1,0:T(8,128)(2,1)}, bf16[256,512]{1,0:T(8,128)(2,1)}, u32[]{:S(2)}, u32[]{:S(2)}) collective-permute-start(bf16[256,512]{1,0:T(8,128)(2,1)} %pad_maximum_fusion.40), channel_id=1, source_target_pairs={{0,1},{1,2},{2,3},{3,0},{4,5},{5,6},{6,7},{7,4},{8,9},{9,10},{10,1... | collective-permute-start | bytes 786440 | tf_op jit(solution)/shard_map/ppermute | solution.py:41
  6.7 39.4 %collective-permute-start.6 = (bf16[256,512]{1,0:T(8,128)(2,1)}, bf16[256,512]{1,0:T(8,128)(2,1)}, u32[]{:S(2)}, u32[]{:S(2)}) collective-permute-start(bf16[256,512]{1,0:T(8,128)(2,1)} %pad_maximum_fusion.40), channel_id=1, source_target_pairs={{0,2},{1,3},{2,0},{3,1},{4,6},{5,7},{6,4},{7,5},{8,10},{9,11},{10,... | collective-permute-start | bytes 786440 | tf_op jit(solution)/shard_map/ppermute | solution.py:41
  43.7 73.6 %collective-permute-start.40 = (bf16[512,512]{1,0:T(8,128)(2,1)S(1)}, bf16[512,512]{1,0:T(8,128)(2,1)S(1)}, u32[]{:S(2)}, u32[]{:S(2)}) collective-permute-start(bf16[512,512]{1,0:T(8,128)(2,1)S(1)} %get-tuple-element.100), channel_id=1, source_target_pairs={{0,16},{8,24},{16,0},{24,8},{1,17},{9,25},{17,1},{25,9},{2,18},{10... | collective-permute-start | bytes 1572872 | tf_op jit(solution)/shard_map/ppermute | solution.py:24
  46.1 69.6 %collective-permute-start.39 = (bf16[512,512]{1,0:T(8,128)(2,1)}, bf16[512,512]{1,0:T(8,128)(2,1)S(1)}, u32[]{:S(2)}, u32[]{:S(2)}) collective-permute-start(bf16[512,512]{1,0:T(8,128)(2,1)} %get-tuple-element.99), channel_id=1, source_target_pairs={{0,4},{4,0},{1,5},{5,1},{2,6},{6,2},{3,7},{7,3},{8,12},{12,8},{9,1... | collective-permute-start | bytes 1572872 | tf_op jit(solution)/shard_map/ppermute | solution.py:36
  132.1 41.2 %collective-permute-start.18 = (bf16[512,1024]{1,0:T(8,128)(2,1)}, bf16[512,1024]{1,0:T(8,128)(2,1)S(1)}, u32[]{:S(2)}, u32[]{:S(2)}) collective-permute-start(bf16[512,1024]{1,0:T(8,128)(2,1)} %slice.911), channel_id=1, source_target_pairs={{0,8},{8,0},{16,24},{24,16},{1,9},{9,1},{17,25},{25,17},{2,10},{10... | collective-permute-start | bytes 3145736 | tf_op jit(solution)/shard_map/ppermute | solution.py:24
  133.8 42.9 %collective-permute-start.34 = (bf16[512,1024]{1,0:T(8,128)(2,1)}, bf16[512,1024]{1,0:T(8,128)(2,1)S(1)}, u32[]{:S(2)}, u32[]{:S(2)}) collective-permute-start(bf16[512,1024]{1,0:T(8,128)(2,1)} %fusion.28), channel_id=1, source_target_pairs={{0,16},{8,24},{16,0},{24,8},{1,17},{9,25},{17,1},{25,9},{2,18},{10... | collective-permute-start | bytes 3145736 | tf_op jit(solution)/shard_map/ppermute | solution.py:24
  136.8 103.6 %collective-permute-start.42 = (bf16[2,512,1024]{2,1,0:T(8,128)(2,1)}, bf16[2,512,1024]{2,1,0:T(8,128)(2,1)}, u32[]{:S(2)}, u32[]{:S(2)}) collective-permute-start(bf16[2,512,1024]{2,1,0:T(8,128)(2,1)} %pad_maximum_fusion.9), channel_id=1, source_target_pairs={{0,8},{8,0},{16,24},{24,16},{1,9},{9,1},{17,25},{25,17},{2,10},{10... | collective-permute-start | bytes 6291464 | tf_op jit(solution)/shard_map/ppermute | solution.py:24
  182.2 60.2 %collective-permute-start.19 = (bf16[512,1024]{1,0:T(8,128)(2,1)}, bf16[512,1024]{1,0:T(8,128)(2,1)}, u32[]{:S(2)}, u32[]{:S(2)}) collective-permute-start(bf16[512,1024]{1,0:T(8,128)(2,1)} %get-tuple-element.79), channel_id=1, source_target_pairs={{0,16},{8,24},{16,0},{24,8},{1,17},{9,25},{17,1},{25,9},{2,18},{10... | collective-permute-start | bytes 3145736 | tf_op jit(solution)/shard_map/ppermute | solution.py:24
  209.0 67.9 %collective-permute-start.28 = (bf16[1152,512]{0,1:T(8,128)(2,1)}, bf16[1152,512]{0,1:T(8,128)(2,1)}, u32[]{:S(2)}, u32[]{:S(2)}) collective-permute-start(bf16[1152,512]{0,1:T(8,128)(2,1)} %concatenate.131), channel_id=1, source_target_pairs={{0,4},{4,0},{1,5},{5,1},{2,6},{6,2},{3,7},{7,3},{8,12},{12,8},{9,1... | collective-permute-start | bytes 3538952 | tf_op jit(solution)/shard_map/ppermute | solution.py:36
  239.9 46.1 %collective-permute-start.24 = (bf16[1152,512]{0,1:T(8,128)(2,1)}, bf16[1152,512]{0,1:T(8,128)(2,1)S(1)}, u32[]{:S(2)}, u32[]{:S(2)}) collective-permute-start(bf16[1152,512]{0,1:T(8,128)(2,1)} %concatenate.129), channel_id=1, source_target_pairs={{0,4},{4,0},{1,5},{5,1},{2,6},{6,2},{3,7},{7,3},{8,12},{12,8},{9,1... | collective-permute-start | bytes 3538952 | tf_op jit(solution)/shard_map/ppermute | solution.py:36
  324.2 57.0 %collective-permute-start.78 = (bf16[1152,512]{1,0:T(8,128)(2,1)S(1)}, bf16[1152,512]{1,0:T(8,128)(2,1)S(1)}, u32[]{:S(2)}, u32[]{:S(2)}) collective-permute-start(bf16[1152,512]{1,0:T(8,128)(2,1)S(1)} %slice.902), channel_id=1, source_target_pairs={{0,4},{4,0},{1,5},{5,1},{2,6},{6,2},{3,7},{7,3},{8,12},{12,8},{9,1... | collective-permute-start | bytes 3538952 | tf_op jit(solution)/shard_map/ppermute | solution.py:36
  333.2 69.9 %collective-permute-start.72 = (bf16[1152,512]{1,0:T(8,128)(2,1)S(1)}, bf16[1152,512]{1,0:T(8,128)(2,1)S(1)}, u32[]{:S(2)}, u32[]{:S(2)}) collective-permute-start(bf16[1152,512]{1,0:T(8,128)(2,1)S(1)} %slice.903), channel_id=1, source_target_pairs={{0,4},{4,0},{1,5},{5,1},{2,6},{6,2},{3,7},{7,3},{8,12},{12,8},{9,1... | collective-permute-start | bytes 3538952 | tf_op jit(solution)/shard_map/ppermute | solution.py:36
  343.7 62.0 %collective-permute-start.66 = (bf16[1152,512]{1,0:T(8,128)(2,1)S(1)}, bf16[1152,512]{1,0:T(8,128)(2,1)}, u32[]{:S(2)}, u32[]{:S(2)}) collective-permute-start(bf16[1152,512]{1,0:T(8,128)(2,1)S(1)} %slice.904), channel_id=1, source_target_pairs={{0,4},{4,0},{1,5},{5,1},{2,6},{6,2},{3,7},{7,3},{8,12},{12,8},{9,1... | collective-permute-start | bytes 3538952 | tf_op jit(solution)/shard_map/ppermute | solution.py:36
  367.1 56.3 %collective-permute-start.44 = (bf16[512,1024]{1,0:T(8,128)(2,1)}, bf16[512,1024]{1,0:T(8,128)(2,1)S(1)}, u32[]{:S(2)}, u32[]{:S(2)}) collective-permute-start(bf16[512,1024]{1,0:T(8,128)(2,1)} %slice.907), channel_id=1, source_target_pairs={{0,8},{8,0},{16,24},{24,16},{1,9},{9,1},{17,25},{25,17},{2,10},{10... | collective-permute-start | bytes 3145736 | tf_op jit(solution)/shard_map/ppermute | solution.py:24
  380.3 103.5 %collective-permute-start.36 = (bf16[512,1024]{1,0:T(8,128)(2,1)}, bf16[512,1024]{1,0:T(8,128)(2,1)S(1)}, u32[]{:S(2)}, u32[]{:S(2)}) collective-permute-start(bf16[512,1024]{1,0:T(8,128)(2,1)} %slice.909), channel_id=1, source_target_pairs={{0,8},{8,0},{16,24},{24,16},{1,9},{9,1},{17,25},{25,17},{2,10},{10... | collective-permute-start | bytes 3145736 | tf_op jit(solution)/shard_map/ppermute | solution.py:24
  384.2 39.3 %collective-permute-start.79 = (bf16[288,512]{1,0:T(8,128)(2,1)S(1)}, bf16[288,512]{1,0:T(8,128)(2,1)S(1)}, u32[]{:S(2)}, u32[]{:S(2)}) collective-permute-start(bf16[288,512]{1,0:T(8,128)(2,1)S(1)} %get-tuple-element.85), channel_id=1, source_target_pairs={{0,3},{1,0},{2,1},{3,2},{4,7},{5,4},{6,5},{7,6},{8,11},{9,8},{10,9... | collective-permute-start | bytes 884744 | tf_op jit(solution)/shard_map/ppermute | solution.py:41
  423.4 40.1 %collective-permute-start.74 = (bf16[288,512]{1,0:T(8,128)(2,1)S(1)}, bf16[288,512]{1,0:T(8,128)(2,1)S(1)}, u32[]{:S(2)}, u32[]{:S(2)}) collective-permute-start(bf16[288,512]{1,0:T(8,128)(2,1)S(1)} %get-tuple-element.90), channel_id=1, source_target_pairs={{0,2},{1,3},{2,0},{3,1},{4,6},{5,7},{6,4},{7,5},{8,10},{9,11},{10,... | collective-permute-start | bytes 884744 | tf_op jit(solution)/shard_map/ppermute | solution.py:41
  464.2 68.5 %collective-permute-start.49 = (bf16[512,1024]{1,0:T(8,128)(2,1)S(1)}, bf16[512,1024]{1,0:T(8,128)(2,1)S(1)}, u32[]{:S(2)}, u32[]{:S(2)}) collective-permute-start(bf16[512,1024]{1,0:T(8,128)(2,1)S(1)} %fusion.30), channel_id=1, source_target_pairs={{0,16},{8,24},{16,0},{24,8},{1,17},{9,25},{17,1},{25,9},{2,18},{10... | collective-permute-start | bytes 3145736 | tf_op jit(solution)/shard_map/ppermute | solution.py:24
  464.8 68.4 %collective-permute-start.45 = (bf16[512,1024]{1,0:T(8,128)(2,1)S(1)}, bf16[512,1024]{1,0:T(8,128)(2,1)S(1)}, u32[]{:S(2)}, u32[]{:S(2)}) collective-permute-start(bf16[512,1024]{1,0:T(8,128)(2,1)S(1)} %fusion.69), channel_id=1, source_target_pairs={{0,16},{8,24},{16,0},{24,8},{1,17},{9,25},{17,1},{25,9},{2,18},{10... | collective-permute-start | bytes 3145736 | tf_op jit(solution)/shard_map/ppermute | solution.py:24
  481.9 43.6 %collective-permute-start.76 = (bf16[1,288,512]{2,1,0:T(8,128)(2,1)S(1)}, bf16[1,288,512]{2,1,0:T(8,128)(2,1)S(1)}, u32[]{:S(2)}, u32[]{:S(2)}) collective-permute-start(bf16[1,288,512]{2,1,0:T(8,128)(2,1)S(1)} %bitcast.257), channel_id=1, source_target_pairs={{0,16},{8,24},{16,0},{24,8},{1,17},{9,25},{17,1},{25,9},{2,18},{10... | collective-permute-start | bytes 884744 | tf_op jit(solution)/shard_map/ppermute | solution.py:24
  483.8 48.1 %collective-permute-start.70 = (bf16[1,288,512]{2,1,0:T(8,128)(2,1)S(1)}, bf16[1,288,512]{2,1,0:T(8,128)(2,1)S(1)}, u32[]{:S(2)}, u32[]{:S(2)}) collective-permute-start(bf16[1,288,512]{2,1,0:T(8,128)(2,1)S(1)} %bitcast.259), channel_id=1, source_target_pairs={{0,16},{8,24},{16,0},{24,8},{1,17},{9,25},{17,1},{25,9},{2,18},{10... | collective-permute-start | bytes 884744 | tf_op jit(solution)/shard_map/ppermute | solution.py:24
  531.8 47.8 %collective-permute-start.83 = (bf16[2,1,288,512]{3,2,1,0:T(8,128)(2,1)}, bf16[2,1,288,512]{3,2,1,0:T(8,128)(2,1)}, u32[]{:S(2)}, u32[]{:S(2)}) collective-permute-start(bf16[2,1,288,512]{3,2,1,0:T(8,128)(2,1)} %pad_maximum_fusion.37), channel_id=1, source_target_pairs={{0,8},{8,0},{16,24},{24,16},{1,9},{9,1},{17,25},{25,17},{2,10},{10... | collective-permute-start | bytes 1769480 | tf_op jit(solution)/shard_map/ppermute | solution.py:24
  554.8 60.9 %collective-permute-start.38 = (bf16[512,512]{1,0:T(8,128)(2,1)S(1)}, bf16[512,512]{1,0:T(8,128)(2,1)S(1)}, u32[]{:S(2)}, u32[]{:S(2)}) collective-permute-start(bf16[512,512]{1,0:T(8,128)(2,1)S(1)} %get-tuple-element.101), channel_id=1, source_target_pairs={{0,4},{4,0},{1,5},{5,1},{2,6},{6,2},{3,7},{7,3},{8,12},{12,8},{9,1... | collective-permute-start | bytes 1572872 | tf_op jit(solution)/shard_map/ppermute | solution.py:36
  585.8 58.3 %collective-permute-start.48 = (bf16[512,1024]{1,0:T(8,128)(2,1)}, bf16[512,1024]{1,0:T(8,128)(2,1)}, u32[]{:S(2)}, u32[]{:S(2)}) collective-permute-start(bf16[512,1024]{1,0:T(8,128)(2,1)} %slice.906), channel_id=1, source_target_pairs={{0,8},{8,0},{16,24},{24,16},{1,9},{9,1},{17,25},{25,17},{2,10},{10... | collective-permute-start | bytes 3145736 | tf_op jit(solution)/shard_map/ppermute | solution.py:24
  (171 other events, 2992.7 us)

commit v2 on v1

v2 whole, which is shorter than its diff:
```python
import jax
import jax.numpy as jnp
from jax import lax
from jax.experimental import pallas as pl
from jax.experimental.pallas import tpu as pltpu
from jax.sharding import PartitionSpec as P

EPSILON = 1e-05
TEAM = 4


def dot_nt(left, right):
    return lax.dot_general(left, right, (((1,), (1,)), ((), ())), preferred_element_type=jnp.float32)


def dot_nn(left, right):
    return lax.dot_general(left, right, (((1,), (0,)), ((), ())), preferred_element_type=jnp.float32)


def dot_tn(left, right):
    return lax.dot_general(left, right, (((0,), (0,)), ((), ())), preferred_element_type=jnp.float32)


def over_dp(values, distance):
    size = lax.axis_size("dp")
    return lax.ppermute(values, "dp", [(i, i ^ distance) for i in range(size)])


def over_core(values):
    return over_dp(values, 1)


def over_x(values):
    return over_dp(values, 2)


def over_row(values):
    return lax.ppermute(values, "row", [(0, 1), (1, 0)])


def col_swap(values, distance):
    size = lax.axis_size("col")
    return lax.ppermute(values, "col", [(i, i ^ distance) for i in range(size)])


def narrow(values):
    return values.astype(jnp.bfloat16)


def wide(values):
    return values.astype(jnp.float32)


def halves(values):
    size = values.shape[0] // 2
    return values[:size], values[size:]


def other_teams(values):
    distance = TEAM
    while distance < lax.axis_size("dp"):
        values = values + over_dp(values, distance)
        distance *= 2
    return values


def after(value, *events):
    return lax.optimization_barrier((value, *events))[0]


def meet(*values):
    return lax.optimization_barrier(values)


def hop(move, value, *waiting):
    return meet(move(value), *waiting)


def stacked(pair, other, parts):
    pieces = jnp.concatenate([pair, other], axis=0)
    if parts > 1:
        pieces = pieces.reshape(4, parts, -1, pair.shape[2]).transpose(1, 0, 2, 3)
    return pieces.reshape(-1, pair.shape[2])


def col_first(piece):
    return jnp.stack([piece, col_swap(piece, 2)])


def col_send(values, parts):
    rows = values.shape[0] // (parts * 4)
    grid = values.reshape(parts, 2, 2 * rows, values.shape[1])
    return narrow(grid[:, 1]), grid[:, 0]


def col_add(kept, received):
    total = kept + wide(received)
    rows = total.shape[1] // 2
    return narrow(total[:, rows:]), total[:, :rows]


def col_last(kept, received):
    return (kept + wide(received)).reshape(-1, kept.shape[2])


def team_rows(piece, parts):
    rows, half = piece.shape[0] // parts, piece.shape[1]
    own = narrow(other_teams(piece)).reshape(parts, rows, half)
    far = over_x(own)
    pair = over_core(jnp.stack([own, far]))
    place = lax.axis_index("dp") % TEAM
    blocks = [own, pair[0], far, pair[1]]
    result = jnp.zeros((parts, TEAM * rows, half), jnp.bfloat16)
    for distance, block in enumerate(blocks):
        result = lax.dynamic_update_slice(result, block, (0, (place ^ distance) * rows, 0))
    return result


def norm_scale(hidden):
    return lax.rsqrt(jnp.mean(hidden * hidden, axis=1, keepdims=True) + EPSILON)


def norm_backward(grad_normed, hidden, row_scale, gain_vector):
    inner_sum = jnp.sum(grad_normed * gain_vector * hidden, axis=1, keepdims=True)
    cubed = row_scale * row_scale * row_scale
    return grad_normed * gain_vector * row_scale - hidden * (cubed / hidden.shape[1]) * inner_sum


def to_blocks(values, dtype):
    half = values.shape[1] // 2
    size = values.shape[0]
    row = lax.axis_index("row")
    received = over_row(narrow(values[:, half:])).astype(dtype)
    result = jnp.zeros((2 * size, half), dtype)
    result = lax.dynamic_update_slice(result, values[:, :half].astype(dtype), (row * size, 0))
    return lax.dynamic_update_slice(result, received, ((1 - row) * size, 0))


ROWS = 256
VMEM_BYTES = 48 * 2**20


def whole(array):
    return pl.BlockSpec(array.shape, lambda i: (0,) * array.ndim)


def row_tiles(array):
    return pl.BlockSpec((ROWS, array.shape[1]), lambda i: (i, 0))


def token_call(kernel, tiled, resident, outs):
    tokens = tiled[0].shape[0]
    shapes = [jax.ShapeDtypeStruct((tokens, columns), dtype) for columns, dtype in outs]
    return pl.pallas_call(
        kernel,
        grid=(tokens // ROWS,),
        in_specs=[row_tiles(one) for one in tiled] + [whole(one) for one in resident],
        out_specs=[row_tiles(one) for one in shapes],
        out_shape=shapes,
        compiler_params=pltpu.CompilerParams(vmem_limit_bytes=VMEM_BYTES),
    )(*tiled, *resident)


def split_nt(left, near, row):
    half = near.shape[1]
    return dot_nt(left[:, :half], near[...]) + dot_nt(left[:, half:], row[...])


def forward_kernel(normed, gate_near, gate_row, up_near, up_row, gate, up, act):
    gate_value = split_nt(normed, gate_near, gate_row)
    up_value = split_nt(normed, up_near, up_row)
    gate[...] = narrow(gate_value)
    up[...] = narrow(up_value)
    act[...] = narrow(gate_value * jax.nn.sigmoid(gate_value) * up_value)


def backward_kernel(
    gate, up, cotangent, down_near, down_row, gate_near, gate_row, up_near, up_row, grad_gate, grad_up, back
):
    half = gate_near.shape[1]
    grad_act = split_nt(cotangent, down_near, down_row)
    gate_value, up_value = wide(gate[...]), wide(up[...])
    sigmoid_gate = jax.nn.sigmoid(gate_value)
    gated = grad_act * sigmoid_gate
    low_gate = narrow(gated * up_value * (1.0 + gate_value * (1.0 - sigmoid_gate)))
    low_up = narrow(gated * gate_value)
    grad_gate[...] = low_gate
    grad_up[...] = low_up
    back[:, :half] = narrow(dot_nn(low_gate, gate_near[...]) + dot_nn(low_up, up_near[...]))
    back[:, half:] = narrow(dot_nn(low_gate, gate_row[...]) + dot_nn(low_up, up_row[...]))


def out_kernel(act, down_near, down_row, out):
    half = down_near.shape[1]
    out[:, :half] = narrow(dot_nn(act[...], down_near[...]))
    out[:, half:] = narrow(dot_nn(act[...], down_row[...]))


def weight_kernel(left_near, left_far, right_near, right_far, own, sent):
    total = dot_tn(left_near[...], right_near[...]) + dot_tn(left_far[...], right_far[...])
    half = own.shape[1]
    own[...] = total[:, :half]
    sent[...] = narrow(total[:, half:])


def weight_grads(lefts, rights, tile):
    tokens, columns = lefts[0].shape
    half = rights[0].shape[1] // 2
    left_spec = pl.BlockSpec((tokens, tile), lambda i: (0, i))
    out_spec = pl.BlockSpec((tile, half), lambda i: (i, 0))
    return pl.pallas_call(
        weight_kernel,
        grid=(columns // tile,),
        in_specs=[left_spec, left_spec, whole(rights[0]), whole(rights[1])],
        out_specs=[out_spec, out_spec],
        out_shape=[
            jax.ShapeDtypeStruct((columns, half), jnp.float32),
            jax.ShapeDtypeStruct((columns, half), jnp.bfloat16),
        ],
        compiler_params=pltpu.CompilerParams(vmem_limit_bytes=VMEM_BYTES),
    )(*lefts, *rights)


def body(
    tokens,
    segment_ids,
    cotangent,
    norm1_gain,
    in_weight,
    conv_weight,
    out_weight,
    norm2_gain,
    gate_weight,
    up_weight,
    down_weight,
):
    place = lax.axis_index("dp") % TEAM
    row = lax.axis_index("row")
    col = lax.axis_index("col")
    cols = lax.axis_size("col")
    sequence = tokens.shape[0]
    size = sequence // 2
    half = tokens.shape[1]

    tokens_other = lax.dynamic_slice_in_dim(tokens, (1 - row) * size, size, 0)
    tokens_own = lax.dynamic_slice_in_dim(tokens, row * size, size, 0)
    tokens_row = over_row(tokens_other)
    tokens_x0 = over_x(tokens_own)
    channels = in_weight.shape[2] // TEAM
    hidden = gate_weight.shape[1] // TEAM
    in_part = lax.dynamic_slice_in_dim(in_weight, place * channels, channels, 2)
    in_part = in_part.transpose(1, 2, 0).reshape(3 * channels, half)
    out_part = lax.dynamic_slice_in_dim(out_weight, place * channels, channels, 0)
    taps_part = lax.dynamic_slice_in_dim(conv_weight, place * channels, channels, 1)
    taps_part = jnp.pad(taps_part, ((0, 13), (0, half - channels)))
    mixer_pair = col_first(jnp.concatenate([in_part, out_part, taps_part], axis=0))
    grads_other = lax.dynamic_slice_in_dim(cotangent, (1 - row) * size, size, 0)
    grads_own = lax.dynamic_slice_in_dim(cotangent, row * size, size, 0)
    gate_part = lax.dynamic_slice_in_dim(gate_weight, place * hidden, hidden, 1).T
    gains = jnp.stack([norm1_gain, norm2_gain])
    gains_row = over_row(gains)
    ids_row = over_row(segment_ids)
    tokens_row, tokens_x0, gains_row, ids_row, mixer_pair, grads_other, gate_part = meet(
        tokens_row, tokens_x0, gains_row, ids_row, mixer_pair, grads_other, gate_part
    )

    tokens_x1 = over_x(tokens_row)
    grads_row = over_row(grads_other)
    mixer_other = col_swap(mixer_pair, 1)
    up_part = lax.dynamic_slice_in_dim(up_weight, place * hidden, hidden, 1).T
    down_part = lax.dynamic_slice_in_dim(down_weight, place * hidden, hidden, 0)
    ids = jnp.stack([segment_ids, ids_row])
    ids = lax.dynamic_index_in_dim(ids, (col // 2) ^ row, 0, keepdims=False)
    ids = lax.dynamic_slice_in_dim(ids, (col % 2) * sequence, sequence, 0)
    ids_far = over_x(ids)
    tokens_x1, grads_row, ids_far, mixer_other, gate_part, grads_own, ids, up_part = meet(
        tokens_x1, grads_row, ids_far, mixer_other, gate_part, grads_own, ids, up_part
    )

    mixer_near = stacked(mixer_pair[:, : 4 * channels], mixer_other[:, : 4 * channels], 4)
    mixer_row = over_row(mixer_near)
    grads_x0, grads_x1 = over_x(grads_own), over_x(grads_row)
    gate_pair = col_first(gate_part)
    near = jnp.concatenate([tokens_own, tokens_row], axis=1)
    far = jnp.concatenate([tokens_x0, tokens_x1], axis=1)
    pair, ids, ids_far = hop(over_core, jnp.stack([near, far]), ids, ids_far)
    near_tokens, far_tokens = (near, pair[0]), (far, pair[1])
    ids_pair, pair = hop(over_core, jnp.stack([ids, ids_far]), pair)
    ids = jnp.stack([ids, ids_pair[0], ids_far, ids_pair[1]])
    keeps = []
    for offset in (1, 2):
        equal = (ids[:, offset:] == ids[:, :-offset]).astype(jnp.float32)
        keeps.append(jnp.pad(equal, ((0, 0), (offset, offset))))
    keep_one = lax.dynamic_slice_in_dim(keeps[0], row * size, size, 1)[:, :, None]
    keep_two = lax.dynamic_slice_in_dim(keeps[1], row * size, size, 1)[:, :, None]
    next_one = lax.dynamic_slice_in_dim(keeps[0], row * size + 1, size, 1)[:, :, None]
    next_two = lax.dynamic_slice_in_dim(keeps[1], row * size + 2, size, 1)[:, :, None]
    keep_one, keep_two, next_one, next_two = (
        (flags[:2], flags[2:]) for flags in (keep_one, keep_two, next_one, next_two)
    )
    near_tokens, far_tokens = (near, pair[0]), (far, pair[1])
    gains = wide(jnp.concatenate([gains, gains_row], axis=1))
    gain_one, gain_two = gains[0], gains[1]
    inputs = [jnp.concatenate(both, axis=0) for both in (near_tokens, far_tokens)]
    normed_one, scale_one = [], []
    for which in (0, 1):
        values = wide(inputs[which])
        scale = norm_scale(values)
        scale_one.append(scale)
        normed_one.append(narrow(values * scale * gain_one))
    gate_pair, up_part = meet(gate_pair, up_part)
    gate_other = col_swap(gate_pair, 1)
    taps = jnp.concatenate(
        [both[which, 4 * channels : 4 * channels + 3, :channels] for both in (mixer_pair, mixer_other) for which in (0, 1)],
        axis=1,
    )
    taps = wide(taps)
    mixer_row, grads_x0, grads_x1, gate_other, normed_one, up_part, down_part = meet(
        mixer_row, grads_x0, grads_x1, gate_other, normed_one, up_part, down_part
    )

    gate_near = stacked(gate_pair, gate_other, 1)
    gate_row = over_row(gate_near)
    up_pair = col_first(up_part)
    mixer = jnp.concatenate([mixer_near, mixer_row], axis=1)
    in_rows, out_rows = mixer[: 3 * cols * channels], mixer[3 * cols * channels :]
    width = cols * channels
    saved, mixed, sums = [None, None], [None, None], [None, None]

    def project(which):
        projected = dot_nt(normed_one[which], in_rows).reshape(2, size, 3 * width)
        mix_input = projected[:, :, :width] * projected[:, :, 2 * width :]
        return projected, mix_input, mix_input[:, size - 2 :]

    def mix(which, projected, mix_input, before):
        input_gate, output_gate, values_part = (
            projected[:, :, :width],
            projected[:, :, width : 2 * width],
            projected[:, :, 2 * width :],
        )
        extended = jnp.concatenate([before, mix_input], axis=1)
        prior_one = keep_one[which] * extended[:, 1 : size + 1]
        prior_two = keep_two[which] * extended[:, :size]
        convolved = taps[2] * mix_input + taps[1] * prior_one + taps[0] * prior_two
        mixed[which] = narrow(output_gate * convolved).reshape(2 * size, width)
        saved[which] = (input_gate, output_gate, values_part, mix_input, prior_one, prior_two, convolved)
        return dot_nn(mixed[which], out_rows)

    def core_sum(partial, *waiting):
        received, *waiting = hop(over_core, narrow(partial[size:]), *waiting)
        return (wide(partial[:size]) + wide(received), *waiting)

    far_projected, far_mix, far_end = project(1)
    near_projected, near_mix, near_end = project(0)
    ends, far_mix, near_mix = hop(over_row, jnp.stack([near_end, far_end]), far_mix, near_mix)
    far_sum, near_mix = core_sum(mix(1, far_projected, far_mix, ends[1]), near_mix)
    from_far = over_x(narrow(far_sum))
    up_pair, near_mix = meet(up_pair, near_mix)
    up_other = col_swap(up_pair, 1)
    (near_sum,) = core_sum(mix(0, near_projected, near_mix, ends[0]))
    to_far = over_x(narrow(near_sum))
    from_far, gate_row, up_other, down_part = meet(from_far, gate_row, up_other, down_part)

    up_near = stacked(up_pair, up_other, 1)
    up_row = over_row(up_near)
    down_pair = col_first(down_part)

    def second_norm(hidden_sum, *waiting):
        scale = norm_scale(hidden_sum)
        normed = narrow(hidden_sum * scale * gain_two)
        received, *waiting = hop(over_core, normed, *waiting)
        return (scale, jnp.concatenate([normed, received], axis=0), *waiting)

    hidden_near = wide(near_tokens[0]) + (near_sum + wide(from_far))
    scale_near, normed_near, gate_near = second_norm(hidden_near, gate_near)
    near = jnp.concatenate([grads_own, grads_row], axis=1)
    far = jnp.concatenate([grads_x0, grads_x1], axis=1)
    pair, down_pair = hop(over_core, jnp.stack([near, far]), down_pair)
    near_grads, far_grads = (near, pair[0]), (far, pair[1])
    down_other = col_swap(down_pair, 1)
    up_row, down_other, to_far = meet(up_row, down_other, to_far)

    down_near = stacked(down_pair, down_other, 1)
    down_row = over_row(down_near)
    hidden_far = wide(far_tokens[0]) + (far_sum + wide(to_far))
    scale_far, normed_far, up_near = second_norm(hidden_far, up_near)
    hiddens, scale_two, normed_two = (hidden_near, hidden_far), (scale_near, scale_far), (normed_near, normed_far)
    cotangents = [jnp.concatenate(both, axis=0) for both in (near_grads, far_grads)]
    units = gate_near.shape[0]
    weights = (gate_near, gate_row, up_near, up_row)
    outs = ((units, jnp.bfloat16),) * 3
    gates, ups, act = zip(*[token_call(forward_kernel, [normed], weights, outs) for normed in normed_two])
    gates, ups, act = list(gates), list(ups), list(act)
    down_own, down_sent = weight_grads(act, cotangents, units // 3)
    down_sent, down_kept = col_send(jnp.concatenate([down_own, wide(down_sent)], axis=1), 1)
    down_moved = col_swap(down_sent, 1)
    down_row, act, gates, ups, down_sent = meet(down_row, act, gates, ups, down_sent)

    grad_gate, grad_up = [None, None], [None, None]

    def hidden_back(which, gate_value, up_value):
        grad_gate[which], grad_up[which], back = token_call(
            backward_kernel,
            [gate_value, up_value, cotangents[which]],
            (down_near, down_row, *weights),
            ((units, jnp.bfloat16), (units, jnp.bfloat16), (2 * half, jnp.bfloat16)),
        )
        return back

    def exchange(partial):
        return partial[:, :half], narrow(partial[:, half:])

    near_back, gates[1], ups[1] = core_sum(hidden_back(0, gates[0], ups[0]), gates[1], ups[1])
    back_to_far = over_x(narrow(near_back))
    far_back, grad_gate, grad_up, act, down_moved = core_sum(
        hidden_back(1, gates[1], ups[1]), grad_gate, grad_up, act, down_moved
    )
    back_from_far = over_x(narrow(far_back))
    down_sent, down_kept = col_add(down_kept, down_moved)
    down_moved = col_swap(down_sent, 2)
    gate_own, gate_sent = weight_grads(grad_gate, normed_two, units // 3)
    gate_moved = over_row(gate_sent)
    grad_up, act, gate_sent = meet(grad_up, act, gate_sent)
    up_own, up_sent = weight_grads(grad_up, normed_two, units // 3)
    outs = [token_call(out_kernel, [one], (down_near, down_row), ((2 * half, jnp.bfloat16),))[0] for one in act]
    received, outs, up_sent = hop(over_core, jnp.stack([outs[0][size:], outs[1][size:]]), outs, up_sent)
    near_out, far_out = (wide(out[:size]) + wide(received[which]) for which, out in enumerate(outs))
    back_to_far, back_from_far, gate_moved, up_sent, down_moved, far_out, near_out = meet(
        back_to_far, back_from_far, gate_moved, up_sent, down_moved, far_out, near_out
    )

    up_moved = over_row(up_sent)
    out_from_far = over_x(narrow(far_out))
    gate_sent, gate_kept = col_send(gate_own + wide(gate_moved), 1)
    gate_moved = col_swap(gate_sent, 1)
    down_own, down_sent = exchange(col_last(down_kept, down_moved))
    back_sums = (near_back + wide(back_from_far), far_back + wide(back_to_far))
    grad_hidden, low = [], []
    for which, cotangent_rows in ((0, near_grads[0]), (1, far_grads[0])):
        grads = wide(cotangent_rows) + norm_backward(
            back_sums[which], hiddens[which], scale_two[which], gain_two
        )
        grad_hidden.append(grads)
        low.append(narrow(grads))
    received, low = hop(over_core, jnp.stack(low), low)
    grad_mixed = [jnp.concatenate([low[which], received[which]], axis=0) for which in (0, 1)]
    gain_two_grad = jnp.sum(back_sums[0] * hidden_near * scale_two[0], axis=0)

    grad_projected = [None, None]

    def mix_back(which):
        grad_y = dot_nt(grad_mixed[which], out_rows).reshape(2, size, width)
        grad_conv = grad_y * saved[which][1]
        return grad_y, grad_conv, grad_conv[:, :2]

    def project_back(which, grad_y, grad_conv, following):
        input_gate, output_gate, values_part, mix_input, prior_one, prior_two, convolved = saved[which]
        conv_local = jnp.stack(
            [
                jnp.sum(grad_conv * prior_two, axis=(0, 1)),
                jnp.sum(grad_conv * prior_one, axis=(0, 1)),
                jnp.sum(grad_conv * mix_input, axis=(0, 1)),
            ]
        )
        extended = jnp.concatenate([grad_conv, following], axis=1)
        grad_mix = (
            taps[2] * grad_conv
            + taps[1] * (next_one[which] * extended[:, 1 : size + 1])
            + taps[0] * (next_two[which] * extended[:, 2:])
        )
        grad_projected[which] = narrow(
            jnp.concatenate([grad_mix * values_part, grad_y * convolved, grad_mix * input_gate], axis=2)
        ).reshape(2 * size, 3 * width)
        return dot_nn(grad_projected[which], in_rows), conv_local

    far_y, far_conv, far_start = mix_back(1)
    near_y, near_conv, near_start = mix_back(0)
    starts, far_conv, near_conv = hop(over_row, jnp.stack([near_start, far_start]), far_conv, near_conv)
    far_one, far_taps = project_back(1, far_y, far_conv, starts[1])
    far_one, near_conv = core_sum(far_one, near_conv)
    one_from_far = over_x(narrow(far_one))
    near_one, near_taps = project_back(0, near_y, near_conv, starts[0])
    near_one, grad_projected, normed_one, mixed, gate_moved = core_sum(
        near_one, grad_projected, normed_one, mixed, gate_moved
    )
    conv_local = near_taps + far_taps
    gate_sent, gate_kept = col_add(gate_kept, gate_moved)
    gate_moved = col_swap(gate_sent, 2)
    mixer_own, mixer_sent = exchange(
        jnp.concatenate(
            [
                dot_tn(grad_projected[0], normed_one[0]) + dot_tn(grad_projected[1], normed_one[1]),
                dot_tn(mixed[0], grad_mixed[0]) + dot_tn(mixed[1], grad_mixed[1]),
            ],
            axis=0,
        )
    )
    up_moved, mixer_sent, gate_moved, down_sent = meet(up_moved, mixer_sent, gate_moved, down_sent)
    mixer_moved = over_row(mixer_sent)
    up_sent, up_kept = col_send(up_own + wide(up_moved), 1)
    up_moved = col_swap(up_sent, 1)
    out_from_far, one_from_far, mixer_sent, up_sent = meet(out_from_far, one_from_far, mixer_sent, up_sent)
    result = narrow(hidden_near + (near_out + wide(out_from_far)))
    grad_normed_one = near_one + wide(one_from_far)
    own_inputs = wide(near_tokens[0])
    own_scale = scale_one[0][:size]
    input_grad = grad_hidden[0] + norm_backward(grad_normed_one, own_inputs, own_scale, gain_one)
    gain_one_grad = jnp.sum(grad_normed_one * own_inputs * own_scale, axis=0)
    down_total = down_own + wide(over_row(down_sent))
    gate_total = col_last(gate_kept, gate_moved)
    up_moved, mixer_moved = meet(up_moved, mixer_moved)
    up_sent, up_kept = col_add(up_kept, up_moved)
    up_moved = col_swap(up_sent, 2)
    mixer_sent, mixer_kept = col_send(mixer_own + wide(mixer_moved), 4)
    mixer_moved = col_swap(mixer_sent, 1)
    up_total = col_last(up_kept, up_moved)
    mixer_sent, mixer_kept = col_add(mixer_kept, mixer_moved)
    mixer_total = col_last(mixer_kept, col_swap(mixer_sent, 2))

    gain_local = jnp.stack([gain_one_grad, gain_two_grad])
    conv_flat = conv_local.reshape(3, cols, channels).transpose(1, 0, 2).reshape(cols, 3 * channels)
    apart = jnp.arange(cols) ^ col
    conv_flat = jnp.take(conv_flat, apart // 2 + apart % 2 * 2, axis=0).reshape(-1)
    sent = jnp.concatenate([gain_local[:, half:].reshape(-1), conv_flat])
    small = jnp.concatenate([gain_local[:, :half].reshape(-1), conv_flat]) + over_row(sent)
    for distance in (1, 2):
        small = small + col_swap(small, distance)
    conv_own = lax.dynamic_slice_in_dim(small[2 * half :], col * 3 * channels, 3 * channels, 0)
    conv_wide = lax.dynamic_update_slice(
        jnp.zeros((TEAM * 3 * channels,), jnp.float32), conv_own, (place * 3 * channels,)
    )
    small = jnp.concatenate([small[: 2 * half], conv_wide])
    small = small + over_x(small)
    small = small + over_core(small)
    small = other_teams(small)
    conv_grad = small[2 * half :].reshape(TEAM, 3, channels).transpose(1, 0, 2).reshape(3, TEAM * channels)

    down_grad = wide(team_rows(down_total, 1)[0])
    gate_grad = wide(team_rows(gate_total, 1)[0].T)
    up_grad = wide(team_rows(up_total, 1)[0].T)
    mixer_grads = team_rows(mixer_total, 4)
    in_grad = wide(mixer_grads[:3].transpose(2, 0, 1))
    out_grad = wide(mixer_grads[3])
    return (
        to_blocks(result, jnp.bfloat16),
        to_blocks(input_grad, jnp.float32),
        small[:half],
        in_grad,
        conv_grad,
        out_grad,
        small[half : 2 * half],
        gate_grad,
        up_grad,
        down_grad,
    )


def solution(mesh):
    return jax.shard_map(
        body,
        mesh=mesh,
        in_specs=(
            P(("dp", "col"), "row"),
            P(("dp", "row")),
            P(("dp", "col"), "row"),
            P("row"),
            P("row", None, "col"),
            P(None, "col"),
            P("col", "row"),
            P("row"),
            P("row", "col"),
            P("row", "col"),
            P("col", "row"),
        ),
        out_specs=(
            P(("dp", "col"), "row"),
            P(("dp", "col"), "row"),
            P("row"),
            P("row", None, "col"),
            P(None, "col"),
            P("col", "row"),
            P("row"),
            P("row", "col"),
            P("row", "col"),
            P("col", "row"),
        ),
        check_vma=False,
    )
```

time: 682 us -> 534 us (0.78)
  matrix products: 115 us -> 15.3 us
  waiting for transfers between devices: 308 us -> 220 us
  Pallas kernels: 0 us -> 74.4 us
  starting transfers between devices: 120 us -> 51.4 us
  other arithmetic: 57.7 us -> 94.1 us
    ppermute x27 -> x0, waiting for transfers between devices: 126 us -> none  [over_col(): lax.ppermute(values, 'col', [(i, (i + shift) % size) for i in range(size)])]
    ppermute x2 -> x18, waiting for transfers between devices: 7.24 us -> 119 us  [col_swap(): return lax.ppermute(values, 'col', [(i, i ^ distance) for i in range(size)])]
    ppermute x27 -> x0, starting transfers between devices: 83.3 us -> none  [over_col(): lax.ppermute(values, 'col', [(i, (i + shift) % size) for i in range(size)])]
    pallas_call x0 -> x9, Pallas kernels: none -> 74.4 us  [the longest x6 52 us: token_call(): pl.pallas_call(kernel, grid=(tokens // ROWS,), in_specs=[row_tiles(one) f...]
    dot_general x10 -> x4, matrix products: 45.4 us -> 5.14 us  [dot_nt(): lax.dot_general(left, right, (((1,), (1,)), ((), ())), preferred_element_...]
    ppermute x19 -> x17, waiting for transfers between devices: 78 us -> 38.2 us  [over_row(): return lax.ppermute(values, 'row', [(0, 1), (1, 0)])]
    ppermute x36 -> x34, waiting for transfers between devices: 96.3 us -> 62.9 us  [over_dp(): return lax.ppermute(values, 'dp', [(i, i ^ distance) for i in range(size)])]
    dot_general x10 -> x4, matrix products: 36.7 us -> 5 us  [dot_nn(): lax.dot_general(left, right, (((1,), (0,)), ((), ())), preferred_element_...]
  transfers between devices with their start and end apart: 84 -> 69, of which waited for: 31 -> 37; matrix products, arithmetic and copies ran while one was open for 30% -> 21% of each run, Pallas kernels for 0% -> 9%
where the time goes in v2:
time: 534 us; the launch traced here: 526 us
  waiting for transfers between devices  220 us (41%)
  other arithmetic  94.1 us (18%)
  Pallas kernels  74.4 us (14%)
  local copies, waits for them, and re-layouts  68.5 us (13%)
  starting transfers between devices  51.4 us (10%)
  matrix products  15.3 us (3%)
    ppermute x18, waiting for transfers between devices, col_swap(): return lax.ppermute(values, 'col', [(i, i ^ distance) for i in range(size)])  119 us
    ppermute x34, waiting for transfers between devices, over_dp(): return lax.ppermute(values, 'dp', [(i, i ^ distance) for i in range(size)])  62.9 us
    pallas_call x6, Pallas kernels, token_call(): pl.pallas_call(kernel, grid=(tokens // ROWS,), in_specs=[row_tiles(one) f...  52 us
    ppermute x17, waiting for transfers between devices, over_row(): return lax.ppermute(values, 'row', [(0, 1), (1, 0)])  38.2 us
    unnamed x221, local copies, waits for them, and re-layouts  32.4 us
    pallas_call x3, Pallas kernels, weight_grads(): pl.pallas_call(weight_kernel, grid=(columns // tile,), in_specs=[left_spe...  22.4 us
    convert_element_type x10, other arithmetic, narrow(): return values.astype(jnp.bfloat16)  22.4 us
    ppermute x34, starting transfers between devices, over_dp(): return lax.ppermute(values, 'dp', [(i, i ^ distance) for i in range(size)])  19.9 us
  transfers between devices with their start and end apart: 69, of which 37 were waited for; matrix products, arithmetic and copies ran while one was open for 21% of the time, Pallas kernels for 9%

profile of v2, /device:TPU:0, one launch (start us, length us, event | category | flops | bytes accessed | tf_op | source)
XLA Modules:
  0.0 526.3 jit_solution(12104817946390414454)
XLA Ops:
  32.2 7.9 %collective-permute-done.7 = s32[1024]{0:T(1024)S(1)} collective-permute-done((s32[1024]{0:T(1024)S(1)}, s32[1024]{0:T(1024)S(1)}, u32[]{:S(2)}, u32[]{:S(2)}) %collective-permute-start.7) | collective-permute-done | bytes 4128 | tf_op jit(solution)/shard_map/ppermute | solution.py:26
  51.6 9.4 %collective-permute-done.12 = bf16[288,512]{1,0:T(8,128)(2,1)S(1)} collective-permute-done((bf16[288,512]{1,0:T(8,128)(2,1)}, bf16[288,512]{1,0:T(8,128)(2,1)S(1)}, u32[]{:S(2)}, u32[]{:S(2)}) %collective-permute-start.12) | collective-permute-done | bytes 294944 | tf_op jit(solution)/shard_map/ppermute | solution.py:43
  64.7 6.9 %fusion.5 = (bf16[1024,1024]{1,0:T(8,128)(2,1)S(1)}, bf16[1024,1024]{1,0:T(8,128)(2,1)S(1)}) fusion(f32[1024]{0:T(1024)S(1)} %add_rsqrt_fusion, f32[1024]{0:T(1024)S(1)} %bitcast.300, bf16[512,1024]{1,0:T(8,128)(2,1)S(1)} %get-tuple-element.338, bf16[512,1024]{1,0:T(8,128)(2,1)S(1)} %copy-done.12, f32[1024]{0:T(1024)S(1)} %add_rsqrt_fusion.1, ...), kind=kLoop, calls=%fused_computation.11 | loop fusion | flops 16777216 | bytes 8400896 | tf_op jit(solution)/shard_map/convert_element_type | solution.py:47
  90.7 14.1 %collective-permute-done.16 = bf16[288,512]{1,0:T(8,128)(2,1)S(1)} collective-permute-done((bf16[288,512]{1,0:T(8,128)(2,1)S(1)}, bf16[288,512]{1,0:T(8,128)(2,1)S(1)}, u32[]{:S(2)}, u32[]{:S(2)}) %collective-permute-start.16) | collective-permute-done | bytes 294944 | tf_op jit(solution)/shard_map/ppermute | solution.py:43
  109.2 8.6 %collective-permute-done.21.gate_row = bf16[1152,512]{1,0:T(8,128)(2,1)S(1)} collective-permute-done((bf16[1152,512]{1,0:T(8,128)(2,1)S(1)}, bf16[1152,512]{1,0:T(8,128)(2,1)S(1)}, u32[]{:S(2)}, u32[]{:S(2)}) %collective-permute-start.21) | collective-permute-done | bytes 1179680 | tf_op jit(solution)/shard_map/ppermute | solution.py:38
  117.8 7.0 %collective-permute-done.22 = bf16[2,288,512]{2,1,0:T(8,128)(2,1)S(1)} collective-permute-done((bf16[2,288,512]{2,1,0:T(8,128)(2,1)S(1)}, bf16[2,288,512]{2,1,0:T(8,128)(2,1)S(1)}, u32[]{:S(2)}, u32[]{:S(2)}) %collective-permute-start.22) | collective-permute-done | bytes 589856 | tf_op jit(solution)/shard_map/ppermute | solution.py:43
  124.9 5.6 %collective-permute-done.20 = bf16[512,1024]{1,0:T(8,128)(2,1)S(1)} collective-permute-done((bf16[512,1024]{1,0:T(8,128)(2,1)S(1)}, bf16[512,1024]{1,0:T(8,128)(2,1)S(1)}, u32[]{:S(2)}, u32[]{:S(2)}) %collective-permute-start.20) | collective-permute-done | bytes 1048608 | tf_op jit(solution)/shard_map/ppermute | solution.py:26
  133.2 14.4 %collective-permute-done.24 = bf16[288,512]{1,0:T(8,128)(2,1)S(1)} collective-permute-done((bf16[288,512]{1,0:T(8,128)(2,1)S(1)}, bf16[288,512]{1,0:T(8,128)(2,1)S(1)}, u32[]{:S(2)}, u32[]{:S(2)}) %collective-permute-start.24) | collective-permute-done | bytes 294944 | tf_op jit(solution)/shard_map/ppermute | solution.py:43
  147.8 15.2 %collective-permute-done.26 = bf16[2,288,512]{2,1,0:T(8,128)(2,1)S(1)} collective-permute-done((bf16[2,288,512]{2,1,0:T(8,128)(2,1)S(1)}, bf16[2,288,512]{2,1,0:T(8,128)(2,1)S(1)}, u32[]{:S(2)}, u32[]{:S(2)}) %collective-permute-start.26) | collective-permute-done | bytes 589856 | tf_op jit(solution)/shard_map/ppermute | solution.py:43
  170.6 8.5 %shard_map.187 = (bf16[1024,1152]{1,0:T(8,128)(2,1)}, bf16[1024,1152]{1,0:T(8,128)(2,1)}, bf16[1024,1152]{1,0:T(8,128)(2,1)}) custom-call(bf16[1024,1024]{1,0:T(8,128)(2,1)} %pad_maximum_fusion.7.normed.right_far, bf16[1152,512]{1,0:T(8,128)(2,1)S(1)} %bitcast.222, bf16[1152,512]{1,0:T(8,128)(2,1)S(1)} %collective-permute-done.21.gate_row, ...), custom_call_target="tpu_custom_call" | custom-call | tf_op jit(solution)/shard_map/pallas_call | solution.py:154
  180.7 8.4 %shard_map.186 = (bf16[1024,1152]{1,0:T(8,128)(2,1)}, bf16[1024,1152]{1,0:T(8,128)(2,1)}, bf16[1024,1152]{1,0:T(8,128)(2,1)}) custom-call(bf16[1024,1024]{1,0:T(8,128)(2,1)} %pad_maximum_fusion.6.normed.right_near, bf16[1152,512]{1,0:T(8,128)(2,1)S(1)} %bitcast.223, bf16[1152,512]{1,0:T(8,128)(2,1)S(1)} %collective-permute-done.21.gate_row, ...), custom_call_target="tpu_custom_call" | custom-call | tf_op jit(solution)/shard_map/pallas_call | solution.py:154
  189.2 7.4 %shard_map.188 = (f32[1152,512]{1,0:T(8,128)}, bf16[1152,512]{1,0:T(8,128)(2,1)S(1)}) custom-call(bf16[1024,1152]{1,0:T(8,128)(2,1)} %get-tuple-element.217.left_near.act, bf16[1024,1152]{1,0:T(8,128)(2,1)} %get-tuple-element.218.left_far.act, bf16[1024,1024]{1,0:T(8,128)(2,1)S(1)} %pad_maximum_fusion.8.right_near.cotangent, ...), custom_call_target="tpu_custom_call" | custom-call | tf_op jit(solution)/shard_map/pallas_call | solution.py:211
  200.9 12.7 %shard_map.189 = (bf16[1024,1152]{1,0:T(8,128)(2,1)}, bf16[1024,1152]{1,0:T(8,128)(2,1)}, bf16[1024,1024]{1,0:T(8,128)(2,1)}) custom-call(bf16[1024,1152]{1,0:T(8,128)(2,1)} %get-tuple-element.193.gate, bf16[1024,1152]{1,0:T(8,128)(2,1)} %get-tuple-element.194.up, bf16[1024,1024]{1,0:T(8,128)(2,1)} %copy-done.5, bf16[1152,512]{1,0:T(8,128)(2,1)S(1)} %bitcast.232, ...), custom_call_target="tpu_custom_call" | custom-call | tf_op jit(solution)/shard_map/pallas_call | solution.py:154
  217.6 12.8 %shard_map.190 = (bf16[1024,1152]{1,0:T(8,128)(2,1)}, bf16[1024,1152]{1,0:T(8,128)(2,1)}, bf16[1024,1024]{1,0:T(8,128)(2,1)}) custom-call(bf16[1024,1152]{1,0:T(8,128)(2,1)} %get-tuple-element.200.gate, bf16[1024,1152]{1,0:T(8,128)(2,1)} %get-tuple-element.201.up, bf16[1024,1024]{1,0:T(8,128)(2,1)} %copy-done.4, bf16[1152,512]{1,0:T(8,128)(2,1)S(1)} %bitcast.233, ...), custom_call_target="tpu_custom_call" | custom-call | tf_op jit(solution)/shard_map/pallas_call | solution.py:154
  232.1 11.2 %collective-permute-done.34 = bf16[1,576,1024]{2,1,0:T(8,128)(2,1)S(1)} collective-permute-done((bf16[1,576,1024]{2,1,0:T(8,128)(2,1)S(1)}, bf16[1,576,1024]{2,1,0:T(8,128)(2,1)S(1)}, u32[]{:S(2)}, u32[]{:S(2)}) %collective-permute-start.34) | collective-permute-done | bytes 1179680 | tf_op jit(solution)/shard_map/ppermute | solution.py:43
  244.4 7.3 %shard_map.191 = (f32[1152,512]{1,0:T(8,128)}, bf16[1152,512]{1,0:T(8,128)(2,1)S(1)}) custom-call(bf16[1024,1152]{1,0:T(8,128)(2,1)} %get-tuple-element.210.left_near, bf16[1024,1152]{1,0:T(8,128)(2,1)} %get-tuple-element.211.left_far, bf16[1024,1024]{1,0:T(8,128)(2,1)S(1)} %copy-done.3, bf16[1024,1024]{1,0:T(8,128)(2,1)S(1)} %copy-done.2), custom_call_target="tpu_custom_call" | custom-call | tf_op jit(solution)/shard_map/pallas_call | solution.py:211
  276.2 7.7 %shard_map.194 = (f32[1152,512]{1,0:T(8,128)}, bf16[1152,512]{1,0:T(8,128)(2,1)S(1)}) custom-call(bf16[1024,1152]{1,0:T(8,128)(2,1)} %get-tuple-element.219.left_near, bf16[1024,1152]{1,0:T(8,128)(2,1)} %get-tuple-element.220.left_far, bf16[1024,1024]{1,0:T(8,128)(2,1)S(1)} %copy-done.3, bf16[1024,1024]{1,0:T(8,128)(2,1)S(1)} %copy-done.2), custom_call_target="tpu_custom_call" | custom-call | tf_op jit(solution)/shard_map/pallas_call | solution.py:211
  293.6 9.9 %collective-permute-done.38 = bf16[1,288,1024]{2,1,0:T(8,128)(2,1)} collective-permute-done((bf16[1,288,1024]{2,1,0:T(8,128)(2,1)}, bf16[1,288,1024]{2,1,0:T(8,128)(2,1)}, u32[]{:S(2)}, u32[]{:S(2)}) %collective-permute-start.38) | collective-permute-done | bytes 589856 | tf_op jit(solution)/shard_map/ppermute | solution.py:43
  303.5 11.3 %collective-permute-done.35 = bf16[512,1024]{1,0:T(8,128)(2,1)} collective-permute-done((bf16[512,1024]{1,0:T(8,128)(2,1)}, bf16[512,1024]{1,0:T(8,128)(2,1)}, u32[]{:S(2)}, u32[]{:S(2)}) %collective-permute-start.35) | collective-permute-done | bytes 1048608 | tf_op jit(solution)/shard_map/ppermute | solution.py:26
  400.1 11.0 %collective-permute-done.43 = bf16[512,1024]{1,0:T(8,128)(2,1)} collective-permute-done((bf16[512,1024]{1,0:T(8,128)(2,1)}, bf16[512,1024]{1,0:T(8,128)(2,1)}, u32[]{:S(2)}, u32[]{:S(2)}) %collective-permute-start.43) | collective-permute-done | bytes 1048608 | tf_op jit(solution)/shard_map/ppermute | solution.py:26
  438.7 9.0 %collective-permute-done.48 = bf16[512,512]{1,0:T(8,128)(2,1)} collective-permute-done((bf16[512,512]{1,0:T(8,128)(2,1)}, bf16[512,512]{1,0:T(8,128)(2,1)}, u32[]{:S(2)}, u32[]{:S(2)}) %collective-permute-start.48) | collective-permute-done | bytes 524320 | tf_op jit(solution)/shard_map/ppermute | solution.py:38
  457.7 11.8 %collective-permute-done.56 = bf16[1024,512]{1,0:T(8,128)(2,1)S(1)} collective-permute-done((bf16[1024,512]{1,0:T(8,128)(2,1)}, bf16[1024,512]{1,0:T(8,128)(2,1)S(1)}, u32[]{:S(2)}, u32[]{:S(2)}) %collective-permute-start.56) | collective-permute-done | bytes 1048608 | tf_op jit(solution)/shard_map/ppermute | solution.py:38
  480.1 7.6 %collective-permute-done.63 = bf16[1,288,512]{2,1,0:T(8,128)(2,1)} collective-permute-done((bf16[1,288,512]{2,1,0:T(8,128)(2,1)}, bf16[1,288,512]{2,1,0:T(8,128)(2,1)}, u32[]{:S(2)}, u32[]{:S(2)}) %collective-permute-start.63) | collective-permute-done | bytes 294944 | tf_op jit(solution)/shard_map/ppermute | solution.py:43
  498.0 9.1 %collective-permute-done.58 = bf16[4,64,512]{2,1,0:T(8,128)(2,1)S(1)} collective-permute-done((bf16[4,64,512]{2,1,0:T(8,128)(2,1)S(1)}, bf16[4,64,512]{2,1,0:T(8,128)(2,1)S(1)}, u32[]{:S(2)}, u32[]{:S(2)}) %collective-permute-start.58) | collective-permute-done | bytes 262176 | tf_op jit(solution)/shard_map/ppermute | solution.py:43
  (548 shorter events, 288.4 us)
Async XLA Ops:
  2.9 22.7 %collective-permute-start.1 = (bf16[512,512]{1,0:T(8,128)(2,1)S(1)}, bf16[512,512]{1,0:T(8,128)(2,1)}, u32[]{:S(2)}, u32[]{:S(2)}) collective-permute-start(bf16[512,512]{1,0:T(8,128)(2,1)S(1)} %get-tuple-element.352), channel_id=1, source_target_pairs={{0,16},{8,24},{16,0},{24,8},{1,17},{9,25},{17,1},{25,9},{2,18},{10... | collective-permute-start | bytes 1572872 | tf_op jit(solution)/shard_map/ppermute | solution.py:26
  48.8 27.7 %collective-permute-start.9 = (bf16[1024,512]{1,0:T(8,128)(2,1)S(1)}, bf16[1024,512]{1,0:T(8,128)(2,1)S(1)}, u32[]{:S(2)}, u32[]{:S(2)}) collective-permute-start(bf16[1024,512]{1,0:T(8,128)(2,1)S(1)} %bitcast.251), channel_id=1, source_target_pairs={{0,4},{4,0},{1,5},{5,1},{2,6},{6,2},{3,7},{7,3},{8,12},{12,8},{9,1... | collective-permute-start | bytes 3145736 | tf_op jit(solution)/shard_map/ppermute | solution.py:38
  49.4 22.2 %collective-permute-start.10 = (bf16[512,512]{1,0:T(8,128)(2,1)S(1)}, bf16[512,512]{1,0:T(8,128)(2,1)S(1)}, u32[]{:S(2)}, u32[]{:S(2)}) collective-permute-start(bf16[512,512]{1,0:T(8,128)(2,1)S(1)} %get-tuple-element.141), channel_id=1, source_target_pairs={{0,16},{8,24},{16,0},{24,8},{1,17},{9,25},{17,1},{25,9},{2,18},{10... | collective-permute-start | bytes 1572872 | tf_op jit(solution)/shard_map/ppermute | solution.py:26
  50.9 23.5 %collective-permute-start.11 = (bf16[512,512]{1,0:T(8,128)(2,1)}, bf16[512,512]{1,0:T(8,128)(2,1)S(1)}, u32[]{:S(2)}, u32[]{:S(2)}) collective-permute-start(bf16[512,512]{1,0:T(8,128)(2,1)} %collective-permute-done.6), channel_id=1, source_target_pairs={{0,16},{8,24},{16,0},{24,8},{1,17},{9,25},{17,1},{25,9},{2,18},{10... | collective-permute-start | bytes 1572872 | tf_op jit(solution)/shard_map/ppermute | solution.py:26
  89.7 28.2 %collective-permute-start.21 = (bf16[1152,512]{1,0:T(8,128)(2,1)S(1)}, bf16[1152,512]{1,0:T(8,128)(2,1)S(1)}, u32[]{:S(2)}, u32[]{:S(2)}) collective-permute-start(bf16[1152,512]{1,0:T(8,128)(2,1)S(1)} %bitcast.221), channel_id=1, source_target_pairs={{0,4},{4,0},{1,5},{5,1},{2,6},{6,2},{3,7},{7,3},{8,12},{12,8},{9,1... | collective-permute-start | bytes 3538952 | tf_op jit(solution)/shard_map/ppermute | solution.py:38
  90.6 57.1 %collective-permute-start.23 = (bf16[2,512,1024]{2,1,0:T(8,128)(2,1)S(1)}, bf16[2,512,1024]{2,1,0:T(8,128)(2,1)S(1)}, u32[]{:S(2)}, u32[]{:S(2)}) collective-permute-start(bf16[2,512,1024]{2,1,0:T(8,128)(2,1)S(1)} %pad_maximum_fusion.5), channel_id=1, source_target_pairs={{0,8},{8,0},{16,24},{24,16},{1,9},{9,1},{17,25},{25,17},{2,10},{10... | collective-permute-start | bytes 6291464 | tf_op jit(solution)/shard_map/ppermute | solution.py:26
  105.2 25.2 %collective-permute-start.20 = (bf16[512,1024]{1,0:T(8,128)(2,1)S(1)}, bf16[512,1024]{1,0:T(8,128)(2,1)S(1)}, u32[]{:S(2)}, u32[]{:S(2)}) collective-permute-start(bf16[512,1024]{1,0:T(8,128)(2,1)S(1)} %fusion.25), channel_id=1, source_target_pairs={{0,16},{8,24},{16,0},{24,8},{1,17},{9,25},{17,1},{25,9},{2,18},{10... | collective-permute-start | bytes 3145736 | tf_op jit(solution)/shard_map/ppermute | solution.py:26
  109.0 22.1 %collective-permute-start.19 = (bf16[512,1024]{1,0:T(8,128)(2,1)S(1)}, bf16[512,1024]{1,0:T(8,128)(2,1)S(1)}, u32[]{:S(2)}, u32[]{:S(2)}) collective-permute-start(bf16[512,1024]{1,0:T(8,128)(2,1)S(1)} %slice.809), channel_id=1, source_target_pairs={{0,8},{8,0},{16,24},{24,16},{1,9},{9,1},{17,25},{25,17},{2,10},{10... | collective-permute-start | bytes 3145736 | tf_op jit(solution)/shard_map/ppermute | solution.py:26
  130.6 32.5 %collective-permute-start.25 = (bf16[1152,512]{1,0:T(8,128)(2,1)S(1)}, bf16[1152,512]{1,0:T(8,128)(2,1)S(1)}, u32[]{:S(2)}, u32[]{:S(2)}) collective-permute-start(bf16[1152,512]{1,0:T(8,128)(2,1)S(1)} %bitcast.226), channel_id=1, source_target_pairs={{0,4},{4,0},{1,5},{5,1},{2,6},{6,2},{3,7},{7,3},{8,12},{12,8},{9,1... | collective-permute-start | bytes 3538952 | tf_op jit(solution)/shard_map/ppermute | solution.py:38
  131.8 31.2 %collective-permute-start.27 = (bf16[512,1024]{1,0:T(8,128)(2,1)S(1)}, bf16[512,1024]{1,0:T(8,128)(2,1)S(1)}, u32[]{:S(2)}, u32[]{:S(2)}) collective-permute-start(bf16[512,1024]{1,0:T(8,128)(2,1)S(1)} %get-tuple-element.333), channel_id=1, source_target_pairs={{0,16},{8,24},{16,0},{24,8},{1,17},{9,25},{17,1},{25,9},{2,18},{10... | collective-permute-start | bytes 3145736 | tf_op jit(solution)/shard_map/ppermute | solution.py:26
  166.1 32.9 %collective-permute-start.28 = (bf16[1152,512]{1,0:T(8,128)(2,1)S(1)}, bf16[1152,512]{1,0:T(8,128)(2,1)S(1)}, u32[]{:S(2)}, u32[]{:S(2)}) collective-permute-start(bf16[1152,512]{1,0:T(8,128)(2,1)S(1)} %bitcast.231), channel_id=1, source_target_pairs={{0,4},{4,0},{1,5},{5,1},{2,6},{6,2},{3,7},{7,3},{8,12},{12,8},{9,1... | collective-permute-start | bytes 3538952 | tf_op jit(solution)/shard_map/ppermute | solution.py:38
  215.1 28.2 %collective-permute-start.34 = (bf16[1,576,1024]{2,1,0:T(8,128)(2,1)S(1)}, bf16[1,576,1024]{2,1,0:T(8,128)(2,1)S(1)}, u32[]{:S(2)}, u32[]{:S(2)}) collective-permute-start(bf16[1,576,1024]{2,1,0:T(8,128)(2,1)S(1)} %fusion.26), channel_id=1, source_target_pairs={{0,1},{1,0},{2,3},{3,2},{4,5},{5,4},{6,7},{7,6},{8,9},{9,8},{10,11... | collective-permute-start | bytes 3538952 | tf_op jit(solution)/shard_map/ppermute | solution.py:43
  267.2 26.4 %collective-permute-start.32 = (bf16[512,1024]{1,0:T(8,128)(2,1)}, bf16[512,1024]{1,0:T(8,128)(2,1)}, u32[]{:S(2)}, u32[]{:S(2)}) collective-permute-start(bf16[512,1024]{1,0:T(8,128)(2,1)} %fusion.18), channel_id=1, source_target_pairs={{0,16},{8,24},{16,0},{24,8},{1,17},{9,25},{17,1},{25,9},{2,18},{10... | collective-permute-start | bytes 3145736 | tf_op jit(solution)/shard_map/ppermute | solution.py:26
  267.9 46.8 %collective-permute-start.36 = (bf16[1152,512]{1,0:T(8,128)(2,1)S(1)}, bf16[1152,512]{1,0:T(8,128)(2,1)}, u32[]{:S(2)}, u32[]{:S(2)}) collective-permute-start(bf16[1152,512]{1,0:T(8,128)(2,1)S(1)} %get-tuple-element.212), channel_id=1, source_target_pairs={{0,4},{4,0},{1,5},{5,1},{2,6},{6,2},{3,7},{7,3},{8,12},{12,8},{9,1... | collective-permute-start | bytes 3538952 | tf_op jit(solution)/shard_map/ppermute | solution.py:38
  270.9 43.9 %collective-permute-start.35 = (bf16[512,1024]{1,0:T(8,128)(2,1)}, bf16[512,1024]{1,0:T(8,128)(2,1)}, u32[]{:S(2)}, u32[]{:S(2)}) collective-permute-start(bf16[512,1024]{1,0:T(8,128)(2,1)} %fusion.19), channel_id=1, source_target_pairs={{0,16},{8,24},{16,0},{24,8},{1,17},{9,25},{17,1},{25,9},{2,18},{10... | collective-permute-start | bytes 3145736 | tf_op jit(solution)/shard_map/ppermute | solution.py:26
  275.8 27.7 %collective-permute-start.38 = (bf16[1,288,1024]{2,1,0:T(8,128)(2,1)}, bf16[1,288,1024]{2,1,0:T(8,128)(2,1)}, u32[]{:S(2)}, u32[]{:S(2)}) collective-permute-start(bf16[1,288,1024]{2,1,0:T(8,128)(2,1)} %slice.811), channel_id=1, source_target_pairs={{0,2},{1,3},{2,0},{3,1},{4,6},{5,7},{6,4},{7,5},{8,10},{9,11},{10,... | collective-permute-start | bytes 1769480 | tf_op jit(solution)/shard_map/ppermute | solution.py:43
  362.2 27.8 %collective-permute-start.44 = (bf16[1152,512]{1,0:T(8,128)(2,1)S(1)}, bf16[1152,512]{1,0:T(8,128)(2,1)}, u32[]{:S(2)}, u32[]{:S(2)}) collective-permute-start(bf16[1152,512]{1,0:T(8,128)(2,1)S(1)} %get-tuple-element.238), channel_id=1, source_target_pairs={{0,4},{4,0},{1,5},{5,1},{2,6},{6,2},{3,7},{7,3},{8,12},{12,8},{9,1... | collective-permute-start | bytes 3538952 | tf_op jit(solution)/shard_map/ppermute | solution.py:38
  363.7 36.5 %collective-permute-start.39 = (bf16[512,1024]{1,0:T(8,128)(2,1)}, bf16[512,1024]{1,0:T(8,128)(2,1)}, u32[]{:S(2)}, u32[]{:S(2)}) collective-permute-start(bf16[512,1024]{1,0:T(8,128)(2,1)} %convert_add_fusion.4), channel_id=1, source_target_pairs={{0,16},{8,24},{16,0},{24,8},{1,17},{9,25},{17,1},{25,9},{2,18},{10... | collective-permute-start | bytes 3145736 | tf_op jit(solution)/shard_map/ppermute | solution.py:26
  370.3 40.9 %collective-permute-start.43 = (bf16[512,1024]{1,0:T(8,128)(2,1)}, bf16[512,1024]{1,0:T(8,128)(2,1)}, u32[]{:S(2)}, u32[]{:S(2)}) collective-permute-start(bf16[512,1024]{1,0:T(8,128)(2,1)} %fusion.17), channel_id=1, source_target_pairs={{0,16},{8,24},{16,0},{24,8},{1,17},{9,25},{17,1},{25,9},{2,18},{10... | collective-permute-start | bytes 3145736 | tf_op jit(solution)/shard_map/ppermute | solution.py:26
  394.5 42.6 %collective-permute-start.66 = (bf16[288,512]{1,0:T(8,128)(2,1)}, bf16[288,512]{1,0:T(8,128)(2,1)}, u32[]{:S(2)}, u32[]{:S(2)}) collective-permute-start(bf16[288,512]{1,0:T(8,128)(2,1)} %slice.814), channel_id=1, source_target_pairs={{0,4},{4,0},{1,5},{5,1},{2,6},{6,2},{3,7},{7,3},{8,12},{12,8},{9,1... | collective-permute-start | bytes 884744 | tf_op jit(solution)/shard_map/ppermute | solution.py:38
  400.1 57.6 %collective-permute-start.55 = (bf16[1,576,512]{2,1,0:T(8,128)(2,1)}, bf16[1,576,512]{2,1,0:T(8,128)(2,1)}, u32[]{:S(2)}, u32[]{:S(2)}) collective-permute-start(bf16[1,576,512]{2,1,0:T(8,128)(2,1)} %fusion.52), channel_id=1, source_target_pairs={{0,1},{1,0},{2,3},{3,2},{4,5},{5,4},{6,7},{7,6},{8,9},{9,8},{10,11... | collective-permute-start | bytes 1769480 | tf_op jit(solution)/shard_map/ppermute | solution.py:43
  422.3 28.2 %collective-permute-start.49 = (bf16[512,512]{1,0:T(8,128)(2,1)}, bf16[512,512]{1,0:T(8,128)(2,1)}, u32[]{:S(2)}, u32[]{:S(2)}) collective-permute-start(bf16[512,512]{1,0:T(8,128)(2,1)} %slice.812), channel_id=1, source_target_pairs={{0,4},{4,0},{1,5},{5,1},{2,6},{6,2},{3,7},{7,3},{8,12},{12,8},{9,1... | collective-permute-start | bytes 1572872 | tf_op jit(solution)/shard_map/ppermute | solution.py:38
  435.5 34.0 %collective-permute-start.56 = (bf16[1024,512]{1,0:T(8,128)(2,1)}, bf16[1024,512]{1,0:T(8,128)(2,1)S(1)}, u32[]{:S(2)}, u32[]{:S(2)}) collective-permute-start(bf16[1024,512]{1,0:T(8,128)(2,1)} %fusion.14), channel_id=1, source_target_pairs={{0,4},{4,0},{1,5},{5,1},{2,6},{6,2},{3,7},{7,3},{8,12},{12,8},{9,1... | collective-permute-start | bytes 3145736 | tf_op jit(solution)/shard_map/ppermute | solution.py:38
  456.5 38.3 %collective-permute-start.68 = (bf16[2,1,288,512]{3,2,1,0:T(8,128)(2,1)}, bf16[2,1,288,512]{3,2,1,0:T(8,128)(2,1)}, u32[]{:S(2)}, u32[]{:S(2)}) collective-permute-start(bf16[2,1,288,512]{3,2,1,0:T(8,128)(2,1)} %pad_maximum_fusion.34), channel_id=1, source_target_pairs={{0,8},{8,0},{16,24},{24,16},{1,9},{9,1},{17,25},{25,17},{2,10},{10... | collective-permute-start | bytes 1769480 | tf_op jit(solution)/shard_map/ppermute | solution.py:26
  (150 other events, 1731.6 us)

commit v3 on v2

v3 whole, which is shorter than its diff:
```python
import jax
import jax.numpy as jnp
from jax import lax
from jax.experimental import pallas as pl
from jax.experimental.pallas import tpu as pltpu
from jax.sharding import PartitionSpec as P

EPSILON = 1e-05
TEAM = 4


def dot_nt(left, right):
    return lax.dot_general(left, right, (((1,), (1,)), ((), ())), preferred_element_type=jnp.float32)


def dot_nn(left, right):
    return lax.dot_general(left, right, (((1,), (0,)), ((), ())), preferred_element_type=jnp.float32)


def dot_tn(left, right):
    return lax.dot_general(left, right, (((0,), (0,)), ((), ())), preferred_element_type=jnp.float32)


def over_dp(values, distance):
    size = lax.axis_size("dp")
    return lax.ppermute(values, "dp", [(i, i ^ distance) for i in range(size)])


def over_core(values):
    return over_dp(values, 1)


def over_x(values):
    return over_dp(values, 2)


def over_row(values):
    return lax.ppermute(values, "row", [(0, 1), (1, 0)])


def col_swap(values, distance):
    size = lax.axis_size("col")
    return lax.ppermute(values, "col", [(i, i ^ distance) for i in range(size)])


def narrow(values):
    return values.astype(jnp.bfloat16)


def wide(values):
    return values.astype(jnp.float32)


def halves(values):
    size = values.shape[0] // 2
    return values[:size], values[size:]


def other_teams(values):
    distance = TEAM
    while distance < lax.axis_size("dp"):
        values = values + over_dp(values, distance)
        distance *= 2
    return values


def after(value, *events):
    return lax.optimization_barrier((value, *events))[0]


def meet(*values):
    return lax.optimization_barrier(values)


def hop(move, value, *waiting):
    return meet(move(value), *waiting)


def stacked(pair, other, parts):
    pieces = jnp.concatenate([pair, other], axis=0)
    if parts > 1:
        pieces = pieces.reshape(4, parts, -1, pair.shape[2]).transpose(1, 0, 2, 3)
    return pieces.reshape(-1, pair.shape[2])


def col_first(piece):
    return jnp.stack([piece, col_swap(piece, 2)])


def col_send(values, parts):
    rows = values.shape[0] // (parts * 4)
    grid = values.reshape(parts, 2, 2 * rows, values.shape[1])
    return narrow(grid[:, 1]), grid[:, 0]


def col_add(kept, received):
    total = kept + wide(received)
    rows = total.shape[1] // 2
    return narrow(total[:, rows:]), total[:, :rows]


def col_last(kept, received):
    return (kept + wide(received)).reshape(-1, kept.shape[2])


def team_first(piece):
    return narrow(other_teams(piece))


def team_rows(own, far, pair, parts):
    rows, half = own.shape[0] // parts, own.shape[1]
    place = lax.axis_index("dp") % TEAM
    result = jnp.zeros((parts, TEAM * rows, half), jnp.bfloat16)
    for distance, block in enumerate((own, pair[0], far, pair[1])):
        block = block.reshape(parts, rows, half)
        result = lax.dynamic_update_slice(result, block, (0, (place ^ distance) * rows, 0))
    return result


def norm_scale(hidden):
    return lax.rsqrt(jnp.mean(hidden * hidden, axis=1, keepdims=True) + EPSILON)


def norm_backward(grad_normed, hidden, row_scale, gain_vector):
    inner_sum = jnp.sum(grad_normed * gain_vector * hidden, axis=1, keepdims=True)
    cubed = row_scale * row_scale * row_scale
    return grad_normed * gain_vector * row_scale - hidden * (cubed / hidden.shape[1]) * inner_sum


def to_blocks(values, received):
    size, half = values.shape
    row = lax.axis_index("row")
    result = jnp.zeros((2 * size, half), values.dtype)
    result = lax.dynamic_update_slice(result, values, (row * size, 0))
    return lax.dynamic_update_slice(result, received.astype(values.dtype), ((1 - row) * size, 0))


ROWS = 256
VMEM_BYTES = 48 * 2**20
COST = pl.CostEstimate(flops=1, bytes_accessed=1, transcendentals=0)


def whole(array):
    return pl.BlockSpec(array.shape, lambda i: (0,) * array.ndim)


def row_tiles(array):
    return pl.BlockSpec((ROWS, array.shape[1]), lambda i: (i, 0))


def token_call(kernel, tiled, resident, outs):
    tokens = tiled[0].shape[0]
    shapes = [jax.ShapeDtypeStruct((tokens, columns), dtype) for columns, dtype in outs]
    return pl.pallas_call(
        kernel,
        grid=(tokens // ROWS,),
        in_specs=[row_tiles(one) for one in tiled] + [whole(one) for one in resident],
        out_specs=[row_tiles(one) for one in shapes],
        out_shape=shapes,
        compiler_params=pltpu.CompilerParams(vmem_limit_bytes=VMEM_BYTES),
        cost_estimate=COST,
    )(*tiled, *resident)


def split_nt(left, near, row):
    half = near.shape[1]
    return dot_nt(left[:, :half], near[...]) + dot_nt(left[:, half:], row[...])


def forward_kernel(normed, gate_near, gate_row, up_near, up_row, gate, up, act):
    gate_value = split_nt(normed, gate_near, gate_row)
    up_value = split_nt(normed, up_near, up_row)
    gate[...] = narrow(gate_value)
    up[...] = narrow(up_value)
    act[...] = narrow(gate_value * jax.nn.sigmoid(gate_value) * up_value)


def backward_kernel(
    gate, up, cotangent, down_near, down_row, gate_near, gate_row, up_near, up_row, grad_gate, grad_up, back
):
    half = gate_near.shape[1]
    grad_act = split_nt(cotangent, down_near, down_row)
    gate_value, up_value = wide(gate[...]), wide(up[...])
    sigmoid_gate = jax.nn.sigmoid(gate_value)
    gated = grad_act * sigmoid_gate
    low_gate = narrow(gated * up_value * (1.0 + gate_value * (1.0 - sigmoid_gate)))
    low_up = narrow(gated * gate_value)
    grad_gate[...] = low_gate
    grad_up[...] = low_up
    back[:, :half] = narrow(dot_nn(low_gate, gate_near[...]) + dot_nn(low_up, up_near[...]))
    back[:, half:] = narrow(dot_nn(low_gate, gate_row[...]) + dot_nn(low_up, up_row[...]))


def out_kernel(act, down_near, down_row, out):
    half = down_near.shape[1]
    out[:, :half] = narrow(dot_nn(act[...], down_near[...]))
    out[:, half:] = narrow(dot_nn(act[...], down_row[...]))


def project_kernel(inputs, gain, in_near, in_row, normed, projected):
    values = wide(inputs[...])
    scale = lax.rsqrt(jnp.mean(values * values, axis=1, keepdims=True) + EPSILON)
    low = narrow(values * scale * gain[...])
    normed[...] = low
    projected[...] = split_nt(low, in_near, in_row)


def mixer_values(projected, flags, before, taps):
    width = taps.shape[1]
    input_gate, output_gate, values_part = (projected[:, part * width : (part + 1) * width] for part in range(3))
    mix_input = input_gate * values_part
    place = lax.broadcasted_iota(jnp.int32, mix_input.shape, 0)
    one, two = before[0, 1:2], before[0, 0:1]
    prior_one = flags[:, 0:1] * jnp.where(place == 0, one, pltpu.roll(mix_input, 1, 0))
    prior_two = jnp.where(place == 0, two, jnp.where(place == 1, one, pltpu.roll(mix_input, 2, 0)))
    prior_two = flags[:, 1:2] * prior_two
    convolved = taps[2:3] * mix_input + taps[1:2] * prior_one + taps[0:1] * prior_two
    return input_gate, output_gate, values_part, mix_input, prior_one, prior_two, convolved


def mix_kernel(projected, flags, before, taps, out_near, out_row, mixed, partial):
    half = out_near.shape[1]
    _, output_gate, _, _, _, _, convolved = mixer_values(projected, flags, before, taps)
    low = narrow(output_gate * convolved)
    mixed[...] = low
    partial[:, :half] = narrow(dot_nn(low, out_near[...]))
    partial[:, half:] = narrow(dot_nn(low, out_row[...]))


def mix_back_kernel(
    grad_mixed, projected, flags, before, behind, taps, out_near, out_row, in_near, in_row, grad_projected, partial, sums
):
    half = out_near.shape[1]
    width = taps.shape[1]
    input_gate, output_gate, values_part, mix_input, prior_one, prior_two, convolved = mixer_values(
        projected, flags, before, taps
    )
    grad_y = split_nt(grad_mixed, out_near, out_row)
    grad_conv = grad_y * output_gate
    for tap, values in enumerate((prior_two, prior_one, mix_input)):
        sums[0, tap : tap + 1] = jnp.sum(grad_conv * values, axis=0, keepdims=True)
    size = grad_conv.shape[0]
    place = lax.broadcasted_iota(jnp.int32, grad_conv.shape, 0)
    one, two = behind[0, 0:1], behind[0, 1:2]
    next_one = jnp.where(place == size - 1, one, pltpu.roll(grad_conv, size - 1, 0))
    next_two = jnp.where(place == size - 2, one, pltpu.roll(grad_conv, size - 2, 0))
    next_two = jnp.where(place == size - 1, two, next_two)
    grad_mix = (
        taps[2:3] * grad_conv
        + taps[1:2] * (flags[:, 2:3] * next_one)
        + taps[0:1] * (flags[:, 3:4] * next_two)
    )
    low = narrow(jnp.concatenate([grad_mix * values_part, grad_y * convolved, grad_mix * input_gate], axis=1))
    grad_projected[...] = low
    partial[:, :half] = narrow(dot_nn(low, in_near[...]))
    partial[:, half:] = narrow(dot_nn(low, in_row[...]))


def sequence_call(kernel, tiled, small, resident, outs, small_outs=()):
    size = tiled[0].shape[0] // 2

    def by_rows(array):
        return pl.BlockSpec((size, array.shape[1]), lambda i: (i, 0))

    def by_first(array):
        return pl.BlockSpec((1, *array.shape[1:]), lambda i: (i, 0, 0))

    shapes = [jax.ShapeDtypeStruct((2 * size, columns), dtype) for columns, dtype in outs]
    small_shapes = [jax.ShapeDtypeStruct((2, *shape), jnp.float32) for shape in small_outs]
    return pl.pallas_call(
        kernel,
        grid=(2,),
        in_specs=[by_rows(one) for one in tiled] + [by_first(one) for one in small] + [whole(one) for one in resident],
        out_specs=[by_rows(one) for one in shapes] + [by_first(one) for one in small_shapes],
        out_shape=shapes + small_shapes,
        compiler_params=pltpu.CompilerParams(vmem_limit_bytes=VMEM_BYTES),
        cost_estimate=COST,
    )(*tiled, *small, *resident)


def weight_kernel(left_near, left_far, right_near, right_far, own, sent):
    total = dot_tn(left_near[...], right_near[...]) + dot_tn(left_far[...], right_far[...])
    half = own.shape[1]
    own[...] = total[:, :half]
    sent[...] = narrow(total[:, half:])


def weight_grads(lefts, rights, tile):
    tokens, columns = lefts[0].shape
    half = rights[0].shape[1] // 2
    left_spec = pl.BlockSpec((tokens, tile), lambda i: (0, i))
    out_spec = pl.BlockSpec((tile, half), lambda i: (i, 0))
    return pl.pallas_call(
        weight_kernel,
        grid=(columns // tile,),
        in_specs=[left_spec, left_spec, whole(rights[0]), whole(rights[1])],
        out_specs=[out_spec, out_spec],
        out_shape=[
            jax.ShapeDtypeStruct((columns, half), jnp.float32),
            jax.ShapeDtypeStruct((columns, half), jnp.bfloat16),
        ],
        compiler_params=pltpu.CompilerParams(vmem_limit_bytes=VMEM_BYTES),
        cost_estimate=COST,
    )(*lefts, *rights)


def body(
    tokens,
    segment_ids,
    cotangent,
    norm1_gain,
    in_weight,
    conv_weight,
    out_weight,
    norm2_gain,
    gate_weight,
    up_weight,
    down_weight,
):
    place = lax.axis_index("dp") % TEAM
    row = lax.axis_index("row")
    col = lax.axis_index("col")
    cols = lax.axis_size("col")
    sequence = tokens.shape[0]
    size = sequence // 2
    half = tokens.shape[1]

    tokens_other = lax.dynamic_slice_in_dim(tokens, (1 - row) * size, size, 0)
    tokens_own = lax.dynamic_slice_in_dim(tokens, row * size, size, 0)
    tokens_row = over_row(tokens_other)
    tokens_x0 = over_x(tokens_own)
    channels = in_weight.shape[2] // TEAM
    hidden = gate_weight.shape[1] // TEAM
    in_part = lax.dynamic_slice_in_dim(in_weight, place * channels, channels, 2)
    in_part = in_part.transpose(1, 2, 0).reshape(3 * channels, half)
    out_part = lax.dynamic_slice_in_dim(out_weight, place * channels, channels, 0)
    taps_part = lax.dynamic_slice_in_dim(conv_weight, place * channels, channels, 1)
    taps_part = jnp.pad(taps_part, ((0, 0), (0, half - channels)))
    gains_part = jnp.pad(jnp.stack([norm1_gain, norm2_gain]), ((0, 11), (0, 0)))
    in_pair = col_first(jnp.concatenate([in_part, taps_part, gains_part, out_part], axis=0))
    grads_other = lax.dynamic_slice_in_dim(cotangent, (1 - row) * size, size, 0)
    grads_own = lax.dynamic_slice_in_dim(cotangent, row * size, size, 0)
    gate_part = lax.dynamic_slice_in_dim(gate_weight, place * hidden, hidden, 1).T
    ids_row = over_row(segment_ids)
    in_pair, tokens_row, tokens_x0, ids_row, grads_other, gate_part = meet(
        in_pair, tokens_row, tokens_x0, ids_row, grads_other, gate_part
    )

    in_other = col_swap(in_pair, 1)
    tokens_x1 = over_x(tokens_row)
    grads_row = over_row(grads_other)
    gate_pair = col_first(gate_part)
    up_part = lax.dynamic_slice_in_dim(up_weight, place * hidden, hidden, 1).T
    down_part = lax.dynamic_slice_in_dim(down_weight, place * hidden, hidden, 0)
    ids = jnp.stack([segment_ids, ids_row])
    ids = lax.dynamic_index_in_dim(ids, (col // 2) ^ row, 0, keepdims=False)
    ids = lax.dynamic_slice_in_dim(ids, (col % 2) * sequence, sequence, 0)
    ids_far = over_x(ids)
    in_other, tokens_x1, grads_row, ids_far, gate_pair, grads_own, ids, up_part, down_part = meet(
        in_other, tokens_x1, grads_row, ids_far, gate_pair, grads_own, ids, up_part, down_part
    )
    in_rows = 3 * channels
    in_near = stacked(in_pair[:, :in_rows], in_other[:, :in_rows], 3)
    in_near = jnp.concatenate([in_near, in_pair[0, in_rows : in_rows + 16]], axis=0)
    out_near = stacked(in_pair[:, in_rows + 16 :], in_other[:, in_rows + 16 :], 1)
    grads_near = jnp.concatenate([grads_own, grads_row], axis=1)
    in_near, out_near, grads_near, up_part, tokens_x1, gate_pair, ids = meet(
        in_near, out_near, grads_near, up_part, tokens_x1, gate_pair, ids
    )

    near = jnp.concatenate([tokens_own, tokens_row], axis=1)
    far = jnp.concatenate([tokens_x0, tokens_x1], axis=1)
    pair, ids_pair = over_core(jnp.stack([near, far])), over_core(jnp.stack([ids, ids_far]))
    pair, ids_pair, in_near, out_near, in_other, grads_near, gate_pair, up_part = meet(
        pair, ids_pair, in_near, out_near, in_other, grads_near, gate_pair, up_part
    )
    in_row = over_row(in_near)
    out_row = over_row(out_near)
    gate_other = col_swap(gate_pair, 1)
    up_pair = col_first(up_part)
    grads_far = over_x(grads_near)
    ids = jnp.stack([ids, ids_pair[0], ids_far, ids_pair[1]])
    keeps = []
    for offset in (1, 2):
        equal = (ids[:, offset:] == ids[:, :-offset]).astype(jnp.float32)
        keeps.append(jnp.pad(equal, ((0, 0), (offset, offset))))
    flags = jnp.stack(
        [
            lax.dynamic_slice_in_dim(keeps[which], row * size + offset, size, 1)
            for which, offset in ((0, 0), (1, 0), (0, 1), (1, 2))
        ],
        axis=2,
    )
    flags = [flags[:2].reshape(2 * size, 4), flags[2:].reshape(2 * size, 4)]
    near_tokens, far_tokens = (near, pair[0]), (far, pair[1])
    inputs = [jnp.concatenate(both, axis=0) for both in (near_tokens, far_tokens)]
    taps = jnp.concatenate(
        [both[which, in_rows : in_rows + 3, :channels] for both in (in_pair, in_other) for which in (0, 1)], axis=1
    )
    taps = wide(taps)
    in_row, out_row, gate_other, up_pair, inputs, taps, flags, down_part = meet(
        in_row, out_row, gate_other, up_pair, inputs, taps, flags, down_part
    )

    width = cols * channels
    gains = jnp.stack([norm1_gain, norm2_gain])
    gains = wide(jnp.concatenate([gains, in_row[4 * in_rows + 3 : 4 * in_rows + 5]], axis=1))
    gain_one, gain_two = gains[0], gains[1]
    in_near, in_row = in_near[: 4 * in_rows], in_row[: 4 * in_rows]
    ends = wide(jnp.concatenate([one[at + size - 8 : at + size] for one in inputs for at in (0, size)], axis=0))
    ends = narrow(ends * norm_scale(ends) * gain_one)
    ends = dot_nt(ends[:, :half], in_near) + dot_nt(ends[:, half:], in_row)
    ends = (ends[:, :width] * ends[:, 2 * width :]).reshape(2, 2, 8, width)[:, :, 6:]
    gate_near = stacked(gate_pair, gate_other, 1)
    before, gate_near, up_pair, down_part, inputs = hop(over_row, ends, gate_near, up_pair, down_part, inputs)
    gate_row = over_row(gate_near)
    up_other = col_swap(up_pair, 1)
    down_pair = col_first(down_part)
    grads_pair = over_core(jnp.stack([grads_near, grads_far]))
    normed_one, projected = zip(
        *[
            token_call(
                project_kernel,
                [one],
                (gain_one[None], in_near, in_row),
                ((2 * half, jnp.bfloat16), (3 * width, jnp.float32)),
            )
            for one in inputs
        ]
    )

    def mix(which):
        return sequence_call(
            mix_kernel,
            [projected[which], flags[which]],
            [before[which]],
            (taps, out_near, out_row),
            ((width, jnp.bfloat16), (2 * half, jnp.bfloat16)),
        )

    def core_sum(partial, *waiting):
        received, *waiting = hop(over_core, narrow(partial[size:]), *waiting)
        return (wide(partial[:size]) + wide(received), *waiting)

    mixed = [None, None]
    mixed[1], far_partial = mix(1)
    mixed[0], near_partial = mix(0)
    up_other, down_pair, gate_row, grads_pair, far_partial, near_partial = meet(
        up_other, down_pair, gate_row, grads_pair, far_partial, near_partial
    )
    up_near = stacked(up_pair, up_other, 1)
    near_grads, far_grads = (grads_near, grads_pair[0]), (grads_far, grads_pair[1])
    cotangents = [jnp.concatenate(both, axis=0) for both in (near_grads, far_grads)]
    received, far_partial, near_partial, up_near, down_pair, cotangents = hop(
        over_core,
        jnp.stack([near_partial[size:], far_partial[size:]]),
        far_partial,
        near_partial,
        up_near,
        down_pair,
        cotangents,
    )
    far_sum = wide(far_partial[:size]) + wide(received[1])
    near_sum = wide(near_partial[:size]) + wide(received[0])
    from_far, to_far = over_x(narrow(far_sum)), over_x(narrow(near_sum))
    up_row = over_row(up_near)
    down_other = col_swap(down_pair, 1)
    from_far, down_other, up_row = meet(from_far, down_other, up_row)
    down_near = stacked(down_pair, down_other, 1)
    from_far, down_near = meet(from_far, down_near)
    down_row = over_row(down_near)
    hidden_near = wide(near_tokens[0]) + (near_sum + wide(from_far))
    scale_near = norm_scale(hidden_near)
    normed_own = narrow(hidden_near * scale_near * gain_two)
    to_far, normed_own = meet(to_far, normed_own)
    hidden_far = wide(far_tokens[0]) + (far_sum + wide(to_far))
    scale_far = norm_scale(hidden_far)
    normed_x = narrow(hidden_far * scale_far * gain_two)
    down_row, normed_own, normed_x = meet(down_row, normed_own, normed_x)
    (pair,) = hop(over_core, jnp.stack([normed_own, normed_x]))
    normed_near = jnp.concatenate([normed_own, pair[0]], axis=0)
    normed_far = jnp.concatenate([normed_x, pair[1]], axis=0)
    hiddens, scale_two, normed_two = (hidden_near, hidden_far), (scale_near, scale_far), (normed_near, normed_far)
    units = gate_near.shape[0]
    weights = (gate_near, gate_row, up_near, up_row)
    wide_outs = ((units, jnp.bfloat16),) * 3

    grad_gate, grad_up = [None, None], [None, None]

    def hidden_back(which, gate_value, up_value):
        grad_gate[which], grad_up[which], back = token_call(
            backward_kernel,
            [gate_value, up_value, cotangents[which]],
            (down_near, down_row, *weights),
            ((units, jnp.bfloat16), (units, jnp.bfloat16), (2 * half, jnp.bfloat16)),
        )
        return back

    def exchange(partial):
        return partial[:, :half], narrow(partial[:, half:])

    gate_value, up_value, act_near = token_call(forward_kernel, [normed_near], weights, wide_outs)
    near_back, normed_far = core_sum(hidden_back(0, gate_value, up_value), normed_far)
    near_send, normed_far = meet(narrow(near_back), normed_far)
    back_to_far = over_x(near_send)
    gate_value, up_value, act_far = token_call(forward_kernel, [normed_far], weights, wide_outs)
    far_partial = hidden_back(1, gate_value, up_value)
    act, normed_two = [act_near, act_far], [normed_near, normed_far]
    back_to_far, far_partial, grad_gate, grad_up, act = meet(back_to_far, far_partial, grad_gate, grad_up, act)
    far_back, grad_gate, grad_up, act = core_sum(far_partial, grad_gate, grad_up, act)
    far_send, grad_gate, grad_up, act = meet(narrow(far_back), grad_gate, grad_up, act)
    back_from_far = over_x(far_send)
    gate_own, gate_sent = weight_grads(grad_gate, normed_two, units // 3)
    gate_moved = over_row(gate_sent)
    gate_sent, grad_up, act = meet(gate_sent, grad_up, act)
    down_own, down_sent = weight_grads(act, cotangents, units // 3)
    down_sent, down_kept = col_send(jnp.concatenate([down_own, wide(down_sent)], axis=1), 1)
    down_moved = col_swap(down_sent, 1)
    down_sent, grad_up, act = meet(down_sent, grad_up, act)
    up_own, up_sent = weight_grads(grad_up, normed_two, units // 3)
    outs = [token_call(out_kernel, [one], (down_near, down_row), ((2 * half, jnp.bfloat16),))[0] for one in act]
    back_from_far, outs, up_sent = meet(back_from_far, outs, up_sent)

    back_sums = (near_back + wide(back_from_far), far_back + wide(back_to_far))
    grad_hidden, low = [], []
    for which, cotangent_rows in ((0, near_grads[0]), (1, far_grads[0])):
        grads = wide(cotangent_rows) + norm_backward(
            back_sums[which], hiddens[which], scale_two[which], gain_two
        )
        grad_hidden.append(grads)
        low.append(narrow(grads))
    gain_two_grad = jnp.sum(back_sums[0] * hidden_near * scale_two[0], axis=0)
    gate_moved, down_moved, low = meet(gate_moved, down_moved, low)
    gate_sent, gate_kept = col_send(gate_own + wide(gate_moved), 1)
    down_sent, down_kept = col_add(down_kept, down_moved)
    low_moved, out_moved = over_core(jnp.stack(low)), over_core(jnp.stack([outs[0][size:], outs[1][size:]]))
    low_moved, out_moved, low, outs, up_sent, gate_sent, down_sent = meet(
        low_moved, out_moved, low, outs, up_sent, gate_sent, down_sent
    )
    grad_mixed = [jnp.concatenate([low[which], low_moved[which]], axis=0) for which in (0, 1)]
    near_out, far_out = (wide(out[:size]) + wide(out_moved[which]) for which, out in enumerate(outs))
    far_out = narrow(far_out)

    starts = jnp.concatenate([one[at : at + 8] for one in grad_mixed for at in (0, size)], axis=0)
    starts = dot_nt(starts[:, :half], out_near) + dot_nt(starts[:, half:], out_row)
    opened = jnp.concatenate([one[at : at + 8, width : 2 * width] for one in projected for at in (0, size)], axis=0)
    starts = (starts * opened).reshape(2, 2, 8, width)[:, :, :2]
    behind, grad_mixed, up_sent, gate_sent, down_sent, far_out, near_out = hop(
        over_row, starts, grad_mixed, up_sent, gate_sent, down_sent, far_out, near_out
    )
    up_moved = over_row(up_sent)
    gate_moved = col_swap(gate_sent, 1)
    down_moved = col_swap(down_sent, 2)
    out_from_far = over_x(far_out)

    def mix_back(which):
        return sequence_call(
            mix_back_kernel,
            [grad_mixed[which], projected[which], flags[which]],
            [before[which], behind[which]],
            (taps, out_near, out_row, in_near, in_row),
            ((3 * width, jnp.bfloat16), (2 * half, jnp.bfloat16)),
            ((3, width),),
        )

    grad_projected = [None, None]
    grad_projected[1], far_one, far_taps = mix_back(1)
    far_one, grad_mixed = meet(far_one, grad_mixed)
    grad_projected[0], near_one, near_taps = mix_back(0)
    in_own, in_sent = weight_grads(grad_projected, normed_one, width)
    out_own, out_sent = weight_grads(mixed, grad_mixed, width)
    mixer_own = jnp.concatenate([in_own, out_own], axis=0)
    mixer_sent = jnp.concatenate([in_sent, out_sent], axis=0)
    out_from_far, up_moved, gate_moved, down_moved, far_one, near_one, mixer_sent = meet(
        out_from_far, up_moved, gate_moved, down_moved, far_one, near_one, mixer_sent
    )
    gate_sent, gate_kept = col_add(gate_kept, gate_moved)
    up_sent, up_kept = col_send(up_own + wide(up_moved), 1)
    down_own, down_sent = exchange(col_last(down_kept, down_moved))
    received, far_one, near_one, mixer_sent, up_sent, gate_sent, down_sent = hop(
        over_core,
        jnp.stack([near_one[size:], far_one[size:]]),
        far_one,
        near_one,
        mixer_sent,
        up_sent,
        gate_sent,
        down_sent,
    )
    mixer_moved = over_row(mixer_sent)
    up_moved = col_swap(up_sent, 1)
    gate_moved = col_swap(gate_sent, 2)
    far_one = narrow(wide(far_one[:size]) + wide(received[1]))
    one_from_far = over_x(far_one)
    near_one = wide(near_one[:size]) + wide(received[0])
    result = narrow(hidden_near + (near_out + wide(out_from_far)))
    conv_local = jnp.sum(near_taps + far_taps, axis=0)
    one_from_far, mixer_moved, up_moved, gate_moved, near_one, result, down_sent = meet(
        one_from_far, mixer_moved, up_moved, gate_moved, near_one, result, down_sent
    )
    mixer_sent, mixer_kept = col_send(mixer_own + wide(mixer_moved), 4)
    up_sent, up_kept = col_add(up_kept, up_moved)
    gate_total = team_first(col_last(gate_kept, gate_moved))
    mixer_sent, up_sent, gate_total, one_from_far, near_one, down_sent = meet(
        mixer_sent, up_sent, gate_total, one_from_far, near_one, down_sent
    )
    mixer_moved = col_swap(mixer_sent, 1)
    up_moved = col_swap(up_sent, 2)
    gate_far = over_x(gate_total)
    down_from_row = over_row(down_sent)
    grad_normed_one = near_one + wide(one_from_far)
    own_inputs = wide(near_tokens[0])
    own_scale = norm_scale(own_inputs)
    input_grad = grad_hidden[0] + norm_backward(grad_normed_one, own_inputs, own_scale, gain_one)
    gain_one_grad = jnp.sum(grad_normed_one * own_inputs * own_scale, axis=0)
    mixer_moved, up_moved, gate_far, down_from_row, input_grad, gain_one_grad = meet(
        mixer_moved, up_moved, gate_far, down_from_row, input_grad, gain_one_grad
    )
    mixer_sent, mixer_kept = col_add(mixer_kept, mixer_moved)
    mixer_sent, up_moved, down_from_row, gate_far, input_grad, result, gain_one_grad = meet(
        mixer_sent, up_moved, down_from_row, gate_far, input_grad, result, gain_one_grad
    )
    mixer_moved = col_swap(mixer_sent, 2)
    up_total = team_first(col_last(up_kept, up_moved))
    down_total = team_first(down_own + wide(down_from_row))
    both = jnp.stack([up_total, down_total])
    both_far = over_x(both)
    input_row = over_row(narrow(input_grad[:, half:]))
    gate_pair = over_core(jnp.stack([gate_total, gate_far]))
    mixer_moved, both_far, gate_pair, result, input_row = meet(mixer_moved, both_far, gate_pair, result, input_row)
    mixer_total = team_first(col_last(mixer_kept, mixer_moved))
    mixer_total, both_far, gate_pair, result, gain_one_grad = meet(
        mixer_total, both_far, gate_pair, result, gain_one_grad
    )
    mixer_far = over_x(mixer_total)
    result_row = over_row(result[:, half:])
    both_pair = over_core(jnp.stack([both, both_far]))
    gate_grad = wide(team_rows(gate_total, gate_far, gate_pair, 1)[0].T)
    mixer_far, both_pair = meet(mixer_far, both_pair)
    up_grad = wide(team_rows(up_total, both_far[0], both_pair[:, 0], 1)[0].T)
    down_grad = wide(team_rows(down_total, both_far[1], both_pair[:, 1], 1)[0])
    mixer_pair = over_core(jnp.stack([mixer_total, mixer_far]))
    mixer_grads = team_rows(mixer_total, mixer_far, mixer_pair, 4)
    in_grad = wide(mixer_grads[:3].transpose(2, 0, 1))
    out_grad = wide(mixer_grads[3])

    gain_local = jnp.stack([gain_one_grad, gain_two_grad])
    conv_flat = conv_local.reshape(3, cols, channels).transpose(1, 0, 2).reshape(cols, 3 * channels)
    apart = jnp.arange(cols) ^ col
    conv_flat = jnp.take(conv_flat, apart // 2 + apart % 2 * 2, axis=0).reshape(-1)
    sent = jnp.concatenate([gain_local[:, half:].reshape(-1), conv_flat])
    small = jnp.concatenate([gain_local[:, :half].reshape(-1), conv_flat]) + over_row(sent)
    for distance in (1, 2):
        small = small + col_swap(small, distance)
    conv_own = lax.dynamic_slice_in_dim(small[2 * half :], col * 3 * channels, 3 * channels, 0)
    conv_wide = lax.dynamic_update_slice(
        jnp.zeros((TEAM * 3 * channels,), jnp.float32), conv_own, (place * 3 * channels,)
    )
    small = jnp.concatenate([small[: 2 * half], conv_wide])
    small = small + over_x(small)
    small = small + over_core(small)
    small = other_teams(small)
    conv_grad = small[2 * half :].reshape(TEAM, 3, channels).transpose(1, 0, 2).reshape(3, TEAM * channels)

    return (
        to_blocks(result[:, :half], result_row),
        to_blocks(input_grad[:, :half], input_row),
        small[:half],
        in_grad,
        conv_grad,
        out_grad,
        small[half : 2 * half],
        gate_grad,
        up_grad,
        down_grad,
    )


def solution(mesh):
    return jax.shard_map(
        body,
        mesh=mesh,
        in_specs=(
            P(("dp", "col"), "row"),
            P(("dp", "row")),
            P(("dp", "col"), "row"),
            P("row"),
            P("row", None, "col"),
            P(None, "col"),
            P("col", "row"),
            P("row"),
            P("row", "col"),
            P("row", "col"),
            P("col", "row"),
        ),
        out_specs=(
            P(("dp", "col"), "row"),
            P(("dp", "col"), "row"),
            P("row"),
            P("row", None, "col"),
            P(None, "col"),
            P("col", "row"),
            P("row"),
            P("row", "col"),
            P("row", "col"),
            P("col", "row"),
        ),
        check_vma=False,
    )
```

time: 534 us -> 501 us (0.938)
  waiting for transfers between devices: 220 us -> 166 us
  Pallas kernels: 74.4 us -> 110 us
  other arithmetic: 94.1 us -> 80.7 us
  matrix products: 15.3 us -> 3.34 us
  starting transfers between devices: 51.4 us -> 61.6 us
    ppermute x18, waiting for transfers between devices: 119 us -> 87 us  [col_swap(): return lax.ppermute(values, 'col', [(i, i ^ distance) for i in range(size)])]
    pallas_call x0 -> x4, Pallas kernels: none -> 20.5 us  [sequence_call(): pl.pallas_call(kernel, grid=(2,), in_specs=[by_rows(one) for one in tiled...]
    ppermute x17, waiting for transfers between devices: 38.2 us -> 18.8 us  [over_row(): return lax.ppermute(values, 'row', [(0, 1), (1, 0)])]
    ppermute x18, starting transfers between devices: 14.2 us -> 27 us  [col_swap(): return lax.ppermute(values, 'col', [(i, i ^ distance) for i in range(size)])]
    convert_element_type x10, other arithmetic: 22.4 us -> 12.1 us  [narrow(): return values.astype(jnp.bfloat16)]
    dot_general x8 -> x0, matrix products: 10.2 us -> none  [the longest x4 5.17 us: dot_tn(): lax.dot_general(left, right, (((0,), (0,)), ((), ())), preferred_element_...]
    pallas_call x6 -> x8, Pallas kernels: 52 us -> 59.9 us  [token_call(): pl.pallas_call(kernel, grid=(tokens // ROWS,), in_specs=[row_tiles(one) f...]
    unnamed x221 -> x202, local copies, waits for them, and re-layouts: 32.4 us -> 24.9 us
  transfers between devices with their start and end apart: 69 -> 63, of which waited for: 37 -> 32; matrix products, arithmetic and copies ran while one was open for 21% -> 20% of each run, Pallas kernels for 9% -> 18%
where the time goes in v3:
time: 501 us; the launch traced here: 494 us
  waiting for transfers between devices  166 us (33%)
  Pallas kernels  110 us (22%)
  other arithmetic  80.7 us (16%)
  local copies, waits for them, and re-layouts  69.6 us (14%)
  starting transfers between devices  61.6 us (12%)
    ppermute x18, waiting for transfers between devices, col_swap(): return lax.ppermute(values, 'col', [(i, i ^ distance) for i in range(size)])  87 us
    ppermute x28, waiting for transfers between devices, over_dp(): return lax.ppermute(values, 'dp', [(i, i ^ distance) for i in range(size)])  60.3 us
    pallas_call x8, Pallas kernels, token_call(): pl.pallas_call(kernel, grid=(tokens // ROWS,), in_specs=[row_tiles(one) f...  59.9 us
    pallas_call x5, Pallas kernels, weight_grads(): pl.pallas_call(weight_kernel, grid=(columns // tile,), in_specs=[left_spe...  29.8 us
    ppermute x18, starting transfers between devices, col_swap(): return lax.ppermute(values, 'col', [(i, i ^ distance) for i in range(size)])  27 us
    unnamed x202, local copies, waits for them, and re-layouts  24.9 us
    pallas_call x4, Pallas kernels, sequence_call(): pl.pallas_call(kernel, grid=(2,), in_specs=[by_rows(one) for one in tiled...  20.5 us
    ppermute x17, waiting for transfers between devices, over_row(): return lax.ppermute(values, 'row', [(0, 1), (1, 0)])  18.8 us
  transfers between devices with their start and end apart: 63, of which 32 were waited for; matrix products, arithmetic and copies ran while one was open for 20% of the time, Pallas kernels for 18%

profile of v3, /device:TPU:0, one launch (start us, length us, event | category | flops | bytes accessed | tf_op | source)
XLA Modules:
  0.0 494.2 jit_solution(11753065116893190891)
XLA Ops:
  33.9 11.4 %collective-permute-done.8 = bf16[288,512]{1,0:T(8,128)(2,1)S(1)} collective-permute-done((bf16[288,512]{1,0:T(8,128)(2,1)S(1)}, bf16[288,512]{1,0:T(8,128)(2,1)S(1)}, u32[]{:S(2)}, u32[]{:S(2)}) %collective-permute-start.8) | collective-permute-done | bytes 294944 | tf_op jit(solution)/shard_map/ppermute | solution.py:43
  69.2 10.9 %collective-permute-done.14 = bf16[288,512]{1,0:T(8,128)(2,1)} collective-permute-done((bf16[288,512]{1,0:T(8,128)(2,1)}, bf16[288,512]{1,0:T(8,128)(2,1)}, u32[]{:S(2)}, u32[]{:S(2)}) %collective-permute-start.14) | collective-permute-done | bytes 294944 | tf_op jit(solution)/shard_map/ppermute | solution.py:43
  83.7 9.2 %collective-permute-done.19 = bf16[512,1024]{1,0:T(8,128)(2,1)S(1)} collective-permute-done((bf16[512,1024]{1,0:T(8,128)(2,1)}, bf16[512,1024]{1,0:T(8,128)(2,1)S(1)}, u32[]{:S(2)}, u32[]{:S(2)}) %collective-permute-start.19) | collective-permute-done | bytes 1048608 | tf_op jit(solution)/shard_map/ppermute | solution.py:26
  107.6 4.4 shard_map.188
  138.5 14.5 %collective-permute-done.23 = bf16[2,288,512]{2,1,0:T(8,128)(2,1)S(1)} collective-permute-done((bf16[2,288,512]{2,1,0:T(8,128)(2,1)S(1)}, bf16[2,288,512]{2,1,0:T(8,128)(2,1)S(1)}, u32[]{:S(2)}, u32[]{:S(2)}) %collective-permute-start.23) | collective-permute-done | bytes 589856 | tf_op jit(solution)/shard_map/ppermute | solution.py:43
  153.0 9.6 %collective-permute-done.22 = bf16[512,1024]{1,0:T(8,128)(2,1)S(1)} collective-permute-done((bf16[512,1024]{1,0:T(8,128)(2,1)S(1)}, bf16[512,1024]{1,0:T(8,128)(2,1)S(1)}, u32[]{:S(2)}, u32[]{:S(2)}) %collective-permute-start.22) | collective-permute-done | bytes 1048608 | tf_op jit(solution)/shard_map/ppermute | solution.py:26
  167.1 22.5 %collective-permute-done.26 = bf16[512,1024]{1,0:T(8,128)(2,1)S(1)} collective-permute-done((bf16[512,1024]{1,0:T(8,128)(2,1)S(1)}, bf16[512,1024]{1,0:T(8,128)(2,1)S(1)}, u32[]{:S(2)}, u32[]{:S(2)}) %collective-permute-start.26) | collective-permute-done | bytes 1048608 | tf_op jit(solution)/shard_map/ppermute | solution.py:26
  198.9 8.4 %shard_map.190 = (bf16[1024,1152]{1,0:T(8,128)(2,1)}, bf16[1024,1152]{1,0:T(8,128)(2,1)}, bf16[1024,1152]{1,0:T(8,128)(2,1)}) custom-call(bf16[1024,1024]{1,0:T(8,128)(2,1)} %pad_maximum_fusion.9.normed.right_near, bf16[1152,512]{1,0:T(8,128)(2,1)S(1)} %bitcast.214, bf16[1152,512]{1,0:T(8,128)(2,1)S(1)} %collective-permute-done.18.gate_row, ...), custom_call_target="tpu_custom_call" | custom-call | flops 1 | bytes 1 | tf_op jit(solution)/shard_map/pallas_call | solution.py:154
  207.2 12.7 %shard_map.191 = (bf16[1024,1152]{1,0:T(8,128)(2,1)}, bf16[1024,1152]{1,0:T(8,128)(2,1)}, bf16[1024,1024]{1,0:T(8,128)(2,1)}) custom-call(bf16[1024,1152]{1,0:T(8,128)(2,1)} %get-tuple-element.299.gate, bf16[1024,1152]{1,0:T(8,128)(2,1)} %get-tuple-element.300.up, bf16[1024,1024]{1,0:T(8,128)(2,1)} %pad_maximum_fusion.6.cotangent.right_near, ...), custom_call_target="tpu_custom_call" | custom-call | flops 1 | bytes 1 | tf_op jit(solution)/shard_map/pallas_call | solution.py:154
  226.9 8.5 %shard_map.192 = (bf16[1024,1152]{1,0:T(8,128)(2,1)}, bf16[1024,1152]{1,0:T(8,128)(2,1)}, bf16[1024,1152]{1,0:T(8,128)(2,1)}) custom-call(bf16[1024,1024]{1,0:T(8,128)(2,1)} %pad_maximum_fusion.10.normed.right_far, bf16[1152,512]{1,0:T(8,128)(2,1)S(1)} %bitcast.216, bf16[1152,512]{1,0:T(8,128)(2,1)S(1)} %collective-permute-done.18.gate_row, ...), custom_call_target="tpu_custom_call" | custom-call | flops 1 | bytes 1 | tf_op jit(solution)/shard_map/pallas_call | solution.py:154
  235.4 12.7 %shard_map.193 = (bf16[1024,1152]{1,0:T(8,128)(2,1)}, bf16[1024,1152]{1,0:T(8,128)(2,1)}, bf16[1024,1024]{1,0:T(8,128)(2,1)}) custom-call(bf16[1024,1152]{1,0:T(8,128)(2,1)} %get-tuple-element.308.gate, bf16[1024,1152]{1,0:T(8,128)(2,1)} %get-tuple-element.309.up, bf16[1024,1024]{1,0:T(8,128)(2,1)} %pad_maximum_fusion.7.cotangent.right_far, ...), custom_call_target="tpu_custom_call" | custom-call | flops 1 | bytes 1 | tf_op jit(solution)/shard_map/pallas_call | solution.py:154
  259.5 7.3 %shard_map.194 = (f32[1152,512]{1,0:T(8,128)}, bf16[1152,512]{1,0:T(8,128)(2,1)S(1)}) custom-call(bf16[1024,1152]{1,0:T(8,128)(2,1)} %get-tuple-element.332.left_near, bf16[1024,1152]{1,0:T(8,128)(2,1)} %get-tuple-element.333.left_far, bf16[1024,1024]{1,0:T(8,128)(2,1)S(1)} %copy-done.2, bf16[1024,1024]{1,0:T(8,128)(2,1)S(1)} %copy-done.3), custom_call_target="tpu_custom_call" | custom-call | flops 1 | bytes 1 | tf_op jit(solution)/shard_map/pallas_call | solution.py:293
  268.4 7.3 %shard_map.195 = (f32[1152,512]{1,0:T(8,128)}, bf16[1152,512]{1,0:T(8,128)(2,1)S(1)}) custom-call(bf16[1024,1152]{1,0:T(8,128)(2,1)} %get-tuple-element.346.left_near.act, bf16[1024,1152]{1,0:T(8,128)(2,1)} %get-tuple-element.347.left_far.act, bf16[1024,1024]{1,0:T(8,128)(2,1)S(1)} %copy-done.4, bf16[1024,1024]{1,0:T(8,128)(2,1)S(1)} %copy-done.5), custom_call_target="tpu_custom_call" | custom-call | flops 1 | bytes 1 | tf_op jit(solution)/shard_map/pallas_call | solution.py:293
  281.1 4.7 shard_map.196
  285.8 4.7 shard_map.197
  290.5 7.3 %shard_map.198 = (f32[1152,512]{1,0:T(8,128)}, bf16[1152,512]{1,0:T(8,128)(2,1)S(1)}) custom-call(bf16[1024,1152]{1,0:T(8,128)(2,1)} %get-tuple-element.348.left_near, bf16[1024,1152]{1,0:T(8,128)(2,1)} %get-tuple-element.349.left_far, bf16[1024,1024]{1,0:T(8,128)(2,1)S(1)} %copy-done.2, bf16[1024,1024]{1,0:T(8,128)(2,1)S(1)} %copy-done.3), custom_call_target="tpu_custom_call" | custom-call | flops 1 | bytes 1 | tf_op jit(solution)/shard_map/pallas_call | solution.py:293
  306.1 4.3 fusion.70
  332.2 7.4 %shard_map.199 = (bf16[1024,768]{1,0:T(8,128)(2,1)S(1)}, bf16[1024,1024]{1,0:T(8,128)(2,1)}, f32[2,3,256]{2,1,0:T(4,128)S(1)}) custom-call(bf16[1024,1024]{1,0:T(8,128)(2,1)} %pad_maximum_fusion.14.grad_mixed.right_far, f32[1024,768]{1,0:T(8,128)} %get-tuple-element.269.projected, f32[1024,4]{1,0:T(8,128)S(1)} %bitcast.237, ...), custom_call_target="tpu_custom_call" | custom-call | flops 1 | bytes 1 | tf_op jit(solution)/shard_map/pallas_call | solution.py:270
  339.6 7.5 %shard_map.200 = (bf16[1024,768]{1,0:T(8,128)(2,1)S(1)}, bf16[1024,1024]{1,0:T(8,128)(2,1)}, f32[2,3,256]{2,1,0:T(4,128)S(1)}) custom-call(bf16[1024,1024]{1,0:T(8,128)(2,1)} %pad_maximum_fusion.13.grad_mixed.right_near, f32[1024,768]{1,0:T(8,128)} %get-tuple-element.276.projected, f32[1024,4]{1,0:T(8,128)S(1)} %bitcast.235, ...), custom_call_target="tpu_custom_call" | custom-call | flops 1 | bytes 1 | tf_op jit(solution)/shard_map/pallas_call | solution.py:270
  349.2 6.5 %shard_map.201 = (f32[768,512]{1,0:T(8,128)S(1)}, bf16[768,512]{1,0:T(8,128)(2,1)S(1)}) custom-call(bf16[1024,768]{1,0:T(8,128)(2,1)S(1)} %get-tuple-element.375.left_near, bf16[1024,768]{1,0:T(8,128)(2,1)S(1)} %get-tuple-element.376.left_far, bf16[1024,1024]{1,0:T(8,128)(2,1)} %copy-done.14, bf16[1024,1024]{1,0:T(8,128)(2,1)} %copy-done.15), custom_call_target="tpu_custom_call" | custom-call | flops 1 | bytes 1 | tf_op jit(solution)/shard_map/pallas_call | solution.py:293
  382.4 14.6 %collective-permute-done.45 = bf16[1,288,512]{2,1,0:T(8,128)(2,1)S(1)} collective-permute-done((bf16[1,288,512]{2,1,0:T(8,128)(2,1)}, bf16[1,288,512]{2,1,0:T(8,128)(2,1)S(1)}, u32[]{:S(2)}, u32[]{:S(2)}) %collective-permute-start.45) | collective-permute-done | bytes 294944 | tf_op jit(solution)/shard_map/ppermute | solution.py:43
  413.2 9.5 %collective-permute-done.47 = bf16[1,288,512]{2,1,0:T(8,128)(2,1)S(1)} collective-permute-done((bf16[1,288,512]{2,1,0:T(8,128)(2,1)S(1)}, bf16[1,288,512]{2,1,0:T(8,128)(2,1)S(1)}, u32[]{:S(2)}, u32[]{:S(2)}) %collective-permute-start.47) | collective-permute-done | bytes 294944 | tf_op jit(solution)/shard_map/ppermute | solution.py:43
  430.1 11.8 %collective-permute-done.50 = bf16[4,64,512]{2,1,0:T(8,128)(2,1)S(1)} collective-permute-done((bf16[4,64,512]{2,1,0:T(8,128)(2,1)S(1)}, bf16[4,64,512]{2,1,0:T(8,128)(2,1)S(1)}, u32[]{:S(2)}, u32[]{:S(2)}) %collective-permute-start.50) | collective-permute-done | bytes 262176 | tf_op jit(solution)/shard_map/ppermute | solution.py:43
  448.5 9.5 %collective-permute-done.55 = f32[1792]{0:T(1024)S(1)} collective-permute-done((f32[1792]{0:T(1024)S(1)}, f32[1792]{0:T(1024)S(1)}, u32[]{:S(2)}, u32[]{:S(2)}) %collective-permute-start.55) | collective-permute-done | bytes 7200 | tf_op jit(solution)/shard_map/ppermute | solution.py:38
  (526 shorter events, 264.3 us)
Async XLA Ops:
  55.7 26.3 %collective-permute-start.11 = (bf16[784,512]{1,0:T(8,128)(2,1)}, bf16[784,512]{1,0:T(8,128)(2,1)}, u32[]{:S(2)}, u32[]{:S(2)}) collective-permute-start(bf16[784,512]{1,0:T(8,128)(2,1)} %pad_maximum_fusion.23), channel_id=1, source_target_pairs={{0,4},{4,0},{1,5},{5,1},{2,6},{6,2},{3,7},{7,3},{8,12},{12,8},{9,1... | collective-permute-start | bytes 2408456 | tf_op jit(solution)/shard_map/ppermute | solution.py:38
  56.8 25.2 %collective-permute-start.12 = (bf16[256,512]{1,0:T(8,128)(2,1)S(1)}, bf16[256,512]{1,0:T(8,128)(2,1)S(1)}, u32[]{:S(2)}, u32[]{:S(2)}) collective-permute-start(bf16[256,512]{1,0:T(8,128)(2,1)S(1)} %bitcast.228), channel_id=1, source_target_pairs={{0,4},{4,0},{1,5},{5,1},{2,6},{6,2},{3,7},{7,3},{8,12},{12,8},{9,1... | collective-permute-start | bytes 786440 | tf_op jit(solution)/shard_map/ppermute | solution.py:38
  57.8 24.3 %collective-permute-start.13 = (bf16[2,288,512]{2,1,0:T(8,128)(2,1)}, bf16[2,288,512]{2,1,0:T(8,128)(2,1)S(1)}, u32[]{:S(2)}, u32[]{:S(2)}) collective-permute-start(bf16[2,288,512]{2,1,0:T(8,128)(2,1)} %pad_maximum_fusion.25), channel_id=1, source_target_pairs={{0,1},{1,0},{2,3},{3,2},{4,5},{5,4},{6,7},{7,6},{8,9},{9,8},{10,11... | collective-permute-start | bytes 1769480 | tf_op jit(solution)/shard_map/ppermute | solution.py:43
  68.6 24.3 %collective-permute-start.19 = (bf16[512,1024]{1,0:T(8,128)(2,1)}, bf16[512,1024]{1,0:T(8,128)(2,1)S(1)}, u32[]{:S(2)}, u32[]{:S(2)}) collective-permute-start(bf16[512,1024]{1,0:T(8,128)(2,1)} %pad_maximum_fusion.21), channel_id=1, source_target_pairs={{0,16},{8,24},{16,0},{24,8},{1,17},{9,25},{17,1},{25,9},{2,18},{10... | collective-permute-start | bytes 3145736 | tf_op jit(solution)/shard_map/ppermute | solution.py:26
  94.5 34.1 %collective-permute-start.20 = (bf16[2,512,1024]{2,1,0:T(8,128)(2,1)}, bf16[2,512,1024]{2,1,0:T(8,128)(2,1)}, u32[]{:S(2)}, u32[]{:S(2)}) collective-permute-start(bf16[2,512,1024]{2,1,0:T(8,128)(2,1)} %pad_maximum_fusion.4), channel_id=1, source_target_pairs={{0,8},{8,0},{16,24},{24,16},{1,9},{9,1},{17,25},{25,17},{2,10},{10... | collective-permute-start | bytes 6291464 | tf_op jit(solution)/shard_map/ppermute | solution.py:26
  101.4 27.2 %collective-permute-start.18 = (bf16[1152,512]{1,0:T(8,128)(2,1)S(1)}, bf16[1152,512]{1,0:T(8,128)(2,1)S(1)}, u32[]{:S(2)}, u32[]{:S(2)}) collective-permute-start(bf16[1152,512]{1,0:T(8,128)(2,1)S(1)} %bitcast.213), channel_id=1, source_target_pairs={{0,4},{4,0},{1,5},{5,1},{2,6},{6,2},{3,7},{7,3},{8,12},{12,8},{9,1... | collective-permute-start | bytes 3538952 | tf_op jit(solution)/shard_map/ppermute | solution.py:38
  102.9 22.5 %collective-permute-start.16 = (bf16[2,288,512]{2,1,0:T(8,128)(2,1)}, bf16[2,288,512]{2,1,0:T(8,128)(2,1)}, u32[]{:S(2)}, u32[]{:S(2)}) collective-permute-start(bf16[2,288,512]{2,1,0:T(8,128)(2,1)} %pad_maximum_fusion.26), channel_id=1, source_target_pairs={{0,1},{1,0},{2,3},{3,2},{4,5},{5,4},{6,7},{7,6},{8,9},{9,8},{10,11... | collective-permute-start | bytes 1769480 | tf_op jit(solution)/shard_map/ppermute | solution.py:43
  135.3 28.4 %collective-permute-start.24 = (bf16[1152,512]{1,0:T(8,128)(2,1)S(1)}, bf16[1152,512]{1,0:T(8,128)(2,1)S(1)}, u32[]{:S(2)}, u32[]{:S(2)}) collective-permute-start(bf16[1152,512]{1,0:T(8,128)(2,1)S(1)} %bitcast.223), channel_id=1, source_target_pairs={{0,4},{4,0},{1,5},{5,1},{2,6},{6,2},{3,7},{7,3},{8,12},{12,8},{9,1... | collective-permute-start | bytes 3538952 | tf_op jit(solution)/shard_map/ppermute | solution.py:38
  137.2 25.3 %collective-permute-start.22 = (bf16[512,1024]{1,0:T(8,128)(2,1)S(1)}, bf16[512,1024]{1,0:T(8,128)(2,1)S(1)}, u32[]{:S(2)}, u32[]{:S(2)}) collective-permute-start(bf16[512,1024]{1,0:T(8,128)(2,1)S(1)} %fusion.12), channel_id=1, source_target_pairs={{0,16},{8,24},{16,0},{24,8},{1,17},{9,25},{17,1},{25,9},{2,18},{10... | collective-permute-start | bytes 3145736 | tf_op jit(solution)/shard_map/ppermute | solution.py:26
  164.7 24.8 %collective-permute-start.26 = (bf16[512,1024]{1,0:T(8,128)(2,1)S(1)}, bf16[512,1024]{1,0:T(8,128)(2,1)S(1)}, u32[]{:S(2)}, u32[]{:S(2)}) collective-permute-start(bf16[512,1024]{1,0:T(8,128)(2,1)S(1)} %get-tuple-element.501), channel_id=1, source_target_pairs={{0,16},{8,24},{16,0},{24,8},{1,17},{9,25},{17,1},{25,9},{2,18},{10... | collective-permute-start | bytes 3145736 | tf_op jit(solution)/shard_map/ppermute | solution.py:26
  165.3 27.3 %collective-permute-start.25 = (bf16[1152,512]{1,0:T(8,128)(2,1)S(1)}, bf16[1152,512]{1,0:T(8,128)(2,1)S(1)}, u32[]{:S(2)}, u32[]{:S(2)}) collective-permute-start(bf16[1152,512]{1,0:T(8,128)(2,1)S(1)} %bitcast.218), channel_id=1, source_target_pairs={{0,4},{4,0},{1,5},{5,1},{2,6},{6,2},{3,7},{7,3},{8,12},{12,8},{9,1... | collective-permute-start | bytes 3538952 | tf_op jit(solution)/shard_map/ppermute | solution.py:38
  225.3 25.3 %collective-permute-start.29 = (bf16[512,1024]{1,0:T(8,128)(2,1)S(1)}, bf16[512,1024]{1,0:T(8,128)(2,1)S(1)}, u32[]{:S(2)}, u32[]{:S(2)}) collective-permute-start(bf16[512,1024]{1,0:T(8,128)(2,1)S(1)} %fusion.10), channel_id=1, source_target_pairs={{0,16},{8,24},{16,0},{24,8},{1,17},{9,25},{17,1},{25,9},{2,18},{10... | collective-permute-start | bytes 3145736 | tf_op jit(solution)/shard_map/ppermute | solution.py:26
  258.0 39.9 %collective-permute-start.33 = (bf16[512,1024]{1,0:T(8,128)(2,1)}, bf16[512,1024]{1,0:T(8,128)(2,1)}, u32[]{:S(2)}, u32[]{:S(2)}) collective-permute-start(bf16[512,1024]{1,0:T(8,128)(2,1)} %fusion.11), channel_id=1, source_target_pairs={{0,16},{8,24},{16,0},{24,8},{1,17},{9,25},{17,1},{25,9},{2,18},{10... | collective-permute-start | bytes 3145736 | tf_op jit(solution)/shard_map/ppermute | solution.py:26
  266.9 43.6 %collective-permute-start.31 = (bf16[1152,512]{1,0:T(8,128)(2,1)S(1)}, bf16[1152,512]{1,0:T(8,128)(2,1)}, u32[]{:S(2)}, u32[]{:S(2)}) collective-permute-start(bf16[1152,512]{1,0:T(8,128)(2,1)S(1)} %get-tuple-element.334), channel_id=1, source_target_pairs={{0,4},{4,0},{1,5},{5,1},{2,6},{6,2},{3,7},{7,3},{8,12},{12,8},{9,1... | collective-permute-start | bytes 3538952 | tf_op jit(solution)/shard_map/ppermute | solution.py:38
  280.4 30.1 %collective-permute-start.32 = (bf16[1,576,1024]{2,1,0:T(8,128)(2,1)}, bf16[1,576,1024]{2,1,0:T(8,128)(2,1)}, u32[]{:S(2)}, u32[]{:S(2)}) collective-permute-start(bf16[1,576,1024]{2,1,0:T(8,128)(2,1)} %fusion.14), channel_id=1, source_target_pairs={{0,1},{1,0},{2,3},{3,2},{4,5},{5,4},{6,7},{7,6},{8,9},{9,8},{10,11... | collective-permute-start | bytes 3538952 | tf_op jit(solution)/shard_map/ppermute | solution.py:43
  326.9 31.7 %collective-permute-start.38 = (bf16[1152,512]{1,0:T(8,128)(2,1)S(1)}, bf16[1152,512]{1,0:T(8,128)(2,1)S(1)}, u32[]{:S(2)}, u32[]{:S(2)}) collective-permute-start(bf16[1152,512]{1,0:T(8,128)(2,1)S(1)} %get-tuple-element.385), channel_id=1, source_target_pairs={{0,4},{4,0},{1,5},{5,1},{2,6},{6,2},{3,7},{7,3},{8,12},{12,8},{9,1... | collective-permute-start | bytes 3538952 | tf_op jit(solution)/shard_map/ppermute | solution.py:38
  328.0 30.7 %collective-permute-start.37 = (bf16[512,1024]{1,0:T(8,128)(2,1)}, bf16[512,1024]{1,0:T(8,128)(2,1)}, u32[]{:S(2)}, u32[]{:S(2)}) collective-permute-start(bf16[512,1024]{1,0:T(8,128)(2,1)} %get-tuple-element.384), channel_id=1, source_target_pairs={{0,16},{8,24},{16,0},{24,8},{1,17},{9,25},{17,1},{25,9},{2,18},{10... | collective-permute-start | bytes 3145736 | tf_op jit(solution)/shard_map/ppermute | solution.py:26
  328.8 28.0 %collective-permute-start.39 = (bf16[1,576,512]{2,1,0:T(8,128)(2,1)}, bf16[1,576,512]{2,1,0:T(8,128)(2,1)S(1)}, u32[]{:S(2)}, u32[]{:S(2)}) collective-permute-start(bf16[1,576,512]{2,1,0:T(8,128)(2,1)} %fusion.20), channel_id=1, source_target_pairs={{0,1},{1,0},{2,3},{3,2},{4,5},{5,4},{6,7},{7,6},{8,9},{9,8},{10,11... | collective-permute-start | bytes 1769480 | tf_op jit(solution)/shard_map/ppermute | solution.py:43
  330.1 28.5 %collective-permute-start.40 = (bf16[1,288,1024]{2,1,0:T(8,128)(2,1)}, bf16[1,288,1024]{2,1,0:T(8,128)(2,1)}, u32[]{:S(2)}, u32[]{:S(2)}) collective-permute-start(bf16[1,288,1024]{2,1,0:T(8,128)(2,1)} %slice.693), channel_id=1, source_target_pairs={{0,2},{1,3},{2,0},{3,1},{4,6},{5,7},{6,4},{7,5},{8,10},{9,11},{10,... | collective-permute-start | bytes 1769480 | tf_op jit(solution)/shard_map/ppermute | solution.py:43
  374.9 25.9 %collective-permute-start.42 = (bf16[512,1024]{1,0:T(8,128)(2,1)}, bf16[512,1024]{1,0:T(8,128)(2,1)}, u32[]{:S(2)}, u32[]{:S(2)}) collective-permute-start(bf16[512,1024]{1,0:T(8,128)(2,1)} %get-tuple-element.507), channel_id=1, source_target_pairs={{0,16},{8,24},{16,0},{24,8},{1,17},{9,25},{17,1},{25,9},{2,18},{10... | collective-permute-start | bytes 3145736 | tf_op jit(solution)/shard_map/ppermute | solution.py:26
  376.1 25.6 %collective-permute-start.43 = (bf16[1024,512]{1,0:T(8,128)(2,1)}, bf16[1024,512]{1,0:T(8,128)(2,1)}, u32[]{:S(2)}, u32[]{:S(2)}) collective-permute-start(bf16[1024,512]{1,0:T(8,128)(2,1)} %pad_maximum_fusion.22), channel_id=1, source_target_pairs={{0,4},{4,0},{1,5},{5,1},{2,6},{6,2},{3,7},{7,3},{8,12},{12,8},{9,1... | collective-permute-start | bytes 3145736 | tf_op jit(solution)/shard_map/ppermute | solution.py:38
  444.0 31.5 %collective-permute-start.54 = (bf16[512,512]{1,0:T(8,128)(2,1)}, bf16[512,512]{1,0:T(8,128)(2,1)}, u32[]{:S(2)}, u32[]{:S(2)}) collective-permute-start(bf16[512,512]{1,0:T(8,128)(2,1)} %get-tuple-element.526), channel_id=1, source_target_pairs={{0,4},{4,0},{1,5},{5,1},{2,6},{6,2},{3,7},{7,3},{8,12},{12,8},{9,1... | collective-permute-start | bytes 1572872 | tf_op jit(solution)/shard_map/ppermute | solution.py:38
  446.1 31.2 %collective-permute-start.60 = (bf16[256,512]{1,0:T(8,128)(2,1)}, bf16[256,512]{1,0:T(8,128)(2,1)}, u32[]{:S(2)}, u32[]{:S(2)}) collective-permute-start(bf16[256,512]{1,0:T(8,128)(2,1)} %bitcast.90), channel_id=1, source_target_pairs={{0,16},{8,24},{16,0},{24,8},{1,17},{9,25},{17,1},{25,9},{2,18},{10... | collective-permute-start | bytes 786440 | tf_op jit(solution)/shard_map/ppermute | solution.py:26
  448.4 28.9 %collective-permute-start.61 = (bf16[2,2,288,512]{3,2,1,0:T(8,128)(2,1)}, bf16[2,2,288,512]{3,2,1,0:T(8,128)(2,1)}, u32[]{:S(2)}, u32[]{:S(2)}) collective-permute-start(bf16[2,2,288,512]{3,2,1,0:T(8,128)(2,1)} %pad_maximum_fusion.19), channel_id=1, source_target_pairs={{0,8},{8,0},{16,24},{24,16},{1,9},{9,1},{17,25},{25,17},{2,10},{10... | collective-permute-start | bytes 3538952 | tf_op jit(solution)/shard_map/ppermute | solution.py:26
  (136 other events, 1223.4 us)

commit v4 on v3

--- a/solution.py
+++ b/solution.py
@@ -136,7 +136,6 @@
 
 
 ROWS = 256
-VMEM_BYTES = 48 * 2**20
 COST = pl.CostEstimate(flops=1, bytes_accessed=1, transcendentals=0)
 
 
@@ -157,7 +156,7 @@
         in_specs=[row_tiles(one) for one in tiled] + [whole(one) for one in resident],
         out_specs=[row_tiles(one) for one in shapes],
         out_shape=shapes,
-        compiler_params=pltpu.CompilerParams(vmem_limit_bytes=VMEM_BYTES),
+        compiler_params=pltpu.CompilerParams(vmem_limit_bytes=20 * 2**20),
         cost_estimate=COST,
     )(*tiled, *resident)
 
@@ -167,34 +166,52 @@
     return dot_nt(left[:, :half], near[...]) + dot_nt(left[:, half:], row[...])
 
 
-def forward_kernel(normed, gate_near, gate_row, up_near, up_row, gate, up, act):
+def gated_kernel(
+    normed, cotangent, gate_near, gate_row, up_near, up_row, down_near, down_row,
+    act, grad_gate, grad_up, back_own, back_sent, out_own, out_sent,
+):
     gate_value = split_nt(normed, gate_near, gate_row)
     up_value = split_nt(normed, up_near, up_row)
-    gate[...] = narrow(gate_value)
-    up[...] = narrow(up_value)
-    act[...] = narrow(gate_value * jax.nn.sigmoid(gate_value) * up_value)
-
-
-def backward_kernel(
-    gate, up, cotangent, down_near, down_row, gate_near, gate_row, up_near, up_row, grad_gate, grad_up, back
-):
-    half = gate_near.shape[1]
     grad_act = split_nt(cotangent, down_near, down_row)
-    gate_value, up_value = wide(gate[...]), wide(up[...])
     sigmoid_gate = jax.nn.sigmoid(gate_value)
-    gated = grad_act * sigmoid_gate
-    low_gate = narrow(gated * up_value * (1.0 + gate_value * (1.0 - sigmoid_gate)))
-    low_up = narrow(gated * gate_value)
+    silu = gate_value * sigmoid_gate
+    low_act = narrow(silu * up_value)
+    low_gate = narrow(grad_act * up_value * (sigmoid_gate * (1.0 + gate_value * (1.0 - sigmoid_gate))))
+    low_up = narrow(grad_act * silu)
+    act[...] = low_act
     grad_gate[...] = low_gate
     grad_up[...] = low_up
-    back[:, :half] = narrow(dot_nn(low_gate, gate_near[...]) + dot_nn(low_up, up_near[...]))
-    back[:, half:] = narrow(dot_nn(low_gate, gate_row[...]) + dot_nn(low_up, up_row[...]))
-
-
-def out_kernel(act, down_near, down_row, out):
-    half = down_near.shape[1]
-    out[:, :half] = narrow(dot_nn(act[...], down_near[...]))
-    out[:, half:] = narrow(dot_nn(act[...], down_row[...]))
+    back = jnp.concatenate(
+        [
+            narrow(dot_nn(low_gate, gate_near[...]) + dot_nn(low_up, up_near[...])),
+            narrow(dot_nn(low_gate, gate_row[...]) + dot_nn(low_up, up_row[...])),
+        ],
+        axis=1,
+    )
+    out = jnp.concatenate(
+        [narrow(dot_nn(low_act, down_near[...])), narrow(dot_nn(low_act, down_row[...]))], axis=1
+    )
+    own_or_sent(back, back_own, back_sent)
+    own_or_sent(out, out_own, out_sent)
+
+
+def gated_call(normed, cotangent, weights):
+    tokens, width = normed.shape
+    units = weights[0].shape[0]
+    steps = tokens // ROWS
+    wide_out = jax.ShapeDtypeStruct((tokens, units), jnp.bfloat16)
+    part_out = jax.ShapeDtypeStruct((tokens // 2, width), jnp.bfloat16)
+    own = pl.BlockSpec((ROWS, width), lambda i: (jnp.minimum(i, steps // 2 - 1), 0))
+    sent = pl.BlockSpec((ROWS, width), lambda i: (jnp.maximum(i - steps // 2, 0), 0))
+    return pl.pallas_call(
+        gated_kernel,
+        grid=(steps,),
+        in_specs=[row_tiles(normed), row_tiles(cotangent)] + [whole(one) for one in weights],
+        out_specs=[row_tiles(wide_out)] * 3 + [own, sent] * 2,
+        out_shape=[wide_out] * 3 + [part_out] * 4,
+        compiler_params=pltpu.CompilerParams(vmem_limit_bytes=36 * 2**20),
+        cost_estimate=COST,
+    )(normed, cotangent, *weights)
 
 
 def project_kernel(inputs, gain, in_near, in_row, normed, projected):
@@ -218,19 +235,30 @@
     return input_gate, output_gate, values_part, mix_input, prior_one, prior_two, convolved
 
 
-def mix_kernel(projected, flags, before, taps, out_near, out_row, mixed, partial):
-    half = out_near.shape[1]
+def own_or_sent(partial, own, sent):
+    first = pl.program_id(0) < pl.num_programs(0) // 2
+
+    @pl.when(first)
+    def _():
+        own[...] = partial
+
+    @pl.when(jnp.logical_not(first))
+    def _():
+        sent[...] = partial
+
+
+def mix_kernel(projected, flags, before, taps, out_near, out_row, mixed, own, sent):
     _, output_gate, _, _, _, _, convolved = mixer_values(projected, flags, before, taps)
     low = narrow(output_gate * convolved)
     mixed[...] = low
-    partial[:, :half] = narrow(dot_nn(low, out_near[...]))
-    partial[:, half:] = narrow(dot_nn(low, out_row[...]))
+    partial = narrow(jnp.concatenate([dot_nn(low, out_near[...]), dot_nn(low, out_row[...])], axis=1))
+    own_or_sent(partial, own, sent)
 
 
 def mix_back_kernel(
-    grad_mixed, projected, flags, before, behind, taps, out_near, out_row, in_near, in_row, grad_projected, partial, sums
+    grad_mixed, projected, flags, before, behind, taps, out_near, out_row, in_near, in_row,
+    grad_projected, sums, own, sent,
 ):
-    half = out_near.shape[1]
     width = taps.shape[1]
     input_gate, output_gate, values_part, mix_input, prior_one, prior_two, convolved = mixer_values(
         projected, flags, before, taps
@@ -252,8 +280,8 @@
     )
     low = narrow(jnp.concatenate([grad_mix * values_part, grad_y * convolved, grad_mix * input_gate], axis=1))
     grad_projected[...] = low
-    partial[:, :half] = narrow(dot_nn(low, in_near[...]))
-    partial[:, half:] = narrow(dot_nn(low, in_row[...]))
+    partial = narrow(jnp.concatenate([dot_nn(low, in_near[...]), dot_nn(low, in_row[...])], axis=1))
+    own_or_sent(partial, own, sent)
 
 
 def sequence_call(kernel, tiled, small, resident, outs, small_outs=()):
@@ -266,14 +294,15 @@
         return pl.BlockSpec((1, *array.shape[1:]), lambda i: (i, 0, 0))
 
     shapes = [jax.ShapeDtypeStruct((2 * size, columns), dtype) for columns, dtype in outs]
+    part = jax.ShapeDtypeStruct((size, 2 * resident[-1].shape[1]), jnp.bfloat16)
     small_shapes = [jax.ShapeDtypeStruct((2, *shape), jnp.float32) for shape in small_outs]
     return pl.pallas_call(
         kernel,
         grid=(2,),
         in_specs=[by_rows(one) for one in tiled] + [by_first(one) for one in small] + [whole(one) for one in resident],
-        out_specs=[by_rows(one) for one in shapes] + [by_first(one) for one in small_shapes],
-        out_shape=shapes + small_shapes,
-        compiler_params=pltpu.CompilerParams(vmem_limit_bytes=VMEM_BYTES),
+        out_specs=[by_rows(one) for one in shapes] + [by_first(one) for one in small_shapes] + [whole(part)] * 2,
+        out_shape=shapes + small_shapes + [part] * 2,
+        compiler_params=pltpu.CompilerParams(vmem_limit_bytes=32 * 2**20),
         cost_estimate=COST,
     )(*tiled, *small, *resident)
 
@@ -299,7 +328,7 @@
             jax.ShapeDtypeStruct((columns, half), jnp.float32),
             jax.ShapeDtypeStruct((columns, half), jnp.bfloat16),
         ],
-        compiler_params=pltpu.CompilerParams(vmem_limit_bytes=VMEM_BYTES),
+        compiler_params=pltpu.CompilerParams(vmem_limit_bytes=28 * 2**20),
         cost_estimate=COST,
     )(*lefts, *rights)
 
@@ -412,11 +441,13 @@
     ends = dot_nt(ends[:, :half], in_near) + dot_nt(ends[:, half:], in_row)
     ends = (ends[:, :width] * ends[:, 2 * width :]).reshape(2, 2, 8, width)[:, :, 6:]
     gate_near = stacked(gate_pair, gate_other, 1)
-    before, gate_near, up_pair, down_part, inputs = hop(over_row, ends, gate_near, up_pair, down_part, inputs)
+    before, gate_near, up_pair, down_part, inputs, grads_own_x = hop(
+        over_row, ends, gate_near, up_pair, down_part, inputs, grads_near
+    )
     gate_row = over_row(gate_near)
     up_other = col_swap(up_pair, 1)
     down_pair = col_first(down_part)
-    grads_pair = over_core(jnp.stack([grads_near, grads_far]))
+    grads_pair = over_core(jnp.stack([grads_own_x, grads_far]))
     normed_one, projected = zip(
         *[
             token_call(
@@ -435,45 +466,35 @@
             [projected[which], flags[which]],
             [before[which]],
             (taps, out_near, out_row),
-            ((width, jnp.bfloat16), (2 * half, jnp.bfloat16)),
+            ((width, jnp.bfloat16),),
         )
 
-    def core_sum(partial, *waiting):
-        received, *waiting = hop(over_core, narrow(partial[size:]), *waiting)
-        return (wide(partial[:size]) + wide(received), *waiting)
-
     mixed = [None, None]
-    mixed[1], far_partial = mix(1)
-    mixed[0], near_partial = mix(0)
-    up_other, down_pair, gate_row, grads_pair, far_partial, near_partial = meet(
-        up_other, down_pair, gate_row, grads_pair, far_partial, near_partial
+    mixed[1], far_own, far_sent = mix(1)
+    mixed[0], near_own, near_sent = mix(0)
+    up_other, down_pair, gate_row, grads_pair, far_own, far_sent, near_own, near_sent = meet(
+        up_other, down_pair, gate_row, grads_pair, far_own, far_sent, near_own, near_sent
     )
     up_near = stacked(up_pair, up_other, 1)
     near_grads, far_grads = (grads_near, grads_pair[0]), (grads_far, grads_pair[1])
     cotangents = [jnp.concatenate(both, axis=0) for both in (near_grads, far_grads)]
-    received, far_partial, near_partial, up_near, down_pair, cotangents = hop(
-        over_core,
-        jnp.stack([near_partial[size:], far_partial[size:]]),
-        far_partial,
-        near_partial,
-        up_near,
-        down_pair,
-        cotangents,
-    )
-    far_sum = wide(far_partial[:size]) + wide(received[1])
-    near_sum = wide(near_partial[:size]) + wide(received[0])
-    from_far, to_far = over_x(narrow(far_sum)), over_x(narrow(near_sum))
+    far_moved, near_moved, far_own, near_own, up_near, down_pair, cotangents = meet(
+        over_core(far_sent), over_core(near_sent), far_own, near_own, up_near, down_pair, cotangents
+    )
+    far_send = narrow(wide(far_own) + wide(far_moved))
+    near_send = narrow(wide(near_own) + wide(near_moved))
+    from_far, to_far = over_x(far_send), over_x(near_send)
     up_row = over_row(up_near)
     down_other = col_swap(down_pair, 1)
     from_far, down_other, up_row = meet(from_far, down_other, up_row)
     down_near = stacked(down_pair, down_other, 1)
     from_far, down_near = meet(from_far, down_near)
     down_row = over_row(down_near)
-    hidden_near = wide(near_tokens[0]) + (near_sum + wide(from_far))
+    hidden_near = wide(near_tokens[0]) + (wide(near_own) + wide(near_moved) + wide(from_far))
     scale_near = norm_scale(hidden_near)
     normed_own = narrow(hidden_near * scale_near * gain_two)
     to_far, normed_own = meet(to_far, normed_own)
-    hidden_far = wide(far_tokens[0]) + (far_sum + wide(to_far))
+    hidden_far = wide(far_tokens[0]) + (wide(far_own) + wide(far_moved) + wide(to_far))
     scale_far = norm_scale(hidden_far)
     normed_x = narrow(hidden_far * scale_far * gain_two)
     down_row, normed_own, normed_x = meet(down_row, normed_own, normed_x)
@@ -482,33 +503,27 @@
     normed_far = jnp.concatenate([normed_x, pair[1]], axis=0)
     hiddens, scale_two, normed_two = (hidden_near, hidden_far), (scale_near, scale_far), (normed_near, normed_far)
     units = gate_near.shape[0]
-    weights = (gate_near, gate_row, up_near, up_row)
-    wide_outs = ((units, jnp.bfloat16),) * 3
-
-    grad_gate, grad_up = [None, None], [None, None]
-
-    def hidden_back(which, gate_value, up_value):
-        grad_gate[which], grad_up[which], back = token_call(
-            backward_kernel,
-            [gate_value, up_value, cotangents[which]],
-            (down_near, down_row, *weights),
-            ((units, jnp.bfloat16), (units, jnp.bfloat16), (2 * half, jnp.bfloat16)),
-        )
-        return back
+    weights = (gate_near, gate_row, up_near, up_row, down_near, down_row)
 
     def exchange(partial):
         return partial[:, :half], narrow(partial[:, half:])
 
-    gate_value, up_value, act_near = token_call(forward_kernel, [normed_near], weights, wide_outs)
-    near_back, normed_far = core_sum(hidden_back(0, gate_value, up_value), normed_far)
-    near_send, normed_far = meet(narrow(near_back), normed_far)
+    act, grad_gate, grad_up = [None, None], [None, None], [None, None]
+    act[0], grad_gate[0], grad_up[0], near_own, near_sent, near_out_own, near_out_sent = gated_call(
+        normed_near, cotangents[0], weights
+    )
+    near_moved, near_own, normed_far = hop(over_core, near_sent, near_own, normed_far)
+    near_send, normed_far = meet(narrow(wide(near_own) + wide(near_moved)), normed_far)
     back_to_far = over_x(near_send)
-    gate_value, up_value, act_far = token_call(forward_kernel, [normed_far], weights, wide_outs)
-    far_partial = hidden_back(1, gate_value, up_value)
-    act, normed_two = [act_near, act_far], [normed_near, normed_far]
-    back_to_far, far_partial, grad_gate, grad_up, act = meet(back_to_far, far_partial, grad_gate, grad_up, act)
-    far_back, grad_gate, grad_up, act = core_sum(far_partial, grad_gate, grad_up, act)
-    far_send, grad_gate, grad_up, act = meet(narrow(far_back), grad_gate, grad_up, act)
+    act[1], grad_gate[1], grad_up[1], far_own, far_sent, far_out_own, far_out_sent = gated_call(
+        normed_far, cotangents[1], weights
+    )
+    normed_two = [normed_near, normed_far]
+    back_to_far, far_own, far_sent, grad_gate, grad_up, act = meet(
+        back_to_far, far_own, far_sent, grad_gate, grad_up, act
+    )
+    far_moved, far_own, grad_gate, grad_up, act = hop(over_core, far_sent, far_own, grad_gate, grad_up, act)
+    far_send, grad_gate, grad_up, act = meet(narrow(wide(far_own) + wide(far_moved)), grad_gate, grad_up, act)
     back_from_far = over_x(far_send)
     gate_own, gate_sent = weight_grads(grad_gate, normed_two, units // 3)
     gate_moved = over_row(gate_sent)
@@ -518,10 +533,12 @@
     down_moved = col_swap(down_sent, 1)
     down_sent, grad_up, act = meet(down_sent, grad_up, act)
     up_own, up_sent = weight_grads(grad_up, normed_two, units // 3)
-    outs = [token_call(out_kernel, [one], (down_near, down_row), ((2 * half, jnp.bfloat16),))[0] for one in act]
-    back_from_far, outs, up_sent = meet(back_from_far, outs, up_sent)
-
-    back_sums = (near_back + wide(back_from_far), far_back + wide(back_to_far))
+    back_from_far, up_sent = meet(back_from_far, up_sent)
+
+    back_sums = (
+        wide(near_own) + wide(near_moved) + wide(back_from_far),
+        wide(far_own) + wide(far_moved) + wide(back_to_far),
+    )
     grad_hidden, low = [], []
     for which, cotangent_rows in ((0, near_grads[0]), (1, far_grads[0])):
         grads = wide(cotangent_rows) + norm_backward(
@@ -533,20 +550,20 @@
     gate_moved, down_moved, low = meet(gate_moved, down_moved, low)
     gate_sent, gate_kept = col_send(gate_own + wide(gate_moved), 1)
     down_sent, down_kept = col_add(down_kept, down_moved)
-    low_moved, out_moved = over_core(jnp.stack(low)), over_core(jnp.stack([outs[0][size:], outs[1][size:]]))
-    low_moved, out_moved, low, outs, up_sent, gate_sent, down_sent = meet(
-        low_moved, out_moved, low, outs, up_sent, gate_sent, down_sent
+    low_moved = over_core(jnp.stack(low))
+    near_out_moved, far_out_moved = over_core(near_out_sent), over_core(far_out_sent)
+    low_moved, near_out_moved, far_out_moved, low, up_sent, gate_sent, down_sent = meet(
+        low_moved, near_out_moved, far_out_moved, low, up_sent, gate_sent, down_sent
     )
     grad_mixed = [jnp.concatenate([low[which], low_moved[which]], axis=0) for which in (0, 1)]
-    near_out, far_out = (wide(out[:size]) + wide(out_moved[which]) for which, out in enumerate(outs))
-    far_out = narrow(far_out)
+    far_out = narrow(wide(far_out_own) + wide(far_out_moved))
 
     starts = jnp.concatenate([one[at : at + 8] for one in grad_mixed for at in (0, size)], axis=0)
     starts = dot_nt(starts[:, :half], out_near) + dot_nt(starts[:, half:], out_row)
     opened = jnp.concatenate([one[at : at + 8, width : 2 * width] for one in projected for at in (0, size)], axis=0)
     starts = (starts * opened).reshape(2, 2, 8, width)[:, :, :2]
-    behind, grad_mixed, up_sent, gate_sent, down_sent, far_out, near_out = hop(
-        over_row, starts, grad_mixed, up_sent, gate_sent, down_sent, far_out, near_out
+    behind, grad_mixed, up_sent, gate_sent, down_sent, far_out = hop(
+        over_row, starts, grad_mixed, up_sent, gate_sent, down_sent, far_out
     )
     up_moved = over_row(up_sent)
     gate_moved = col_swap(gate_sent, 1)
@@ -559,44 +576,51 @@
             [grad_mixed[which], projected[which], flags[which]],
             [before[which], behind[which]],
             (taps, out_near, out_row, in_near, in_row),
-            ((3 * width, jnp.bfloat16), (2 * half, jnp.bfloat16)),
+            ((3 * width, jnp.bfloat16),),
             ((3, width),),
         )
 
     grad_projected = [None, None]
-    grad_projected[1], far_one, far_taps = mix_back(1)
+    grad_projected[1], far_taps, far_one, far_one_sent = mix_back(1)
     far_one, grad_mixed = meet(far_one, grad_mixed)
-    grad_projected[0], near_one, near_taps = mix_back(0)
+    grad_projected[0], near_taps, near_one, near_one_sent = mix_back(0)
     in_own, in_sent = weight_grads(grad_projected, normed_one, width)
     out_own, out_sent = weight_grads(mixed, grad_mixed, width)
     mixer_own = jnp.concatenate([in_own, out_own], axis=0)
     mixer_sent = jnp.concatenate([in_sent, out_sent], axis=0)
-    out_from_far, up_moved, gate_moved, down_moved, far_one, near_one, mixer_sent = meet(
-        out_from_far, up_moved, gate_moved, down_moved, far_one, near_one, mixer_sent
+    out_from_far, up_moved, gate_moved, down_moved, far_one, near_one, near_one_sent, mixer_sent = meet(
+        out_from_far, up_moved, gate_moved, down_moved, far_one, near_one, near_one_sent, mixer_sent
     )
     gate_sent, gate_kept = col_add(gate_kept, gate_moved)
     up_sent, up_kept = col_send(up_own + wide(up_moved), 1)
     down_own, down_sent = exchange(col_last(down_kept, down_moved))
-    received, far_one, near_one, mixer_sent, up_sent, gate_sent, down_sent = hop(
-        over_core,
-        jnp.stack([near_one[size:], far_one[size:]]),
-        far_one,
-        near_one,
-        mixer_sent,
-        up_sent,
-        gate_sent,
-        down_sent,
-    )
+    far_one_moved, near_one_moved, far_one, near_one, mixer_sent, up_sent, gate_sent, down_sent = meet(
+        over_core(far_one_sent), over_core(near_one_sent), far_one, near_one, mixer_sent, up_sent, gate_sent, down_sent
+    )
+    one_send = narrow(wide(far_one) + wide(far_one_moved))
+    one_send, mixer_sent, far_one, near_one = meet(one_send, mixer_sent, far_one, near_one)
     mixer_moved = over_row(mixer_sent)
     up_moved = col_swap(up_sent, 1)
     gate_moved = col_swap(gate_sent, 2)
-    far_one = narrow(wide(far_one[:size]) + wide(received[1]))
-    one_from_far = over_x(far_one)
-    near_one = wide(near_one[:size]) + wide(received[0])
-    result = narrow(hidden_near + (near_out + wide(out_from_far)))
+    one_from_far = over_x(one_send)
+    result = narrow(hidden_near + (wide(near_out_own) + wide(near_out_moved) + wide(out_from_far)))
+    gain_one_grad = 0.0
+    for rows, one in (
+        (near_tokens[0], near_one), (near_tokens[1], near_one_sent), (far_tokens[0], far_one), (far_tokens[1], far_one_sent)
+    ):
+        rows = wide(rows)
+        gain_one_grad = gain_one_grad + jnp.sum(wide(one) * (rows * norm_scale(rows)), axis=0)
     conv_local = jnp.sum(near_taps + far_taps, axis=0)
-    one_from_far, mixer_moved, up_moved, gate_moved, near_one, result, down_sent = meet(
-        one_from_far, mixer_moved, up_moved, gate_moved, near_one, result, down_sent
+    gain_local = jnp.stack([gain_one_grad, gain_two_grad])
+    conv_flat = conv_local.reshape(3, cols, channels).transpose(1, 0, 2).reshape(cols, 3 * channels)
+    apart = jnp.arange(cols) ^ col
+    conv_flat = jnp.take(conv_flat, apart // 2 + apart % 2 * 2, axis=0).reshape(-1)
+    small = jnp.concatenate([gain_local[:, :half].reshape(-1), conv_flat, gain_local[:, half:].reshape(-1)])
+    small, up_moved, gate_moved = meet(small, up_moved, gate_moved)
+    for distance in (1, 2):
+        small = small + col_swap(small, distance)
+    one_from_far, mixer_moved, up_moved, gate_moved, near_one, result, down_sent, small = meet(
+        one_from_far, mixer_moved, up_moved, gate_moved, near_one, result, down_sent, small
     )
     mixer_sent, mixer_kept = col_send(mixer_own + wide(mixer_moved), 4)
     up_sent, up_kept = col_add(up_kept, up_moved)
@@ -607,18 +631,27 @@
     mixer_moved = col_swap(mixer_sent, 1)
     up_moved = col_swap(up_sent, 2)
     gate_far = over_x(gate_total)
+    kept = 2 * half + 3 * width
+    sent = jnp.concatenate([small[kept:], small[2 * half : kept]])
+    small = small[:kept] + over_row(sent)
+    small, down_sent = meet(small, down_sent)
     down_from_row = over_row(down_sent)
-    grad_normed_one = near_one + wide(one_from_far)
+    conv_own = lax.dynamic_slice_in_dim(small[2 * half :], col * 3 * channels, 3 * channels, 0)
+    conv_wide = lax.dynamic_update_slice(
+        jnp.zeros((TEAM * 3 * channels,), jnp.float32), conv_own, (place * 3 * channels,)
+    )
+    small = jnp.concatenate([small[: 2 * half], conv_wide])
+    small = small + over_x(small)
+    grad_normed_one = wide(near_one) + wide(near_one_moved) + wide(one_from_far)
     own_inputs = wide(near_tokens[0])
     own_scale = norm_scale(own_inputs)
     input_grad = grad_hidden[0] + norm_backward(grad_normed_one, own_inputs, own_scale, gain_one)
-    gain_one_grad = jnp.sum(grad_normed_one * own_inputs * own_scale, axis=0)
-    mixer_moved, up_moved, gate_far, down_from_row, input_grad, gain_one_grad = meet(
-        mixer_moved, up_moved, gate_far, down_from_row, input_grad, gain_one_grad
+    mixer_moved, up_moved, gate_far, down_from_row, input_grad, small = meet(
+        mixer_moved, up_moved, gate_far, down_from_row, input_grad, small
     )
     mixer_sent, mixer_kept = col_add(mixer_kept, mixer_moved)
-    mixer_sent, up_moved, down_from_row, gate_far, input_grad, result, gain_one_grad = meet(
-        mixer_sent, up_moved, down_from_row, gate_far, input_grad, result, gain_one_grad
+    mixer_sent, up_moved, down_from_row, gate_far, input_grad, result, small = meet(
+        mixer_sent, up_moved, down_from_row, gate_far, input_grad, result, small
     )
     mixer_moved = col_swap(mixer_sent, 2)
     up_total = team_first(col_last(up_kept, up_moved))
@@ -626,12 +659,12 @@
     both = jnp.stack([up_total, down_total])
     both_far = over_x(both)
     input_row = over_row(narrow(input_grad[:, half:]))
+    small = other_teams(small + over_core(small))
+    conv_grad = small[2 * half :].reshape(TEAM, 3, channels).transpose(1, 0, 2).reshape(3, TEAM * channels)
     gate_pair = over_core(jnp.stack([gate_total, gate_far]))
     mixer_moved, both_far, gate_pair, result, input_row = meet(mixer_moved, both_far, gate_pair, result, input_row)
     mixer_total = team_first(col_last(mixer_kept, mixer_moved))
-    mixer_total, both_far, gate_pair, result, gain_one_grad = meet(
-        mixer_total, both_far, gate_pair, result, gain_one_grad
-    )
+    mixer_total, both_far, gate_pair, result = meet(mixer_total, both_far, gate_pair, result)
     mixer_far = over_x(mixer_total)
     result_row = over_row(result[:, half:])
     both_pair = over_core(jnp.stack([both, both_far]))
@@ -643,24 +676,6 @@
     mixer_grads = team_rows(mixer_total, mixer_far, mixer_pair, 4)
     in_grad = wide(mixer_grads[:3].transpose(2, 0, 1))
     out_grad = wide(mixer_grads[3])
-
-    gain_local = jnp.stack([gain_one_grad, gain_two_grad])
-    conv_flat = conv_local.reshape(3, cols, channels).transpose(1, 0, 2).reshape(cols, 3 * channels)
-    apart = jnp.arange(cols) ^ col
-    conv_flat = jnp.take(conv_flat, apart // 2 + apart % 2 * 2, axis=0).reshape(-1)
-    sent = jnp.concatenate([gain_local[:, half:].reshape(-1), conv_flat])
-    small = jnp.concatenate([gain_local[:, :half].reshape(-1), conv_flat]) + over_row(sent)
-    for distance in (1, 2):
-        small = small + col_swap(small, distance)
-    conv_own = lax.dynamic_slice_in_dim(small[2 * half :], col * 3 * channels, 3 * channels, 0)
-    conv_wide = lax.dynamic_update_slice(
-        jnp.zeros((TEAM * 3 * channels,), jnp.float32), conv_own, (place * 3 * channels,)
-    )
-    small = jnp.concatenate([small[: 2 * half], conv_wide])
-    small = small + over_x(small)
-    small = small + over_core(small)
-    small = other_teams(small)
-    conv_grad = small[2 * half :].reshape(TEAM, 3, channels).transpose(1, 0, 2).reshape(3, TEAM * channels)
 
     return (
         to_blocks(result[:, :half], result_row),

time: 501 us -> 472 us (0.942)
  Pallas kernels: 110 us -> 82.1 us
  waiting for transfers between devices: 166 us -> 155 us
  starting transfers between devices: 61.6 us -> 68.5 us
  local copies, waits for them, and re-layouts: 69.6 us -> 76.2 us
    pallas_call x8 -> x2, Pallas kernels: 59.9 us -> 5.97 us  [token_call(): pl.pallas_call(kernel, grid=(tokens // ROWS,), in_specs=[row_tiles(one) f...]
    pallas_call x0 -> x2, Pallas kernels: none -> 38.3 us  [gated_call(): pl.pallas_call(gated_kernel, grid=(steps,), in_specs=[row_tiles(normed),...]
    add x4 -> x3, other arithmetic: 8.26 us -> 0.02 us  [the longest x1 0.01 us: body(): gain_one_grad + jnp.sum(wide(one) * (rows * norm_scale(rows)), axis=0)]
    pallas_call x4, Pallas kernels: 20.5 us -> 13.5 us  [sequence_call(): pl.pallas_call(kernel, grid=(2,), in_specs=[by_rows(one) for one in tiled...]
    convert_element_type x10 -> x12, other arithmetic: 12.1 us -> 18.3 us  [narrow(): return values.astype(jnp.bfloat16)]
    ppermute x28 -> x31, waiting for transfers between devices: 60.3 us -> 54.4 us  [over_dp(): return lax.ppermute(values, 'dp', [(i, i ^ distance) for i in range(size)])]
    pallas_call x5, Pallas kernels: 29.8 us -> 24.3 us  [weight_grads(): pl.pallas_call(weight_kernel, grid=(columns // tile,), in_specs=[left_spe...]
    reduce_sum x1 -> x5, other arithmetic: 2.27 us -> 7.6 us  [the longest x4 5.64 us: body(): jnp.sum(wide(one) * (rows * norm_scale(rows)), axis=0)]
  transfers between devices with their start and end apart: 63 -> 66, of which waited for: 32 -> 34; matrix products, arithmetic and copies ran while one was open for 20% -> 23% of each run, Pallas kernels for 18% -> 14%
where the time goes in v4:
time: 472 us; the launch traced here: 466 us
  waiting for transfers between devices  155 us (33%)
  Pallas kernels  82.1 us (17%)
  other arithmetic  77.9 us (17%)
  local copies, waits for them, and re-layouts  76.2 us (16%)
  starting transfers between devices  68.5 us (15%)
    ppermute x18, waiting for transfers between devices, col_swap(): return lax.ppermute(values, 'col', [(i, i ^ distance) for i in range(size)])  81.7 us
    ppermute x31, waiting for transfers between devices, over_dp(): return lax.ppermute(values, 'dp', [(i, i ^ distance) for i in range(size)])  54.4 us
    pallas_call x2, Pallas kernels, gated_call(): pl.pallas_call(gated_kernel, grid=(steps,), in_specs=[row_tiles(normed),...  38.3 us
    ppermute x18, starting transfers between devices, col_swap(): return lax.ppermute(values, 'col', [(i, i ^ distance) for i in range(size)])  30 us
    unnamed x226, local copies, waits for them, and re-layouts  28.2 us
    pallas_call x5, Pallas kernels, weight_grads(): pl.pallas_call(weight_kernel, grid=(columns // tile,), in_specs=[left_spe...  24.3 us
    ppermute x17, starting transfers between devices, over_row(): return lax.ppermute(values, 'row', [(0, 1), (1, 0)])  21.2 us
    ppermute x17, waiting for transfers between devices, over_row(): return lax.ppermute(values, 'row', [(0, 1), (1, 0)])  18.8 us
  transfers between devices with their start and end apart: 66, of which 34 were waited for; matrix products, arithmetic and copies ran while one was open for 23% of the time, Pallas kernels for 14%

profile of v4, /device:TPU:0, one launch (start us, length us, event | category | flops | bytes accessed | tf_op | source)
XLA Modules:
  0.0 465.9 jit_solution(14588477384858784284)
XLA Ops:
  5.9 4.0 collective-permute-start
  33.9 11.4 %collective-permute-done.8 = bf16[288,512]{1,0:T(8,128)(2,1)S(1)} collective-permute-done((bf16[288,512]{1,0:T(8,128)(2,1)S(1)}, bf16[288,512]{1,0:T(8,128)(2,1)S(1)}, u32[]{:S(2)}, u32[]{:S(2)}) %collective-permute-start.8) | collective-permute-done | bytes 294944 | tf_op jit(solution)/shard_map/ppermute | solution.py:43
  69.4 10.7 %collective-permute-done.14 = bf16[288,512]{1,0:T(8,128)(2,1)} collective-permute-done((bf16[288,512]{1,0:T(8,128)(2,1)}, bf16[288,512]{1,0:T(8,128)(2,1)}, u32[]{:S(2)}, u32[]{:S(2)}) %collective-permute-start.14) | collective-permute-done | bytes 294944 | tf_op jit(solution)/shard_map/ppermute | solution.py:43
  116.7 5.1 %collective-permute-done.18.gate_row = bf16[1152,512]{1,0:T(8,128)(2,1)S(1)} collective-permute-done((bf16[1152,512]{1,0:T(8,128)(2,1)S(1)}, bf16[1152,512]{1,0:T(8,128)(2,1)S(1)}, u32[]{:S(2)}, u32[]{:S(2)}) %collective-permute-start.18) | collective-permute-done | bytes 1179680 | tf_op jit(solution)/shard_map/ppermute | solution.py:38
  129.2 14.1 %collective-permute-done.24 = bf16[2,288,512]{2,1,0:T(8,128)(2,1)S(1)} collective-permute-done((bf16[2,288,512]{2,1,0:T(8,128)(2,1)S(1)}, bf16[2,288,512]{2,1,0:T(8,128)(2,1)S(1)}, u32[]{:S(2)}, u32[]{:S(2)}) %collective-permute-start.24) | collective-permute-done | bytes 589856 | tf_op jit(solution)/shard_map/ppermute | solution.py:43
  143.3 9.6 %collective-permute-done.23 = bf16[512,1024]{1,0:T(8,128)(2,1)S(1)} collective-permute-done((bf16[512,1024]{1,0:T(8,128)(2,1)S(1)}, bf16[512,1024]{1,0:T(8,128)(2,1)S(1)}, u32[]{:S(2)}, u32[]{:S(2)}) %collective-permute-start.23) | collective-permute-done | bytes 1048608 | tf_op jit(solution)/shard_map/ppermute | solution.py:26
  157.4 22.1 %collective-permute-done.27 = bf16[512,1024]{1,0:T(8,128)(2,1)S(1)} collective-permute-done((bf16[512,1024]{1,0:T(8,128)(2,1)S(1)}, bf16[512,1024]{1,0:T(8,128)(2,1)S(1)}, u32[]{:S(2)}, u32[]{:S(2)}) %collective-permute-start.27) | collective-permute-done | bytes 1048608 | tf_op jit(solution)/shard_map/ppermute | solution.py:26
  182.8 4.1 collective-permute-done.28
  187.3 19.1 %shard_map.190 = (bf16[1024,1152]{1,0:T(8,128)(2,1)S(1)}, bf16[1024,1152]{1,0:T(8,128)(2,1)}, bf16[1024,1152]{1,0:T(8,128)(2,1)}, bf16[512,1024]{1,0:T(8,128)(2,...) custom-call(bf16[1024,1024]{1,0:T(8,128)(2,1)S(1)} %pad_maximum_fusion.8.normed., ...), custom_call_target="tpu_custom_call" | custom-call | flops 1 | bytes 1 | tf_op jit(solution)/shard_map/pallas_call | solution.py:206
  212.9 19.2 %shard_map.191 = (bf16[1024,1152]{1,0:T(8,128)(2,1)S(1)}, bf16[1024,1152]{1,0:T(8,128)(2,1)}, bf16[1024,1152]{1,0:T(8,128)(2,1)}, bf16[512,1024]{1,0:T(8,128)(2,...) custom-call(bf16[1024,1024]{1,0:T(8,128)(2,1)S(1)} %pad_maximum_fusion.9.normed., ...), custom_call_target="tpu_custom_call" | custom-call | flops 1 | bytes 1 | tf_op jit(solution)/shard_map/pallas_call | solution.py:206
  233.1 3.8 collective-permute-done.30
  243.3 6.0 %shard_map.192 = (f32[1152,512]{1,0:T(8,128)S(1)}, bf16[1152,512]{1,0:T(8,128)(2,1)S(1)}) custom-call(bf16[1024,1152]{1,0:T(8,128)(2,1)S(1)} %copy-done.21, bf16[1024,1152]{1,0:T(8,128)(2,1)S(1)} %copy-done.24, bf16[1024,1024]{1,0:T(8,128)(2,1)S(1)} %pad_maximum_fusion.8.normed.right_near, bf16[1024,1024]{1,0:T(8,128)(2,1)S(1)} %pad_maximum_fusion.9.normed.right_far), custom_call_target="tpu_custom_call" | custom-call | flops 1 | bytes 1 | tf_op jit(solution)/shard_map/pallas_call | solution.py:322
  250.9 6.0 %shard_map.193 = (f32[1152,512]{1,0:T(8,128)S(1)}, bf16[1152,512]{1,0:T(8,128)(2,1)S(1)}) custom-call(bf16[1024,1152]{1,0:T(8,128)(2,1)S(1)} %copy-done.19, bf16[1024,1152]{1,0:T(8,128)(2,1)S(1)} %copy-done.23, bf16[1024,1024]{1,0:T(8,128)(2,1)S(1)} %pad_maximum_fusion.5.cotangent.right_near, bf16[1024,1024]{1,0:T(8,128)(2,1)S(1)} %pad_maximum_fusion.6.cotangent.right_far), custom_call_target="tpu_custom_call" | custom-call | flops 1 | bytes 1 | tf_op jit(solution)/shard_map/pallas_call | solution.py:322
  263.6 6.8 %shard_map.194 = (f32[1152,512]{1,0:T(8,128)S(1)}, bf16[1152,512]{1,0:T(8,128)(2,1)}) custom-call(bf16[1024,1152]{1,0:T(8,128)(2,1)S(1)} %copy-done.17, bf16[1024,1152]{1,0:T(8,128)(2,1)S(1)} %copy-done.20, bf16[1024,1024]{1,0:T(8,128)(2,1)S(1)} %pad_maximum_fusion.8.normed.right_near, bf16[1024,1024]{1,0:T(8,128)(2,1)S(1)} %pad_maximum_fusion.9.normed.right_far), custom_call_target="tpu_custom_call" | custom-call | flops 1 | bytes 1 | tf_op jit(solution)/shard_map/pallas_call | solution.py:322
  275.9 4.4 fusion.76
  280.3 10.4 %collective-permute-done.33 = bf16[1,576,1024]{2,1,0:T(8,128)(2,1)} collective-permute-done((bf16[1,576,1024]{2,1,0:T(8,128)(2,1)}, bf16[1,576,1024]{2,1,0:T(8,128)(2,1)}, u32[]{:S(2)}, u32[]{:S(2)}) %collective-permute-start.33) | collective-permute-done | bytes 1179680 | tf_op jit(solution)/shard_map/ppermute | solution.py:43
  308.7 5.8 %shard_map.195 = (bf16[1024,768]{1,0:T(8,128)(2,1)S(1)}, f32[2,3,256]{2,1,0:T(4,128)S(1)}, bf16[512,1024]{1,0:T(8,128)(2,1)S(1)}, bf16[512,1024]{1,0:T(8,128)(2,1)}) custom-call(bf16[1024,1024]{1,0:T(8,128)(2,1)S(1)} %pad_maximum_fusion.12.grad_mixed.right_far, f32[1024,768]{1,0:T(8,128)S(1)} %copy-done.5, f32[1024,4]{1,0:T(8,128)S(1)} %bitcast.205, ...), custom_call_target="tpu_custom_call" | custom-call | flops 1 | bytes 1 | tf_op jit(solution)/shard_map/pallas_call | solution.py:299
  314.6 4.8 %shard_map.196 = (bf16[1024,768]{1,0:T(8,128)(2,1)S(1)}, f32[2,3,256]{2,1,0:T(4,128)S(1)}, bf16[512,1024]{1,0:T(8,128)(2,1)S(1)}, bf16[512,1024]{1,0:T(8,128)(2,1)S(1)}) custom-call(bf16[1024,1024]{1,0:T(8,128)(2,1)S(1)} %pad_maximum_fusion.11.grad_mixed.right_near, f32[1024,768]{1,0:T(8,128)S(1)} %copy-done.3, f32[1024,4]{1,0:T(8,128)S(1)} %bitcast.203, ...), custom_call_target="tpu_custom_call" | custom-call | flops 1 | bytes 1 | tf_op jit(solution)/shard_map/pallas_call | solution.py:299
  322.3 4.3 shard_map.197
  329.7 4.0 collective-permute-done.42
  344.7 3.9 add_convert_fusion.1
  356.3 15.4 %collective-permute-done.48 = bf16[1,288,512]{2,1,0:T(8,128)(2,1)S(1)} collective-permute-done((bf16[1,288,512]{2,1,0:T(8,128)(2,1)S(1)}, bf16[1,288,512]{2,1,0:T(8,128)(2,1)S(1)}, u32[]{:S(2)}, u32[]{:S(2)}) %collective-permute-start.48) | collective-permute-done | bytes 294944 | tf_op jit(solution)/shard_map/ppermute | solution.py:43
  380.4 4.0 add_convert_fusion
  418.9 8.0 %collective-permute-done.60 = bf16[512,512]{1,0:T(8,128)(2,1)} collective-permute-done((bf16[512,512]{1,0:T(8,128)(2,1)}, bf16[512,512]{1,0:T(8,128)(2,1)}, u32[]{:S(2)}, u32[]{:S(2)}) %collective-permute-start.60) | collective-permute-done | bytes 524320 | tf_op jit(solution)/shard_map/ppermute | solution.py:38
  (554 shorter events, 255.8 us)
Async XLA Ops:
  25.6 20.6 %collective-permute-start.5 = (bf16[512,512]{1,0:T(8,128)(2,1)S(1)}, bf16[512,512]{1,0:T(8,128)(2,1)S(1)}, u32[]{:S(2)}, u32[]{:S(2)}) collective-permute-start(bf16[512,512]{1,0:T(8,128)(2,1)S(1)} %collective-permute-done.1), channel_id=1, source_target_pairs={{0,16},{8,24},{16,0},{24,8},{1,17},{9,25},{17,1},{25,9},{2,18},{10... | collective-permute-start | bytes 1572872 | tf_op jit(solution)/shard_map/ppermute | solution.py:26
  55.7 25.8 %collective-permute-start.11 = (bf16[784,512]{1,0:T(8,128)(2,1)}, bf16[784,512]{1,0:T(8,128)(2,1)}, u32[]{:S(2)}, u32[]{:S(2)}) collective-permute-start(bf16[784,512]{1,0:T(8,128)(2,1)} %pad_maximum_fusion.20), channel_id=1, source_target_pairs={{0,4},{4,0},{1,5},{5,1},{2,6},{6,2},{3,7},{7,3},{8,12},{12,8},{9,1... | collective-permute-start | bytes 2408456 | tf_op jit(solution)/shard_map/ppermute | solution.py:38
  56.8 24.7 %collective-permute-start.12 = (bf16[256,512]{1,0:T(8,128)(2,1)S(1)}, bf16[256,512]{1,0:T(8,128)(2,1)S(1)}, u32[]{:S(2)}, u32[]{:S(2)}) collective-permute-start(bf16[256,512]{1,0:T(8,128)(2,1)S(1)} %bitcast.196), channel_id=1, source_target_pairs={{0,4},{4,0},{1,5},{5,1},{2,6},{6,2},{3,7},{7,3},{8,12},{12,8},{9,1... | collective-permute-start | bytes 786440 | tf_op jit(solution)/shard_map/ppermute | solution.py:38
  57.8 23.7 %collective-permute-start.13 = (bf16[2,288,512]{2,1,0:T(8,128)(2,1)}, bf16[2,288,512]{2,1,0:T(8,128)(2,1)S(1)}, u32[]{:S(2)}, u32[]{:S(2)}) collective-permute-start(bf16[2,288,512]{2,1,0:T(8,128)(2,1)} %pad_maximum_fusion.22), channel_id=1, source_target_pairs={{0,1},{1,0},{2,3},{3,2},{4,5},{5,4},{6,7},{7,6},{8,9},{9,8},{10,11... | collective-permute-start | bytes 1769480 | tf_op jit(solution)/shard_map/ppermute | solution.py:43
  68.8 24.3 %collective-permute-start.19 = (bf16[512,1024]{1,0:T(8,128)(2,1)}, bf16[512,1024]{1,0:T(8,128)(2,1)S(1)}, u32[]{:S(2)}, u32[]{:S(2)}) collective-permute-start(bf16[512,1024]{1,0:T(8,128)(2,1)} %pad_maximum_fusion.18), channel_id=1, source_target_pairs={{0,16},{8,24},{16,0},{24,8},{1,17},{9,25},{17,1},{25,9},{2,18},{10... | collective-permute-start | bytes 3145736 | tf_op jit(solution)/shard_map/ppermute | solution.py:26
  93.3 28.5 %collective-permute-start.20 = (bf16[2,512,1024]{2,1,0:T(8,128)(2,1)S(1)}, bf16[2,512,1024]{2,1,0:T(8,128)(2,1)S(1)}, u32[]{:S(2)}, u32[]{:S(2)}) collective-permute-start(bf16[2,512,1024]{2,1,0:T(8,128)(2,1)S(1)} %pad_maximum_fusion.4), channel_id=1, source_target_pairs={{0,8},{8,0},{16,24},{24,16},{1,9},{9,1},{17,25},{25,17},{2,10},{10... | collective-permute-start | bytes 6291464 | tf_op jit(solution)/shard_map/ppermute | solution.py:26
  93.4 28.4 %collective-permute-start.18 = (bf16[1152,512]{1,0:T(8,128)(2,1)S(1)}, bf16[1152,512]{1,0:T(8,128)(2,1)S(1)}, u32[]{:S(2)}, u32[]{:S(2)}) collective-permute-start(bf16[1152,512]{1,0:T(8,128)(2,1)S(1)} %bitcast.187), channel_id=1, source_target_pairs={{0,4},{4,0},{1,5},{5,1},{2,6},{6,2},{3,7},{7,3},{8,12},{12,8},{9,1... | collective-permute-start | bytes 3538952 | tf_op jit(solution)/shard_map/ppermute | solution.py:38
  95.0 21.7 %collective-permute-start.16 = (bf16[2,288,512]{2,1,0:T(8,128)(2,1)S(1)}, bf16[2,288,512]{2,1,0:T(8,128)(2,1)S(1)}, u32[]{:S(2)}, u32[]{:S(2)}) collective-permute-start(bf16[2,288,512]{2,1,0:T(8,128)(2,1)S(1)} %pad_maximum_fusion.23), channel_id=1, source_target_pairs={{0,1},{1,0},{2,3},{3,2},{4,5},{5,4},{6,7},{7,6},{8,9},{9,8},{10,11... | collective-permute-start | bytes 1769480 | tf_op jit(solution)/shard_map/ppermute | solution.py:43
  126.0 28.0 %collective-permute-start.25 = (bf16[1152,512]{1,0:T(8,128)(2,1)S(1)}, bf16[1152,512]{1,0:T(8,128)(2,1)S(1)}, u32[]{:S(2)}, u32[]{:S(2)}) collective-permute-start(bf16[1152,512]{1,0:T(8,128)(2,1)S(1)} %bitcast.190), channel_id=1, source_target_pairs={{0,4},{4,0},{1,5},{5,1},{2,6},{6,2},{3,7},{7,3},{8,12},{12,8},{9,1... | collective-permute-start | bytes 3538952 | tf_op jit(solution)/shard_map/ppermute | solution.py:38
  127.9 25.0 %collective-permute-start.23 = (bf16[512,1024]{1,0:T(8,128)(2,1)S(1)}, bf16[512,1024]{1,0:T(8,128)(2,1)S(1)}, u32[]{:S(2)}, u32[]{:S(2)}) collective-permute-start(bf16[512,1024]{1,0:T(8,128)(2,1)S(1)} %fusion.17), channel_id=1, source_target_pairs={{0,16},{8,24},{16,0},{24,8},{1,17},{9,25},{17,1},{25,9},{2,18},{10... | collective-permute-start | bytes 3145736 | tf_op jit(solution)/shard_map/ppermute | solution.py:26
  155.0 24.4 %collective-permute-start.27 = (bf16[512,1024]{1,0:T(8,128)(2,1)S(1)}, bf16[512,1024]{1,0:T(8,128)(2,1)S(1)}, u32[]{:S(2)}, u32[]{:S(2)}) collective-permute-start(bf16[512,1024]{1,0:T(8,128)(2,1)S(1)} %get-tuple-element.547), channel_id=1, source_target_pairs={{0,16},{8,24},{16,0},{24,8},{1,17},{9,25},{17,1},{25,9},{2,18},{10... | collective-permute-start | bytes 3145736 | tf_op jit(solution)/shard_map/ppermute | solution.py:26
  155.6 26.9 %collective-permute-start.26 = (bf16[1152,512]{1,0:T(8,128)(2,1)S(1)}, bf16[1152,512]{1,0:T(8,128)(2,1)S(1)}, u32[]{:S(2)}, u32[]{:S(2)}) collective-permute-start(bf16[1152,512]{1,0:T(8,128)(2,1)S(1)} %bitcast.193), channel_id=1, source_target_pairs={{0,4},{4,0},{1,5},{5,1},{2,6},{6,2},{3,7},{7,3},{8,12},{12,8},{9,1... | collective-permute-start | bytes 3538952 | tf_op jit(solution)/shard_map/ppermute | solution.py:38
  211.4 25.5 %collective-permute-start.30 = (bf16[512,1024]{1,0:T(8,128)(2,1)}, bf16[512,1024]{1,0:T(8,128)(2,1)}, u32[]{:S(2)}, u32[]{:S(2)}) collective-permute-start(bf16[512,1024]{1,0:T(8,128)(2,1)} %fusion.19), channel_id=1, source_target_pairs={{0,16},{8,24},{16,0},{24,8},{1,17},{9,25},{17,1},{25,9},{2,18},{10... | collective-permute-start | bytes 3145736 | tf_op jit(solution)/shard_map/ppermute | solution.py:26
  240.0 31.8 %collective-permute-start.34 = (bf16[512,1024]{1,0:T(8,128)(2,1)S(1)}, bf16[512,1024]{1,0:T(8,128)(2,1)S(1)}, u32[]{:S(2)}, u32[]{:S(2)}) collective-permute-start(bf16[512,1024]{1,0:T(8,128)(2,1)S(1)} %fusion.20), channel_id=1, source_target_pairs={{0,16},{8,24},{16,0},{24,8},{1,17},{9,25},{17,1},{25,9},{2,18},{10... | collective-permute-start | bytes 3145736 | tf_op jit(solution)/shard_map/ppermute | solution.py:26
  249.3 31.0 %collective-permute-start.32 = (bf16[1152,512]{1,0:T(8,128)(2,1)S(1)}, bf16[1152,512]{1,0:T(8,128)(2,1)}, u32[]{:S(2)}, u32[]{:S(2)}) collective-permute-start(bf16[1152,512]{1,0:T(8,128)(2,1)S(1)} %get-tuple-element.359), channel_id=1, source_target_pairs={{0,4},{4,0},{1,5},{5,1},{2,6},{6,2},{3,7},{7,3},{8,12},{12,8},{9,1... | collective-permute-start | bytes 3538952 | tf_op jit(solution)/shard_map/ppermute | solution.py:38
  262.9 27.8 %collective-permute-start.33 = (bf16[1,576,1024]{2,1,0:T(8,128)(2,1)}, bf16[1,576,1024]{2,1,0:T(8,128)(2,1)}, u32[]{:S(2)}, u32[]{:S(2)}) collective-permute-start(bf16[1,576,1024]{2,1,0:T(8,128)(2,1)} %fusion.21), channel_id=1, source_target_pairs={{0,1},{1,0},{2,3},{3,2},{4,5},{5,4},{6,7},{7,6},{8,9},{9,8},{10,11... | collective-permute-start | bytes 3538952 | tf_op jit(solution)/shard_map/ppermute | solution.py:43
  304.5 29.2 %collective-permute-start.41 = (bf16[1152,512]{1,0:T(8,128)(2,1)}, bf16[1152,512]{1,0:T(8,128)(2,1)}, u32[]{:S(2)}, u32[]{:S(2)}) collective-permute-start(bf16[1152,512]{1,0:T(8,128)(2,1)} %get-tuple-element.408), channel_id=1, source_target_pairs={{0,4},{4,0},{1,5},{5,1},{2,6},{6,2},{3,7},{7,3},{8,12},{12,8},{9,1... | collective-permute-start | bytes 3538952 | tf_op jit(solution)/shard_map/ppermute | solution.py:38
  305.7 28.0 %collective-permute-start.40 = (bf16[512,1024]{1,0:T(8,128)(2,1)}, bf16[512,1024]{1,0:T(8,128)(2,1)}, u32[]{:S(2)}, u32[]{:S(2)}) collective-permute-start(bf16[512,1024]{1,0:T(8,128)(2,1)} %add_convert_fusion.2), channel_id=1, source_target_pairs={{0,16},{8,24},{16,0},{24,8},{1,17},{9,25},{17,1},{25,9},{2,18},{10... | collective-permute-start | bytes 3145736 | tf_op jit(solution)/shard_map/ppermute | solution.py:26
  306.3 27.4 %collective-permute-start.42 = (bf16[1,576,512]{2,1,0:T(8,128)(2,1)}, bf16[1,576,512]{2,1,0:T(8,128)(2,1)}, u32[]{:S(2)}, u32[]{:S(2)}) collective-permute-start(bf16[1,576,512]{2,1,0:T(8,128)(2,1)} %fusion.27), channel_id=1, source_target_pairs={{0,1},{1,0},{2,3},{3,2},{4,5},{5,4},{6,7},{7,6},{8,9},{9,8},{10,11... | collective-permute-start | bytes 1769480 | tf_op jit(solution)/shard_map/ppermute | solution.py:43
  307.1 26.7 %collective-permute-start.43 = (bf16[1,288,1024]{2,1,0:T(8,128)(2,1)}, bf16[1,288,1024]{2,1,0:T(8,128)(2,1)}, u32[]{:S(2)}, u32[]{:S(2)}) collective-permute-start(bf16[1,288,1024]{2,1,0:T(8,128)(2,1)} %slice.591), channel_id=1, source_target_pairs={{0,2},{1,3},{2,0},{3,1},{4,6},{5,7},{6,4},{7,5},{8,10},{9,11},{10,... | collective-permute-start | bytes 1769480 | tf_op jit(solution)/shard_map/ppermute | solution.py:43
  314.6 30.1 %collective-permute-start.39 = (bf16[512,1024]{1,0:T(8,128)(2,1)}, bf16[512,1024]{1,0:T(8,128)(2,1)}, u32[]{:S(2)}, u32[]{:S(2)}) collective-permute-start(bf16[512,1024]{1,0:T(8,128)(2,1)} %get-tuple-element.406), channel_id=1, source_target_pairs={{0,8},{8,0},{16,24},{24,16},{1,9},{9,1},{17,25},{25,17},{2,10},{10... | collective-permute-start | bytes 3145736 | tf_op jit(solution)/shard_map/ppermute | solution.py:26
  348.6 35.8 %collective-permute-start.45 = (bf16[512,1024]{1,0:T(8,128)(2,1)}, bf16[512,1024]{1,0:T(8,128)(2,1)}, u32[]{:S(2)}, u32[]{:S(2)}) collective-permute-start(bf16[512,1024]{1,0:T(8,128)(2,1)} %add_convert_fusion.1), channel_id=1, source_target_pairs={{0,16},{8,24},{16,0},{24,8},{1,17},{9,25},{17,1},{25,9},{2,18},{10... | collective-permute-start | bytes 3145736 | tf_op jit(solution)/shard_map/ppermute | solution.py:26
  350.1 34.4 %collective-permute-start.46 = (bf16[1024,512]{1,0:T(8,128)(2,1)}, bf16[1024,512]{1,0:T(8,128)(2,1)}, u32[]{:S(2)}, u32[]{:S(2)}) collective-permute-start(bf16[1024,512]{1,0:T(8,128)(2,1)} %pad_maximum_fusion.19), channel_id=1, source_target_pairs={{0,4},{4,0},{1,5},{5,1},{2,6},{6,2},{3,7},{7,3},{8,12},{12,8},{9,1... | collective-permute-start | bytes 3145736 | tf_op jit(solution)/shard_map/ppermute | solution.py:38
  352.4 21.5 %collective-permute-start.47 = (bf16[1,576,512]{2,1,0:T(8,128)(2,1)S(1)}, bf16[1,576,512]{2,1,0:T(8,128)(2,1)S(1)}, u32[]{:S(2)}, u32[]{:S(2)}) collective-permute-start(bf16[1,576,512]{2,1,0:T(8,128)(2,1)S(1)} %fusion.28), channel_id=1, source_target_pairs={{0,1},{1,0},{2,3},{3,2},{4,5},{5,4},{6,7},{7,6},{8,9},{9,8},{10,11... | collective-permute-start | bytes 1769480 | tf_op jit(solution)/shard_map/ppermute | solution.py:43
  (152 other events, 1353.6 us)

commit v5 on v4

--- a/solution.py
+++ b/solution.py
@@ -1,3 +1,5 @@
+import functools
+
 import jax
 import jax.numpy as jnp
 from jax import lax
@@ -333,6 +335,30 @@
     )(*lefts, *rights)
 
 
+def assemble_kernel(turned, place, own, far, pair, out, rows):
+    count = own.shape[0]
+    for distance, block in enumerate((own[...], pair[0], far[...], pair[1])):
+        start = pl.multiple_of((place[0] ^ distance) * count, 16)
+        rows[pl.ds(start, count), :] = wide(block)
+    out[...] = rows[...].T if turned else rows[...]
+
+
+def assemble(own, far, pair, turned):
+    count, half = own.shape
+    shape = (half, TEAM * count) if turned else (TEAM * count, half)
+    place = (lax.axis_index("dp") % TEAM).astype(jnp.int32).reshape(1)
+    vmem = pl.BlockSpec(memory_space=pltpu.VMEM)
+    return pl.pallas_call(
+        functools.partial(assemble_kernel, turned),
+        in_specs=[pl.BlockSpec(memory_space=pltpu.SMEM), vmem, vmem, vmem],
+        out_specs=vmem,
+        out_shape=jax.ShapeDtypeStruct(shape, jnp.float32),
+        scratch_shapes=[pltpu.VMEM((TEAM * count, half), jnp.float32)],
+        compiler_params=pltpu.CompilerParams(vmem_limit_bytes=16 * 2**20),
+        cost_estimate=COST,
+    )(place, own, far, pair)
+
+
 def body(
     tokens,
     segment_ids,
@@ -436,18 +462,17 @@
     gains = wide(jnp.concatenate([gains, in_row[4 * in_rows + 3 : 4 * in_rows + 5]], axis=1))
     gain_one, gain_two = gains[0], gains[1]
     in_near, in_row = in_near[: 4 * in_rows], in_row[: 4 * in_rows]
+    gate_near = stacked(gate_pair, gate_other, 1)
+    gate_near, up_pair, down_part, inputs = meet(gate_near, up_pair, down_part, inputs)
+    gate_row = over_row(gate_near)
+    up_other = col_swap(up_pair, 1)
+    down_pair = col_first(down_part)
+    grads_pair = over_core(jnp.stack([grads_near, grads_far]))
     ends = wide(jnp.concatenate([one[at + size - 8 : at + size] for one in inputs for at in (0, size)], axis=0))
     ends = narrow(ends * norm_scale(ends) * gain_one)
     ends = dot_nt(ends[:, :half], in_near) + dot_nt(ends[:, half:], in_row)
     ends = (ends[:, :width] * ends[:, 2 * width :]).reshape(2, 2, 8, width)[:, :, 6:]
-    gate_near = stacked(gate_pair, gate_other, 1)
-    before, gate_near, up_pair, down_part, inputs, grads_own_x = hop(
-        over_row, ends, gate_near, up_pair, down_part, inputs, grads_near
-    )
-    gate_row = over_row(gate_near)
-    up_other = col_swap(up_pair, 1)
-    down_pair = col_first(down_part)
-    grads_pair = over_core(jnp.stack([grads_own_x, grads_far]))
+    before = over_row(ends)
     normed_one, projected = zip(
         *[
             token_call(
@@ -525,15 +550,18 @@
     far_moved, far_own, grad_gate, grad_up, act = hop(over_core, far_sent, far_own, grad_gate, grad_up, act)
     far_send, grad_gate, grad_up, act = meet(narrow(wide(far_own) + wide(far_moved)), grad_gate, grad_up, act)
     back_from_far = over_x(far_send)
-    gate_own, gate_sent = weight_grads(grad_gate, normed_two, units // 3)
-    gate_moved = over_row(gate_sent)
-    gate_sent, grad_up, act = meet(gate_sent, grad_up, act)
+    near_out_moved, far_out_moved = over_core(near_out_sent), over_core(far_out_sent)
     down_own, down_sent = weight_grads(act, cotangents, units // 3)
     down_sent, down_kept = col_send(jnp.concatenate([down_own, wide(down_sent)], axis=1), 1)
     down_moved = col_swap(down_sent, 1)
-    down_sent, grad_up, act = meet(down_sent, grad_up, act)
+    down_sent, grad_gate, grad_up = meet(down_sent, grad_gate, grad_up)
+    gate_own, gate_sent = weight_grads(grad_gate, normed_two, units // 3)
+    gate_moved = over_row(gate_sent)
+    gate_sent, grad_up = meet(gate_sent, grad_up)
     up_own, up_sent = weight_grads(grad_up, normed_two, units // 3)
-    back_from_far, up_sent = meet(back_from_far, up_sent)
+    back_from_far, up_sent, near_out_moved, far_out_moved = meet(
+        back_from_far, up_sent, near_out_moved, far_out_moved
+    )
 
     back_sums = (
         wide(near_own) + wide(near_moved) + wide(back_from_far),
@@ -551,10 +579,7 @@
     gate_sent, gate_kept = col_send(gate_own + wide(gate_moved), 1)
     down_sent, down_kept = col_add(down_kept, down_moved)
     low_moved = over_core(jnp.stack(low))
-    near_out_moved, far_out_moved = over_core(near_out_sent), over_core(far_out_sent)
-    low_moved, near_out_moved, far_out_moved, low, up_sent, gate_sent, down_sent = meet(
-        low_moved, near_out_moved, far_out_moved, low, up_sent, gate_sent, down_sent
-    )
+    low_moved, low, up_sent, gate_sent, down_sent = meet(low_moved, low, up_sent, gate_sent, down_sent)
     grad_mixed = [jnp.concatenate([low[which], low_moved[which]], axis=0) for which in (0, 1)]
     far_out = narrow(wide(far_out_own) + wide(far_out_moved))
 
@@ -588,22 +613,6 @@
     out_own, out_sent = weight_grads(mixed, grad_mixed, width)
     mixer_own = jnp.concatenate([in_own, out_own], axis=0)
     mixer_sent = jnp.concatenate([in_sent, out_sent], axis=0)
-    out_from_far, up_moved, gate_moved, down_moved, far_one, near_one, near_one_sent, mixer_sent = meet(
-        out_from_far, up_moved, gate_moved, down_moved, far_one, near_one, near_one_sent, mixer_sent
-    )
-    gate_sent, gate_kept = col_add(gate_kept, gate_moved)
-    up_sent, up_kept = col_send(up_own + wide(up_moved), 1)
-    down_own, down_sent = exchange(col_last(down_kept, down_moved))
-    far_one_moved, near_one_moved, far_one, near_one, mixer_sent, up_sent, gate_sent, down_sent = meet(
-        over_core(far_one_sent), over_core(near_one_sent), far_one, near_one, mixer_sent, up_sent, gate_sent, down_sent
-    )
-    one_send = narrow(wide(far_one) + wide(far_one_moved))
-    one_send, mixer_sent, far_one, near_one = meet(one_send, mixer_sent, far_one, near_one)
-    mixer_moved = over_row(mixer_sent)
-    up_moved = col_swap(up_sent, 1)
-    gate_moved = col_swap(gate_sent, 2)
-    one_from_far = over_x(one_send)
-    result = narrow(hidden_near + (wide(near_out_own) + wide(near_out_moved) + wide(out_from_far)))
     gain_one_grad = 0.0
     for rows, one in (
         (near_tokens[0], near_one), (near_tokens[1], near_one_sent), (far_tokens[0], far_one), (far_tokens[1], far_one_sent)
@@ -616,9 +625,29 @@
     apart = jnp.arange(cols) ^ col
     conv_flat = jnp.take(conv_flat, apart // 2 + apart % 2 * 2, axis=0).reshape(-1)
     small = jnp.concatenate([gain_local[:, :half].reshape(-1), conv_flat, gain_local[:, half:].reshape(-1)])
-    small, up_moved, gate_moved = meet(small, up_moved, gate_moved)
-    for distance in (1, 2):
-        small = small + col_swap(small, distance)
+    out_from_far, up_moved, gate_moved, down_moved, far_one, near_one, near_one_sent, mixer_sent, small = meet(
+        out_from_far, up_moved, gate_moved, down_moved, far_one, near_one, near_one_sent, mixer_sent, small
+    )
+    far_one_moved, near_one_moved, small_moved, far_one, near_one, mixer_sent, up_moved, gate_moved, down_moved = meet(
+        over_core(far_one_sent), over_core(near_one_sent), col_swap(small, 1),
+        far_one, near_one, mixer_sent, up_moved, gate_moved, down_moved,
+    )
+    one_send = narrow(wide(far_one) + wide(far_one_moved))
+    small = small + small_moved
+    one_send, mixer_sent, small, up_moved, gate_moved, down_moved, near_one, far_one = meet(
+        one_send, mixer_sent, small, up_moved, gate_moved, down_moved, near_one, far_one
+    )
+    one_from_far = over_x(one_send)
+    mixer_moved = over_row(mixer_sent)
+    small_moved = col_swap(small, 2)
+    gate_sent, gate_kept = col_add(gate_kept, gate_moved)
+    up_sent, up_kept = col_send(up_own + wide(up_moved), 1)
+    down_own, down_sent = exchange(col_last(down_kept, down_moved))
+    up_sent, gate_sent = meet(up_sent, gate_sent)
+    up_moved = col_swap(up_sent, 1)
+    gate_moved = col_swap(gate_sent, 2)
+    result = narrow(hidden_near + (wide(near_out_own) + wide(near_out_moved) + wide(out_from_far)))
+    small = small + small_moved
     one_from_far, mixer_moved, up_moved, gate_moved, near_one, result, down_sent, small = meet(
         one_from_far, mixer_moved, up_moved, gate_moved, near_one, result, down_sent, small
     )
@@ -659,27 +688,31 @@
     both = jnp.stack([up_total, down_total])
     both_far = over_x(both)
     input_row = over_row(narrow(input_grad[:, half:]))
-    small = other_teams(small + over_core(small))
+    gate_pair = over_core(jnp.stack([gate_total, gate_far]))
+    small_moved = over_core(small)
+    gate_grad = assemble(gate_total, gate_far, gate_pair, True)
+    small = other_teams(small + small_moved)
     conv_grad = small[2 * half :].reshape(TEAM, 3, channels).transpose(1, 0, 2).reshape(3, TEAM * channels)
-    gate_pair = over_core(jnp.stack([gate_total, gate_far]))
-    mixer_moved, both_far, gate_pair, result, input_row = meet(mixer_moved, both_far, gate_pair, result, input_row)
+    mixer_moved, both_far, gate_grad, result, conv_grad, input_row = meet(
+        mixer_moved, both_far, gate_grad, result, conv_grad, input_row
+    )
     mixer_total = team_first(col_last(mixer_kept, mixer_moved))
-    mixer_total, both_far, gate_pair, result = meet(mixer_total, both_far, gate_pair, result)
+    mixer_total, both_far = meet(mixer_total, both_far)
     mixer_far = over_x(mixer_total)
+    both_pair = over_core(jnp.stack([both, both_far]))
+    up_grad = assemble(up_total, both_far[0], both_pair[:, 0], True)
     result_row = over_row(result[:, half:])
-    both_pair = over_core(jnp.stack([both, both_far]))
-    gate_grad = wide(team_rows(gate_total, gate_far, gate_pair, 1)[0].T)
-    mixer_far, both_pair = meet(mixer_far, both_pair)
-    up_grad = wide(team_rows(up_total, both_far[0], both_pair[:, 0], 1)[0].T)
-    down_grad = wide(team_rows(down_total, both_far[1], both_pair[:, 1], 1)[0])
+    mixer_far, up_grad, both_pair, input_grad = meet(
+        mixer_far, up_grad, both_pair, to_blocks(input_grad[:, :half], input_row)
+    )
     mixer_pair = over_core(jnp.stack([mixer_total, mixer_far]))
+    down_grad = assemble(down_total, both_far[1], both_pair[:, 1], False)
     mixer_grads = team_rows(mixer_total, mixer_far, mixer_pair, 4)
     in_grad = wide(mixer_grads[:3].transpose(2, 0, 1))
     out_grad = wide(mixer_grads[3])
-
     return (
         to_blocks(result[:, :half], result_row),
-        to_blocks(input_grad[:, :half], input_row),
+        input_grad,
         small[:half],
         in_grad,
         conv_grad,

time: 472 us -> 443 us (0.939)
  local copies, waits for them, and re-layouts: 76.2 us -> 50 us
  Pallas kernels: 82.1 us -> 88.2 us
    dynamic_update_slice x13 -> x4, local copies, waits for them, and re-layouts: 12.3 us -> 1.05 us  [team_rows(): lax.dynamic_update_slice(result, block, (0, (place ^ distance) * rows, 0))]
    unnamed x226 -> x166, local copies, waits for them, and re-layouts: 28.2 us -> 17 us
    pallas_call x0 -> x3, Pallas kernels: none -> 6.19 us  [assemble(): pl.pallas_call(functools.partial(assemble_kernel, turned), in_specs=[pl.B...]
    ppermute x17, waiting for transfers between devices: 18.8 us -> 24.9 us  [over_row(): return lax.ppermute(values, 'row', [(0, 1), (1, 0)])]
    convert_element_type x12 -> x14, other arithmetic: 18.3 us -> 18.1 us  [narrow(): return values.astype(jnp.bfloat16)]
  transfers between devices with their start and end apart: 66 -> 66, of which waited for: 34 -> 35; matrix products, arithmetic and copies ran while one was open for 23% -> 21% of each run, Pallas kernels for 14% -> 14%
where the time goes in v5:
time: 443 us; the launch traced here: 437 us
  waiting for transfers between devices  152 us (34%)
  Pallas kernels  88.2 us (20%)
  other arithmetic  76.6 us (17%)
  starting transfers between devices  64.1 us (14%)
  local copies, waits for them, and re-layouts  50 us (11%)
    ppermute x18, waiting for transfers between devices, col_swap(): return lax.ppermute(values, 'col', [(i, i ^ distance) for i in range(size)])  77 us
    ppermute x31, waiting for transfers between devices, over_dp(): return lax.ppermute(values, 'dp', [(i, i ^ distance) for i in range(size)])  50.2 us
    pallas_call x2, Pallas kernels, gated_call(): pl.pallas_call(gated_kernel, grid=(steps,), in_specs=[row_tiles(normed),...  38.4 us
    ppermute x18, starting transfers between devices, col_swap(): return lax.ppermute(values, 'col', [(i, i ^ distance) for i in range(size)])  26.8 us
    ppermute x17, waiting for transfers between devices, over_row(): return lax.ppermute(values, 'row', [(0, 1), (1, 0)])  24.9 us
    pallas_call x5, Pallas kernels, weight_grads(): pl.pallas_call(weight_kernel, grid=(columns // tile,), in_specs=[left_spe...  24.3 us
    ppermute x17, starting transfers between devices, over_row(): return lax.ppermute(values, 'row', [(0, 1), (1, 0)])  20.3 us
    convert_element_type x14, other arithmetic, narrow(): return values.astype(jnp.bfloat16)  18.1 us
  transfers between devices with their start and end apart: 66, of which 35 were waited for; matrix products, arithmetic and copies ran while one was open for 21% of the time, Pallas kernels for 14%

profile of v5, /device:TPU:0, one launch (start us, length us, event | category | flops | bytes accessed | tf_op | source)
XLA Modules:
  0.0 437.0 jit_solution(2910919593655685979)
XLA Ops:
  5.9 4.0 collective-permute-start
  33.9 11.4 %collective-permute-done.8 = bf16[288,512]{1,0:T(8,128)(2,1)S(1)} collective-permute-done((bf16[288,512]{1,0:T(8,128)(2,1)S(1)}, bf16[288,512]{1,0:T(8,128)(2,1)S(1)}, u32[]{:S(2)}, u32[]{:S(2)}) %collective-permute-start.8) | collective-permute-done | bytes 294944 | tf_op jit(solution)/shard_map/ppermute | solution.py:45
  69.2 10.9 %collective-permute-done.14 = bf16[288,512]{1,0:T(8,128)(2,1)} collective-permute-done((bf16[288,512]{1,0:T(8,128)(2,1)}, bf16[288,512]{1,0:T(8,128)(2,1)}, u32[]{:S(2)}, u32[]{:S(2)}) %collective-permute-start.14) | collective-permute-done | bytes 294944 | tf_op jit(solution)/shard_map/ppermute | solution.py:45
  108.7 5.2 %collective-permute-done.20 = f32[2,2,2,256]{3,2,1,0:T(2,128)S(1)} collective-permute-done((f32[2,2,2,256]{3,2,1,0:T(2,128)S(1)}, f32[2,2,2,256]{3,2,1,0:T(2,128)S(1)}, u32[]{:S(2)}, u32[]{:S(2)}) %collective-permute-start.20) | collective-permute-done | bytes 8224 | tf_op jit(solution)/shard_map/ppermute | solution.py:40
  123.9 14.5 %collective-permute-done.24 = bf16[2,288,512]{2,1,0:T(8,128)(2,1)S(1)} collective-permute-done((bf16[2,288,512]{2,1,0:T(8,128)(2,1)S(1)}, bf16[2,288,512]{2,1,0:T(8,128)(2,1)S(1)}, u32[]{:S(2)}, u32[]{:S(2)}) %collective-permute-start.24) | collective-permute-done | bytes 589856 | tf_op jit(solution)/shard_map/ppermute | solution.py:45
  138.5 9.6 %collective-permute-done.23 = bf16[512,1024]{1,0:T(8,128)(2,1)S(1)} collective-permute-done((bf16[512,1024]{1,0:T(8,128)(2,1)S(1)}, bf16[512,1024]{1,0:T(8,128)(2,1)S(1)}, u32[]{:S(2)}, u32[]{:S(2)}) %collective-permute-start.23) | collective-permute-done | bytes 1048608 | tf_op jit(solution)/shard_map/ppermute | solution.py:28
  152.5 22.1 %collective-permute-done.27 = bf16[512,1024]{1,0:T(8,128)(2,1)S(1)} collective-permute-done((bf16[512,1024]{1,0:T(8,128)(2,1)S(1)}, bf16[512,1024]{1,0:T(8,128)(2,1)S(1)}, u32[]{:S(2)}, u32[]{:S(2)}) %collective-permute-start.27) | collective-permute-done | bytes 1048608 | tf_op jit(solution)/shard_map/ppermute | solution.py:28
  177.9 4.1 collective-permute-done.28
  183.4 19.1 %shard_map.190 = (bf16[1024,1152]{1,0:T(8,128)(2,1)S(1)}, bf16[1024,1152]{1,0:T(8,128)(2,1)}, bf16[1024,1152]{1,0:T(8,128)(2,1)}, bf16[512,1024]{1,0:T(8,128)(2,...) custom-call(bf16[1024,1024]{1,0:T(8,128)(2,1)S(1)} %pad_maximum_fusion.8.normed., ...), custom_call_target="tpu_custom_call" | custom-call | flops 1 | bytes 1 | tf_op jit(solution)/shard_map/pallas_call | solution.py:208
  209.1 19.2 %shard_map.191 = (bf16[1024,1152]{1,0:T(8,128)(2,1)S(1)}, bf16[1024,1152]{1,0:T(8,128)(2,1)}, bf16[1024,1152]{1,0:T(8,128)(2,1)}, bf16[512,1024]{1,0:T(8,128)(2,...) custom-call(bf16[1024,1024]{1,0:T(8,128)(2,1)S(1)} %pad_maximum_fusion.9.normed., ...), custom_call_target="tpu_custom_call" | custom-call | flops 1 | bytes 1 | tf_op jit(solution)/shard_map/pallas_call | solution.py:208
  228.4 4.8 %collective-permute-done.30 = bf16[512,1024]{1,0:T(8,128)(2,1)} collective-permute-done((bf16[512,1024]{1,0:T(8,128)(2,1)}, bf16[512,1024]{1,0:T(8,128)(2,1)}, u32[]{:S(2)}, u32[]{:S(2)}) %collective-permute-start.30) | collective-permute-done | bytes 1048608 | tf_op jit(solution)/shard_map/ppermute | solution.py:28
  241.1 6.0 %shard_map.192 = (f32[1152,512]{1,0:T(8,128)S(1)}, bf16[1152,512]{1,0:T(8,128)(2,1)S(1)}) custom-call(bf16[1024,1152]{1,0:T(8,128)(2,1)S(1)} %copy-done.17, bf16[1024,1152]{1,0:T(8,128)(2,1)S(1)} %get-tuple-element.359.left_far, bf16[1024,1024]{1,0:T(8,128)(2,1)S(1)} %pad_maximum_fusion.5.cotangent.right_near, ...), custom_call_target="tpu_custom_call" | custom-call | flops 1 | bytes 1 | tf_op jit(solution)/shard_map/pallas_call | solution.py:324
  253.4 6.0 %shard_map.193 = (f32[1152,512]{1,0:T(8,128)S(1)}, bf16[1152,512]{1,0:T(8,128)(2,1)S(1)}) custom-call(bf16[1024,1152]{1,0:T(8,128)(2,1)S(1)} %copy-done.14, bf16[1024,1152]{1,0:T(8,128)(2,1)S(1)} %copy-done.18, bf16[1024,1024]{1,0:T(8,128)(2,1)S(1)} %pad_maximum_fusion.8.normed.right_near, bf16[1024,1024]{1,0:T(8,128)(2,1)S(1)} %pad_maximum_fusion.9.normed.right_far), custom_call_target="tpu_custom_call" | custom-call | flops 1 | bytes 1 | tf_op jit(solution)/shard_map/pallas_call | solution.py:324
  261.0 6.8 %shard_map.194 = (f32[1152,512]{1,0:T(8,128)S(1)}, bf16[1152,512]{1,0:T(8,128)(2,1)}) custom-call(bf16[1024,1152]{1,0:T(8,128)(2,1)S(1)} %copy-done.13, bf16[1024,1152]{1,0:T(8,128)(2,1)S(1)} %copy-done.15, bf16[1024,1024]{1,0:T(8,128)(2,1)S(1)} %pad_maximum_fusion.8.normed.right_near, bf16[1024,1024]{1,0:T(8,128)(2,1)S(1)} %pad_maximum_fusion.9.normed.right_far), custom_call_target="tpu_custom_call" | custom-call | flops 1 | bytes 1 | tf_op jit(solution)/shard_map/pallas_call | solution.py:324
  272.0 4.5 %fusion.70 = (bf16[512,1024]{1,0:T(8,128)(2,1)S(1)}, f32[512,1024]{1,0:T(8,128)}, bf16[512,1024]{1,0:T(8,128)(2,1)S(1)}) fusion(f32[512]{0:T(512)S(1)} %get-tuple-element.531, f32[512,1024]{1,0:T(8,128)S(1)} %copy-done.35, f32[512]{0:T(512)S(1)} %get-tuple-element.601, f32[512]{0:T(512)S(1)} %get-tuple-element.602, f32[1024]{0:T(1024)S(1)} %bitcast.234, ...), kind=kLoop, calls=%fused_computation.259 | loop fusion | flops 13631488 | bytes 16793600 | tf_op jit(solution)/shard_map/convert_element_type | solution.py:49
  276.5 10.6 %collective-permute-done.32 = bf16[1152,512]{1,0:T(8,128)(2,1)} collective-permute-done((bf16[1152,512]{1,0:T(8,128)(2,1)S(1)}, bf16[1152,512]{1,0:T(8,128)(2,1)}, u32[]{:S(2)}, u32[]{:S(2)}) %collective-permute-start.32) | collective-permute-done | bytes 1179680 | tf_op jit(solution)/shard_map/ppermute | solution.py:40
  300.2 5.8 %shard_map.195 = (bf16[1024,768]{1,0:T(8,128)(2,1)S(1)}, f32[2,3,256]{2,1,0:T(4,128)S(1)}, bf16[512,1024]{1,0:T(8,128)(2,1)S(1)}, bf16[512,1024]{1,0:T(8,128)(2,1)}) custom-call(bf16[1024,1024]{1,0:T(8,128)(2,1)S(1)} %pad_maximum_fusion.12.grad_mixed.right_far, f32[1024,768]{1,0:T(8,128)S(1)} %copy-done.5, f32[1024,4]{1,0:T(8,128)S(1)} %bitcast.194, ...), custom_call_target="tpu_custom_call" | custom-call | flops 1 | bytes 1 | tf_op jit(solution)/shard_map/pallas_call | solution.py:301
  310.7 4.8 %shard_map.196 = (bf16[1024,768]{1,0:T(8,128)(2,1)S(1)}, f32[2,3,256]{2,1,0:T(4,128)S(1)}, bf16[512,1024]{1,0:T(8,128)(2,1)S(1)}, bf16[512,1024]{1,0:T(8,128)(2,1)S(1)}) custom-call(bf16[1024,1024]{1,0:T(8,128)(2,1)S(1)} %pad_maximum_fusion.11.grad_mixed.right_near, f32[1024,768]{1,0:T(8,128)S(1)} %copy-done.3, f32[1024,4]{1,0:T(8,128)S(1)} %bitcast.192, ...), custom_call_target="tpu_custom_call" | custom-call | flops 1 | bytes 1 | tf_op jit(solution)/shard_map/pallas_call | solution.py:301
  323.5 4.3 shard_map.197
  334.6 4.0 collective-permute-done.43
  338.8 3.6 collective-permute-done.45
  358.0 10.2 %collective-permute-done.50 = f32[2816]{0:T(1024)S(1)} collective-permute-done((f32[2816]{0:T(1024)S(1)}, f32[2816]{0:T(1024)S(1)}, u32[]{:S(2)}, u32[]{:S(2)}) %collective-permute-start.50) | collective-permute-done | bytes 11296 | tf_op jit(solution)/shard_map/ppermute | solution.py:45
  382.6 4.7 %collective-permute-done.52 = bf16[1,288,512]{2,1,0:T(8,128)(2,1)S(1)} collective-permute-done((bf16[1,288,512]{2,1,0:T(8,128)(2,1)S(1)}, bf16[1,288,512]{2,1,0:T(8,128)(2,1)S(1)}, u32[]{:S(2)}, u32[]{:S(2)}) %collective-permute-start.52) | collective-permute-done | bytes 294944 | tf_op jit(solution)/shard_map/ppermute | solution.py:45
  400.8 9.4 %collective-permute-done.57 = bf16[4,64,512]{2,1,0:T(8,128)(2,1)} collective-permute-done((bf16[4,64,512]{2,1,0:T(8,128)(2,1)}, bf16[4,64,512]{2,1,0:T(8,128)(2,1)}, u32[]{:S(2)}, u32[]{:S(2)}) %collective-permute-start.57) | collective-permute-done | bytes 262176 | tf_op jit(solution)/shard_map/ppermute | solution.py:45
  (484 shorter events, 228.7 us)
Async XLA Ops:
  55.7 25.8 %collective-permute-start.11 = (bf16[784,512]{1,0:T(8,128)(2,1)}, bf16[784,512]{1,0:T(8,128)(2,1)}, u32[]{:S(2)}, u32[]{:S(2)}) collective-permute-start(bf16[784,512]{1,0:T(8,128)(2,1)} %pad_maximum_fusion.20), channel_id=1, source_target_pairs={{0,4},{4,0},{1,5},{5,1},{2,6},{6,2},{3,7},{7,3},{8,12},{12,8},{9,1... | collective-permute-start | bytes 2408456 | tf_op jit(solution)/shard_map/ppermute | solution.py:40
  56.8 24.7 %collective-permute-start.12 = (bf16[256,512]{1,0:T(8,128)(2,1)S(1)}, bf16[256,512]{1,0:T(8,128)(2,1)S(1)}, u32[]{:S(2)}, u32[]{:S(2)}) collective-permute-start(bf16[256,512]{1,0:T(8,128)(2,1)S(1)} %bitcast.185), channel_id=1, source_target_pairs={{0,4},{4,0},{1,5},{5,1},{2,6},{6,2},{3,7},{7,3},{8,12},{12,8},{9,1... | collective-permute-start | bytes 786440 | tf_op jit(solution)/shard_map/ppermute | solution.py:40
  57.8 23.7 %collective-permute-start.13 = (bf16[2,288,512]{2,1,0:T(8,128)(2,1)}, bf16[2,288,512]{2,1,0:T(8,128)(2,1)S(1)}, u32[]{:S(2)}, u32[]{:S(2)}) collective-permute-start(bf16[2,288,512]{2,1,0:T(8,128)(2,1)} %pad_maximum_fusion.22), channel_id=1, source_target_pairs={{0,1},{1,0},{2,3},{3,2},{4,5},{5,4},{6,7},{7,6},{8,9},{9,8},{10,11... | collective-permute-start | bytes 1769480 | tf_op jit(solution)/shard_map/ppermute | solution.py:45
  64.1 24.5 %collective-permute-start.18 = (bf16[512,1024]{1,0:T(8,128)(2,1)}, bf16[512,1024]{1,0:T(8,128)(2,1)}, u32[]{:S(2)}, u32[]{:S(2)}) collective-permute-start(bf16[512,1024]{1,0:T(8,128)(2,1)} %pad_maximum_fusion.18), channel_id=1, source_target_pairs={{0,16},{8,24},{16,0},{24,8},{1,17},{9,25},{17,1},{25,9},{2,18},{10... | collective-permute-start | bytes 3145736 | tf_op jit(solution)/shard_map/ppermute | solution.py:28
  83.4 33.5 %collective-permute-start.15 = (bf16[2,288,512]{2,1,0:T(8,128)(2,1)S(1)}, bf16[2,288,512]{2,1,0:T(8,128)(2,1)S(1)}, u32[]{:S(2)}, u32[]{:S(2)}) collective-permute-start(bf16[2,288,512]{2,1,0:T(8,128)(2,1)S(1)} %pad_maximum_fusion.23), channel_id=1, source_target_pairs={{0,1},{1,0},{2,3},{3,2},{4,5},{5,4},{6,7},{7,6},{8,9},{9,8},{10,11... | collective-permute-start | bytes 1769480 | tf_op jit(solution)/shard_map/ppermute | solution.py:45
  86.7 30.1 %collective-permute-start.17 = (bf16[1152,512]{1,0:T(8,128)(2,1)S(1)}, bf16[1152,512]{1,0:T(8,128)(2,1)S(1)}, u32[]{:S(2)}, u32[]{:S(2)}) collective-permute-start(bf16[1152,512]{1,0:T(8,128)(2,1)S(1)} %bitcast.176), channel_id=1, source_target_pairs={{0,4},{4,0},{1,5},{5,1},{2,6},{6,2},{3,7},{7,3},{8,12},{12,8},{9,1... | collective-permute-start | bytes 3538952 | tf_op jit(solution)/shard_map/ppermute | solution.py:40
  90.4 26.5 %collective-permute-start.19 = (bf16[2,512,1024]{2,1,0:T(8,128)(2,1)S(1)}, bf16[2,512,1024]{2,1,0:T(8,128)(2,1)S(1)}, u32[]{:S(2)}, u32[]{:S(2)}) collective-permute-start(bf16[2,512,1024]{2,1,0:T(8,128)(2,1)S(1)} %pad_maximum_fusion.4), channel_id=1, source_target_pairs={{0,8},{8,0},{16,24},{24,16},{1,9},{9,1},{17,25},{25,17},{2,10},{10... | collective-permute-start | bytes 6291464 | tf_op jit(solution)/shard_map/ppermute | solution.py:28
  121.1 28.0 %collective-permute-start.25 = (bf16[1152,512]{1,0:T(8,128)(2,1)S(1)}, bf16[1152,512]{1,0:T(8,128)(2,1)S(1)}, u32[]{:S(2)}, u32[]{:S(2)}) collective-permute-start(bf16[1152,512]{1,0:T(8,128)(2,1)S(1)} %bitcast.179), channel_id=1, source_target_pairs={{0,4},{4,0},{1,5},{5,1},{2,6},{6,2},{3,7},{7,3},{8,12},{12,8},{9,1... | collective-permute-start | bytes 3538952 | tf_op jit(solution)/shard_map/ppermute | solution.py:40
  123.0 25.0 %collective-permute-start.23 = (bf16[512,1024]{1,0:T(8,128)(2,1)S(1)}, bf16[512,1024]{1,0:T(8,128)(2,1)S(1)}, u32[]{:S(2)}, u32[]{:S(2)}) collective-permute-start(bf16[512,1024]{1,0:T(8,128)(2,1)S(1)} %fusion.17), channel_id=1, source_target_pairs={{0,16},{8,24},{16,0},{24,8},{1,17},{9,25},{17,1},{25,9},{2,18},{10... | collective-permute-start | bytes 3145736 | tf_op jit(solution)/shard_map/ppermute | solution.py:28
  150.1 24.4 %collective-permute-start.27 = (bf16[512,1024]{1,0:T(8,128)(2,1)S(1)}, bf16[512,1024]{1,0:T(8,128)(2,1)S(1)}, u32[]{:S(2)}, u32[]{:S(2)}) collective-permute-start(bf16[512,1024]{1,0:T(8,128)(2,1)S(1)} %get-tuple-element.551), channel_id=1, source_target_pairs={{0,16},{8,24},{16,0},{24,8},{1,17},{9,25},{17,1},{25,9},{2,18},{10... | collective-permute-start | bytes 3145736 | tf_op jit(solution)/shard_map/ppermute | solution.py:28
  150.7 26.9 %collective-permute-start.26 = (bf16[1152,512]{1,0:T(8,128)(2,1)S(1)}, bf16[1152,512]{1,0:T(8,128)(2,1)S(1)}, u32[]{:S(2)}, u32[]{:S(2)}) collective-permute-start(bf16[1152,512]{1,0:T(8,128)(2,1)S(1)} %bitcast.182), channel_id=1, source_target_pairs={{0,4},{4,0},{1,5},{5,1},{2,6},{6,2},{3,7},{7,3},{8,12},{12,8},{9,1... | collective-permute-start | bytes 3538952 | tf_op jit(solution)/shard_map/ppermute | solution.py:40
  207.6 25.5 %collective-permute-start.30 = (bf16[512,1024]{1,0:T(8,128)(2,1)}, bf16[512,1024]{1,0:T(8,128)(2,1)}, u32[]{:S(2)}, u32[]{:S(2)}) collective-permute-start(bf16[512,1024]{1,0:T(8,128)(2,1)} %fusion.19), channel_id=1, source_target_pairs={{0,16},{8,24},{16,0},{24,8},{1,17},{9,25},{17,1},{25,9},{2,18},{10... | collective-permute-start | bytes 3145736 | tf_op jit(solution)/shard_map/ppermute | solution.py:28
  234.9 34.3 %collective-permute-start.35 = (bf16[512,1024]{1,0:T(8,128)(2,1)S(1)}, bf16[512,1024]{1,0:T(8,128)(2,1)}, u32[]{:S(2)}, u32[]{:S(2)}) collective-permute-start(bf16[512,1024]{1,0:T(8,128)(2,1)S(1)} %get-tuple-element.375), channel_id=1, source_target_pairs={{0,8},{8,0},{16,24},{24,16},{1,9},{9,1},{17,25},{25,17},{2,10},{10... | collective-permute-start | bytes 3145736 | tf_op jit(solution)/shard_map/ppermute | solution.py:28
  235.4 33.7 %collective-permute-start.36 = (bf16[512,1024]{1,0:T(8,128)(2,1)S(1)}, bf16[512,1024]{1,0:T(8,128)(2,1)}, u32[]{:S(2)}, u32[]{:S(2)}) collective-permute-start(bf16[512,1024]{1,0:T(8,128)(2,1)S(1)} %get-tuple-element.376), channel_id=1, source_target_pairs={{0,8},{8,0},{16,24},{24,16},{1,9},{9,1},{17,25},{25,17},{2,10},{10... | collective-permute-start | bytes 3145736 | tf_op jit(solution)/shard_map/ppermute | solution.py:28
  237.2 32.0 %collective-permute-start.34 = (bf16[512,1024]{1,0:T(8,128)(2,1)}, bf16[512,1024]{1,0:T(8,128)(2,1)S(1)}, u32[]{:S(2)}, u32[]{:S(2)}) collective-permute-start(bf16[512,1024]{1,0:T(8,128)(2,1)} %fusion.20), channel_id=1, source_target_pairs={{0,16},{8,24},{16,0},{24,8},{1,17},{9,25},{17,1},{25,9},{2,18},{10... | collective-permute-start | bytes 3145736 | tf_op jit(solution)/shard_map/ppermute | solution.py:28
  253.1 34.0 %collective-permute-start.33 = (bf16[1,576,1024]{2,1,0:T(8,128)(2,1)}, bf16[1,576,1024]{2,1,0:T(8,128)(2,1)}, u32[]{:S(2)}, u32[]{:S(2)}) collective-permute-start(bf16[1,576,1024]{2,1,0:T(8,128)(2,1)} %fusion.21), channel_id=1, source_target_pairs={{0,1},{1,0},{2,3},{3,2},{4,5},{5,4},{6,7},{7,6},{8,9},{9,8},{10,11... | collective-permute-start | bytes 3538952 | tf_op jit(solution)/shard_map/ppermute | solution.py:45
  259.4 27.7 %collective-permute-start.32 = (bf16[1152,512]{1,0:T(8,128)(2,1)S(1)}, bf16[1152,512]{1,0:T(8,128)(2,1)}, u32[]{:S(2)}, u32[]{:S(2)}) collective-permute-start(bf16[1152,512]{1,0:T(8,128)(2,1)S(1)} %get-tuple-element.368), channel_id=1, source_target_pairs={{0,4},{4,0},{1,5},{5,1},{2,6},{6,2},{3,7},{7,3},{8,12},{12,8},{9,1... | collective-permute-start | bytes 3538952 | tf_op jit(solution)/shard_map/ppermute | solution.py:40
  306.0 32.8 %collective-permute-start.39 = (bf16[512,1024]{1,0:T(8,128)(2,1)}, bf16[512,1024]{1,0:T(8,128)(2,1)}, u32[]{:S(2)}, u32[]{:S(2)}) collective-permute-start(bf16[512,1024]{1,0:T(8,128)(2,1)} %get-tuple-element.407), channel_id=1, source_target_pairs={{0,8},{8,0},{16,24},{24,16},{1,9},{9,1},{17,25},{25,17},{2,10},{10... | collective-permute-start | bytes 3145736 | tf_op jit(solution)/shard_map/ppermute | solution.py:28
  306.2 32.5 %collective-permute-start.40 = (bf16[512,1024]{1,0:T(8,128)(2,1)}, bf16[512,1024]{1,0:T(8,128)(2,1)}, u32[]{:S(2)}, u32[]{:S(2)}) collective-permute-start(bf16[512,1024]{1,0:T(8,128)(2,1)} %add_convert_fusion.2), channel_id=1, source_target_pairs={{0,16},{8,24},{16,0},{24,8},{1,17},{9,25},{17,1},{25,9},{2,18},{10... | collective-permute-start | bytes 3145736 | tf_op jit(solution)/shard_map/ppermute | solution.py:28
  306.7 31.9 %collective-permute-start.41 = (bf16[1152,512]{1,0:T(8,128)(2,1)}, bf16[1152,512]{1,0:T(8,128)(2,1)}, u32[]{:S(2)}, u32[]{:S(2)}) collective-permute-start(bf16[1152,512]{1,0:T(8,128)(2,1)} %get-tuple-element.409), channel_id=1, source_target_pairs={{0,4},{4,0},{1,5},{5,1},{2,6},{6,2},{3,7},{7,3},{8,12},{12,8},{9,1... | collective-permute-start | bytes 3538952 | tf_op jit(solution)/shard_map/ppermute | solution.py:40
  308.1 26.5 %collective-permute-start.42 = (bf16[1,576,512]{2,1,0:T(8,128)(2,1)}, bf16[1,576,512]{2,1,0:T(8,128)(2,1)}, u32[]{:S(2)}, u32[]{:S(2)}) collective-permute-start(bf16[1,576,512]{2,1,0:T(8,128)(2,1)} %fusion.27), channel_id=1, source_target_pairs={{0,1},{1,0},{2,3},{3,2},{4,5},{5,4},{6,7},{7,6},{8,9},{9,8},{10,11... | collective-permute-start | bytes 1769480 | tf_op jit(solution)/shard_map/ppermute | solution.py:45
  309.8 28.8 %collective-permute-start.43 = (bf16[1,288,1024]{2,1,0:T(8,128)(2,1)}, bf16[1,288,1024]{2,1,0:T(8,128)(2,1)}, u32[]{:S(2)}, u32[]{:S(2)}) collective-permute-start(bf16[1,288,1024]{2,1,0:T(8,128)(2,1)} %slice.560), channel_id=1, source_target_pairs={{0,2},{1,3},{2,0},{3,1},{4,6},{5,7},{6,4},{7,5},{8,10},{9,11},{10,... | collective-permute-start | bytes 1769480 | tf_op jit(solution)/shard_map/ppermute | solution.py:45
  344.1 26.3 %collective-permute-start.46 = (bf16[512,1024]{1,0:T(8,128)(2,1)S(1)}, bf16[512,1024]{1,0:T(8,128)(2,1)S(1)}, u32[]{:S(2)}, u32[]{:S(2)}) collective-permute-start(bf16[512,1024]{1,0:T(8,128)(2,1)S(1)} %add_convert_fusion.1), channel_id=1, source_target_pairs={{0,16},{8,24},{16,0},{24,8},{1,17},{9,25},{17,1},{25,9},{2,18},{10... | collective-permute-start | bytes 3145736 | tf_op jit(solution)/shard_map/ppermute | solution.py:28
  345.6 24.7 %collective-permute-start.47 = (bf16[1024,512]{1,0:T(8,128)(2,1)}, bf16[1024,512]{1,0:T(8,128)(2,1)S(1)}, u32[]{:S(2)}, u32[]{:S(2)}) collective-permute-start(bf16[1024,512]{1,0:T(8,128)(2,1)} %pad_maximum_fusion.19), channel_id=1, source_target_pairs={{0,4},{4,0},{1,5},{5,1},{2,6},{6,2},{3,7},{7,3},{8,12},{12,8},{9,1... | collective-permute-start | bytes 3145736 | tf_op jit(solution)/shard_map/ppermute | solution.py:40
  (123 other events, 1063.4 us)

commit v6 on v5

--- a/solution.py
+++ b/solution.py
@@ -96,7 +96,7 @@
 
 
 def col_add(kept, received):
-    total = kept + wide(received)
+    total = wide(kept) + wide(received)
     rows = total.shape[1] // 2
     return narrow(total[:, rows:]), total[:, :rows]
 
@@ -316,6 +316,25 @@
     sent[...] = narrow(total[:, half:])
 
 
+def whole_weight_kernel(left_near, left_far, right_near, right_far, out):
+    out[...] = narrow(dot_tn(left_near[...], right_near[...]) + dot_tn(left_far[...], right_far[...]))
+
+
+def whole_weight_grads(lefts, rights, tile):
+    tokens, columns = lefts[0].shape
+    width = rights[0].shape[1]
+    left_spec = pl.BlockSpec((tokens, tile), lambda i: (0, i))
+    return pl.pallas_call(
+        whole_weight_kernel,
+        grid=(columns // tile,),
+        in_specs=[left_spec, left_spec, whole(rights[0]), whole(rights[1])],
+        out_specs=pl.BlockSpec((tile, width), lambda i: (i, 0)),
+        out_shape=jax.ShapeDtypeStruct((columns, width), jnp.bfloat16),
+        compiler_params=pltpu.CompilerParams(vmem_limit_bytes=28 * 2**20),
+        cost_estimate=COST,
+    )(*lefts, *rights)
+
+
 def weight_grads(lefts, rights, tile):
     tokens, columns = lefts[0].shape
     half = rights[0].shape[1] // 2
@@ -335,28 +354,28 @@
     )(*lefts, *rights)
 
 
-def assemble_kernel(turned, place, own, far, pair, out, rows):
+def assemble_kernel(turned, place, own, far, core_own, core_far, out, rows):
     count = own.shape[0]
-    for distance, block in enumerate((own[...], pair[0], far[...], pair[1])):
+    for distance, block in enumerate((own[...], core_own[...], far[...], core_far[...])):
         start = pl.multiple_of((place[0] ^ distance) * count, 16)
         rows[pl.ds(start, count), :] = wide(block)
     out[...] = rows[...].T if turned else rows[...]
 
 
-def assemble(own, far, pair, turned):
+def assemble(own, far, core_own, core_far, turned):
     count, half = own.shape
     shape = (half, TEAM * count) if turned else (TEAM * count, half)
     place = (lax.axis_index("dp") % TEAM).astype(jnp.int32).reshape(1)
     vmem = pl.BlockSpec(memory_space=pltpu.VMEM)
     return pl.pallas_call(
         functools.partial(assemble_kernel, turned),
-        in_specs=[pl.BlockSpec(memory_space=pltpu.SMEM), vmem, vmem, vmem],
+        in_specs=[pl.BlockSpec(memory_space=pltpu.SMEM)] + [vmem] * 4,
         out_specs=vmem,
         out_shape=jax.ShapeDtypeStruct(shape, jnp.float32),
         scratch_shapes=[pltpu.VMEM((TEAM * count, half), jnp.float32)],
         compiler_params=pltpu.CompilerParams(vmem_limit_bytes=16 * 2**20),
         cost_estimate=COST,
-    )(place, own, far, pair)
+    )(place, own, far, core_own, core_far)
 
 
 def body(
@@ -551,8 +570,7 @@
     far_send, grad_gate, grad_up, act = meet(narrow(wide(far_own) + wide(far_moved)), grad_gate, grad_up, act)
     back_from_far = over_x(far_send)
     near_out_moved, far_out_moved = over_core(near_out_sent), over_core(far_out_sent)
-    down_own, down_sent = weight_grads(act, cotangents, units // 3)
-    down_sent, down_kept = col_send(jnp.concatenate([down_own, wide(down_sent)], axis=1), 1)
+    down_sent, down_kept = col_send(whole_weight_grads(act, cotangents, units // 3), 1)
     down_moved = col_swap(down_sent, 1)
     down_sent, grad_gate, grad_up = meet(down_sent, grad_gate, grad_up)
     gate_own, gate_sent = weight_grads(grad_gate, normed_two, units // 3)
@@ -685,29 +703,26 @@
     mixer_moved = col_swap(mixer_sent, 2)
     up_total = team_first(col_last(up_kept, up_moved))
     down_total = team_first(down_own + wide(down_from_row))
-    both = jnp.stack([up_total, down_total])
-    both_far = over_x(both)
+    up_far, down_far = over_x(up_total), over_x(down_total)
     input_row = over_row(narrow(input_grad[:, half:]))
-    gate_pair = over_core(jnp.stack([gate_total, gate_far]))
     small_moved = over_core(small)
-    gate_grad = assemble(gate_total, gate_far, gate_pair, True)
+    gate_grad = assemble(gate_total, gate_far, over_core(gate_total), over_core(gate_far), True)
     small = other_teams(small + small_moved)
     conv_grad = small[2 * half :].reshape(TEAM, 3, channels).transpose(1, 0, 2).reshape(3, TEAM * channels)
-    mixer_moved, both_far, gate_grad, result, conv_grad, input_row = meet(
-        mixer_moved, both_far, gate_grad, result, conv_grad, input_row
+    mixer_moved, up_far, down_far, gate_grad, result, conv_grad, input_row = meet(
+        mixer_moved, up_far, down_far, gate_grad, result, conv_grad, input_row
     )
     mixer_total = team_first(col_last(mixer_kept, mixer_moved))
-    mixer_total, both_far = meet(mixer_total, both_far)
+    mixer_total, up_far, down_far, result = meet(mixer_total, up_far, down_far, result)
     mixer_far = over_x(mixer_total)
-    both_pair = over_core(jnp.stack([both, both_far]))
-    up_grad = assemble(up_total, both_far[0], both_pair[:, 0], True)
+    mixer_core = over_core(mixer_total)
     result_row = over_row(result[:, half:])
-    mixer_far, up_grad, both_pair, input_grad = meet(
-        mixer_far, up_grad, both_pair, to_blocks(input_grad[:, :half], input_row)
-    )
-    mixer_pair = over_core(jnp.stack([mixer_total, mixer_far]))
-    down_grad = assemble(down_total, both_far[1], both_pair[:, 1], False)
-    mixer_grads = team_rows(mixer_total, mixer_far, mixer_pair, 4)
+    up_grad = assemble(up_total, up_far, over_core(up_total), over_core(up_far), True)
+    mixer_far, mixer_core, up_grad, input_grad = meet(
+        mixer_far, mixer_core, up_grad, to_blocks(input_grad[:, :half], input_row)
+    )
+    mixer_grads = team_rows(mixer_total, mixer_far, (mixer_core, over_core(mixer_far)), 4)
+    down_grad = assemble(down_total, down_far, over_core(down_total), over_core(down_far), False)
     in_grad = wide(mixer_grads[:3].transpose(2, 0, 1))
     out_grad = wide(mixer_grads[3])
     return (

time: 443 us -> 437 us (0.986)
  other arithmetic: 76.6 us -> 64.2 us
  waiting for transfers between devices: 152 us -> 157 us
    unnamed x166 -> x182, local copies, waits for them, and re-layouts: 17 us -> 25.2 us
    pallas_call x5 -> x4, Pallas kernels: 24.3 us -> 18.3 us  [weight_grads(): pl.pallas_call(weight_kernel, grid=(columns // tile,), in_specs=[left_spe...]
    pallas_call x0 -> x1, Pallas kernels: none -> 5.97 us  [whole_weight_grads(): pl.pallas_call(whole_weight_kernel, grid=(columns // tile,), in_specs=[le...]
    another operation x4 -> x0, other arithmetic: 5.29 us -> none  [the longest x2 3.42 us: body(): both_pair = over_core(jnp.stack([both, both_far]))]
    ppermute x31 -> x37, waiting for transfers between devices: 50.2 us -> 54.4 us  [over_dp(): return lax.ppermute(values, 'dp', [(i, i ^ distance) for i in range(size)])]
    ppermute x31 -> x37, starting transfers between devices: 17 us -> 18.2 us  [over_dp(): return lax.ppermute(values, 'dp', [(i, i ^ distance) for i in range(size)])]
  transfers between devices with their start and end apart: 66 -> 72, of which waited for: 35 -> 35; matrix products, arithmetic and copies ran while one was open for 21% -> 18% of each run, Pallas kernels for 14% -> 15%
where the time goes in v6:
time: 437 us; the launch traced here: 432 us
  waiting for transfers between devices  157 us (36%)
  Pallas kernels  88.3 us (20%)
  starting transfers between devices  65.8 us (15%)
  other arithmetic  64.2 us (15%)
  local copies, waits for them, and re-layouts  49.9 us (11%)
    ppermute x18, waiting for transfers between devices, col_swap(): return lax.ppermute(values, 'col', [(i, i ^ distance) for i in range(size)])  75.4 us
    ppermute x37, waiting for transfers between devices, over_dp(): return lax.ppermute(values, 'dp', [(i, i ^ distance) for i in range(size)])  54.4 us
    pallas_call x2, Pallas kernels, gated_call(): pl.pallas_call(gated_kernel, grid=(steps,), in_specs=[row_tiles(normed),...  38.4 us
    ppermute x17, waiting for transfers between devices, over_row(): return lax.ppermute(values, 'row', [(0, 1), (1, 0)])  27.5 us
    ppermute x18, starting transfers between devices, col_swap(): return lax.ppermute(values, 'col', [(i, i ^ distance) for i in range(size)])  26.1 us
    unnamed x182, local copies, waits for them, and re-layouts  25.2 us
    ppermute x17, starting transfers between devices, over_row(): return lax.ppermute(values, 'row', [(0, 1), (1, 0)])  21.5 us
    pallas_call x4, Pallas kernels, weight_grads(): pl.pallas_call(weight_kernel, grid=(columns // tile,), in_specs=[left_spe...  18.3 us
  transfers between devices with their start and end apart: 72, of which 35 were waited for; matrix products, arithmetic and copies ran while one was open for 18% of the time, Pallas kernels for 15%

profile of v6, /device:TPU:0, one launch (start us, length us, event | category | flops | bytes accessed | tf_op | source)
XLA Modules:
  0.0 431.6 jit_solution(3734972464084610372)
XLA Ops:
  5.9 4.0 collective-permute-start
  33.9 11.4 %collective-permute-done.8 = bf16[288,512]{1,0:T(8,128)(2,1)S(1)} collective-permute-done((bf16[288,512]{1,0:T(8,128)(2,1)S(1)}, bf16[288,512]{1,0:T(8,128)(2,1)S(1)}, u32[]{:S(2)}, u32[]{:S(2)}) %collective-permute-start.8) | collective-permute-done | bytes 294944 | tf_op jit(solution)/shard_map/ppermute | solution.py:45
  69.2 10.8 %collective-permute-done.14 = bf16[288,512]{1,0:T(8,128)(2,1)} collective-permute-done((bf16[288,512]{1,0:T(8,128)(2,1)}, bf16[288,512]{1,0:T(8,128)(2,1)}, u32[]{:S(2)}, u32[]{:S(2)}) %collective-permute-start.14) | collective-permute-done | bytes 294944 | tf_op jit(solution)/shard_map/ppermute | solution.py:45
  108.7 5.2 %collective-permute-done.20 = f32[2,2,2,256]{3,2,1,0:T(2,128)S(1)} collective-permute-done((f32[2,2,2,256]{3,2,1,0:T(2,128)S(1)}, f32[2,2,2,256]{3,2,1,0:T(2,128)S(1)}, u32[]{:S(2)}, u32[]{:S(2)}) %collective-permute-start.20) | collective-permute-done | bytes 8224 | tf_op jit(solution)/shard_map/ppermute | solution.py:40
  124.7 14.5 %collective-permute-done.24 = bf16[2,288,512]{2,1,0:T(8,128)(2,1)S(1)} collective-permute-done((bf16[2,288,512]{2,1,0:T(8,128)(2,1)S(1)}, bf16[2,288,512]{2,1,0:T(8,128)(2,1)S(1)}, u32[]{:S(2)}, u32[]{:S(2)}) %collective-permute-start.24) | collective-permute-done | bytes 589856 | tf_op jit(solution)/shard_map/ppermute | solution.py:45
  139.2 9.6 %collective-permute-done.23 = bf16[512,1024]{1,0:T(8,128)(2,1)S(1)} collective-permute-done((bf16[512,1024]{1,0:T(8,128)(2,1)S(1)}, bf16[512,1024]{1,0:T(8,128)(2,1)S(1)}, u32[]{:S(2)}, u32[]{:S(2)}) %collective-permute-start.23) | collective-permute-done | bytes 1048608 | tf_op jit(solution)/shard_map/ppermute | solution.py:28
  153.3 22.1 %collective-permute-done.27 = bf16[512,1024]{1,0:T(8,128)(2,1)S(1)} collective-permute-done((bf16[512,1024]{1,0:T(8,128)(2,1)S(1)}, bf16[512,1024]{1,0:T(8,128)(2,1)S(1)}, u32[]{:S(2)}, u32[]{:S(2)}) %collective-permute-start.27) | collective-permute-done | bytes 1048608 | tf_op jit(solution)/shard_map/ppermute | solution.py:28
  178.7 4.1 collective-permute-done.28
  183.2 19.1 %shard_map.190 = (bf16[1024,1152]{1,0:T(8,128)(2,1)S(1)}, bf16[1024,1152]{1,0:T(8,128)(2,1)}, bf16[1024,1152]{1,0:T(8,128)(2,1)}, bf16[512,1024]{1,0:T(8,128)(2,...) custom-call(bf16[1024,1024]{1,0:T(8,128)(2,1)S(1)} %pad_maximum_fusion.7.normed., ...), custom_call_target="tpu_custom_call" | custom-call | flops 1 | bytes 1 | tf_op jit(solution)/shard_map/pallas_call | solution.py:208
  210.4 19.2 %shard_map.191 = (bf16[1024,1152]{1,0:T(8,128)(2,1)S(1)}, bf16[1024,1152]{1,0:T(8,128)(2,1)}, bf16[1024,1152]{1,0:T(8,128)(2,1)}, bf16[512,1024]{1,0:T(8,128)(2,...) custom-call(bf16[1024,1024]{1,0:T(8,128)(2,1)S(1)} %pad_maximum_fusion.8.normed., ...), custom_call_target="tpu_custom_call" | custom-call | flops 1 | bytes 1 | tf_op jit(solution)/shard_map/pallas_call | solution.py:208
  229.7 4.8 %collective-permute-done.30 = bf16[512,1024]{1,0:T(8,128)(2,1)} collective-permute-done((bf16[512,1024]{1,0:T(8,128)(2,1)}, bf16[512,1024]{1,0:T(8,128)(2,1)}, u32[]{:S(2)}, u32[]{:S(2)}) %collective-permute-start.30) | collective-permute-done | bytes 1048608 | tf_op jit(solution)/shard_map/ppermute | solution.py:28
  243.9 6.0 %shard_map.192 = bf16[1152,1024]{1,0:T(8,128)(2,1)S(1)} custom-call(bf16[1024,1152]{1,0:T(8,128)(2,1)S(1)} %copy-done.19, bf16[1024,1152]{1,0:T(8,128)(2,1)S(1)} %copy-done.23, bf16[1024,1024]{1,0:T(8,128)(2,1)S(1)} %pad_maximum_fusion.4.cotangent.right_near, bf16[1024,1024]{1,0:T(8,128)(2,1)S(1)} %pad_maximum_fusion.5.cotangent.right_far), custom_call_target="tpu_custom_call" | custom-call | flops 1 | bytes 1 | tf_op jit(solution)/shard_map/pallas_call | solution.py:327
  252.0 6.0 %shard_map.193 = (f32[1152,512]{1,0:T(8,128)S(1)}, bf16[1152,512]{1,0:T(8,128)(2,1)S(1)}) custom-call(bf16[1024,1152]{1,0:T(8,128)(2,1)S(1)} %copy-done.17, bf16[1024,1152]{1,0:T(8,128)(2,1)S(1)} %copy-done.21, bf16[1024,1024]{1,0:T(8,128)(2,1)S(1)} %pad_maximum_fusion.7.normed.right_near, bf16[1024,1024]{1,0:T(8,128)(2,1)S(1)} %pad_maximum_fusion.8.normed.right_far), custom_call_target="tpu_custom_call" | custom-call | flops 1 | bytes 1 | tf_op jit(solution)/shard_map/pallas_call | solution.py:343
  259.6 6.7 %shard_map.194 = (f32[1152,512]{1,0:T(8,128)S(1)}, bf16[1152,512]{1,0:T(8,128)(2,1)}) custom-call(bf16[1024,1152]{1,0:T(8,128)(2,1)S(1)} %copy-done.16, bf16[1024,1152]{1,0:T(8,128)(2,1)S(1)} %copy-done.20, bf16[1024,1024]{1,0:T(8,128)(2,1)S(1)} %pad_maximum_fusion.7.normed.right_near, bf16[1024,1024]{1,0:T(8,128)(2,1)S(1)} %pad_maximum_fusion.8.normed.right_far), custom_call_target="tpu_custom_call" | custom-call | flops 1 | bytes 1 | tf_op jit(solution)/shard_map/pallas_call | solution.py:343
  270.4 4.5 %fusion.68 = (bf16[512,1024]{1,0:T(8,128)(2,1)S(1)}, f32[512,1024]{1,0:T(8,128)}, bf16[512,1024]{1,0:T(8,128)(2,1)S(1)}) fusion(f32[512]{0:T(512)S(1)} %get-tuple-element.533, f32[512,1024]{1,0:T(8,128)S(1)} %copy-done.45, f32[512]{0:T(512)S(1)} %get-tuple-element.597, f32[512]{0:T(512)S(1)} %get-tuple-element.598, f32[1024]{0:T(1024)S(1)} %bitcast.212, ...), kind=kLoop, calls=%fused_computation.249 | loop fusion | flops 13631488 | bytes 16793600 | tf_op jit(solution)/shard_map/convert_element_type | solution.py:49
  274.9 11.0 %collective-permute-done.32 = bf16[1152,512]{1,0:T(8,128)(2,1)} collective-permute-done((bf16[1152,512]{1,0:T(8,128)(2,1)S(1)}, bf16[1152,512]{1,0:T(8,128)(2,1)}, u32[]{:S(2)}, u32[]{:S(2)}) %collective-permute-start.32) | collective-permute-done | bytes 1179680 | tf_op jit(solution)/shard_map/ppermute | solution.py:40
  300.8 5.8 %shard_map.195 = (bf16[1024,768]{1,0:T(8,128)(2,1)S(1)}, f32[2,3,256]{2,1,0:T(4,128)S(1)}, bf16[512,1024]{1,0:T(8,128)(2,1)S(1)}, bf16[512,1024]{1,0:T(8,128)(2,1)}) custom-call(bf16[1024,1024]{1,0:T(8,128)(2,1)S(1)} %pad_maximum_fusion.11.grad_mixed.right_far, f32[1024,768]{1,0:T(8,128)S(1)} %copy-done.5, f32[1024,4]{1,0:T(8,128)S(1)} %bitcast.180, ...), custom_call_target="tpu_custom_call" | custom-call | flops 1 | bytes 1 | tf_op jit(solution)/shard_map/pallas_call | solution.py:301
  310.3 4.8 %shard_map.196 = (bf16[1024,768]{1,0:T(8,128)(2,1)S(1)}, f32[2,3,256]{2,1,0:T(4,128)S(1)}, bf16[512,1024]{1,0:T(8,128)(2,1)S(1)}, bf16[512,1024]{1,0:T(8,128)(2,1)S(1)}) custom-call(bf16[1024,1024]{1,0:T(8,128)(2,1)S(1)} %pad_maximum_fusion.10.grad_mixed.right_near, f32[1024,768]{1,0:T(8,128)S(1)} %copy-done.3, f32[1024,4]{1,0:T(8,128)S(1)} %bitcast.178, ...), custom_call_target="tpu_custom_call" | custom-call | flops 1 | bytes 1 | tf_op jit(solution)/shard_map/pallas_call | solution.py:301
  323.3 4.3 %shard_map.197 = (f32[768,512]{1,0:T(8,128)S(1)}, bf16[768,512]{1,0:T(8,128)(2,1)S(1)}) custom-call(bf16[1024,768]{1,0:T(8,128)(2,1)S(1)} %get-tuple-element.397.left_near, bf16[1024,768]{1,0:T(8,128)(2,1)S(1)} %get-tuple-element.398.left_far, bf16[1024,1024]{1,0:T(8,128)(2,1)S(1)} %copy-done.25, bf16[1024,1024]{1,0:T(8,128)(2,1)S(1)} %copy-done.27), custom_call_target="tpu_custom_call" | custom-call | flops 1 | bytes 1 | tf_op jit(solution)/shard_map/pallas_call | solution.py:343
  338.5 3.6 collective-permute-done.45
  357.6 10.2 %collective-permute-done.50 = f32[2816]{0:T(1024)S(1)} collective-permute-done((f32[2816]{0:T(1024)S(1)}, f32[2816]{0:T(1024)S(1)}, u32[]{:S(2)}, u32[]{:S(2)}) %collective-permute-start.50) | collective-permute-done | bytes 11296 | tf_op jit(solution)/shard_map/ppermute | solution.py:45
  383.0 4.0 collective-permute-done.52
  401.3 8.7 %collective-permute-done.57 = bf16[4,64,512]{2,1,0:T(8,128)(2,1)S(1)} collective-permute-done((bf16[4,64,512]{2,1,0:T(8,128)(2,1)S(1)}, bf16[4,64,512]{2,1,0:T(8,128)(2,1)S(1)}, u32[]{:S(2)}, u32[]{:S(2)}) %collective-permute-start.57) | collective-permute-done | bytes 262176 | tf_op jit(solution)/shard_map/ppermute | solution.py:45
  422.3 5.1 %collective-permute-done.64 = bf16[512,512]{1,0:T(8,128)(2,1)S(1)} collective-permute-done((bf16[512,512]{1,0:T(8,128)(2,1)S(1)}, bf16[512,512]{1,0:T(8,128)(2,1)S(1)}, u32[]{:S(2)}, u32[]{:S(2)}) %collective-permute-start.64) | collective-permute-done | bytes 524320 | tf_op jit(solution)/shard_map/ppermute | solution.py:40
  (501 shorter events, 223.1 us)
Async XLA Ops:
  55.6 25.8 %collective-permute-start.11 = (bf16[784,512]{1,0:T(8,128)(2,1)}, bf16[784,512]{1,0:T(8,128)(2,1)}, u32[]{:S(2)}, u32[]{:S(2)}) collective-permute-start(bf16[784,512]{1,0:T(8,128)(2,1)} %pad_maximum_fusion.18), channel_id=1, source_target_pairs={{0,4},{4,0},{1,5},{5,1},{2,6},{6,2},{3,7},{7,3},{8,12},{12,8},{9,1... | collective-permute-start | bytes 2408456 | tf_op jit(solution)/shard_map/ppermute | solution.py:40
  56.7 24.7 %collective-permute-start.12 = (bf16[256,512]{1,0:T(8,128)(2,1)S(1)}, bf16[256,512]{1,0:T(8,128)(2,1)S(1)}, u32[]{:S(2)}, u32[]{:S(2)}) collective-permute-start(bf16[256,512]{1,0:T(8,128)(2,1)S(1)} %bitcast.169), channel_id=1, source_target_pairs={{0,4},{4,0},{1,5},{5,1},{2,6},{6,2},{3,7},{7,3},{8,12},{12,8},{9,1... | collective-permute-start | bytes 786440 | tf_op jit(solution)/shard_map/ppermute | solution.py:40
  57.7 23.7 %collective-permute-start.13 = (bf16[2,288,512]{2,1,0:T(8,128)(2,1)}, bf16[2,288,512]{2,1,0:T(8,128)(2,1)S(1)}, u32[]{:S(2)}, u32[]{:S(2)}) collective-permute-start(bf16[2,288,512]{2,1,0:T(8,128)(2,1)} %pad_maximum_fusion.20), channel_id=1, source_target_pairs={{0,1},{1,0},{2,3},{3,2},{4,5},{5,4},{6,7},{7,6},{8,9},{9,8},{10,11... | collective-permute-start | bytes 1769480 | tf_op jit(solution)/shard_map/ppermute | solution.py:45
  64.0 24.5 %collective-permute-start.18 = (bf16[512,1024]{1,0:T(8,128)(2,1)}, bf16[512,1024]{1,0:T(8,128)(2,1)}, u32[]{:S(2)}, u32[]{:S(2)}) collective-permute-start(bf16[512,1024]{1,0:T(8,128)(2,1)} %pad_maximum_fusion.16), channel_id=1, source_target_pairs={{0,16},{8,24},{16,0},{24,8},{1,17},{9,25},{17,1},{25,9},{2,18},{10... | collective-permute-start | bytes 3145736 | tf_op jit(solution)/shard_map/ppermute | solution.py:28
  83.3 34.2 %collective-permute-start.15 = (bf16[2,288,512]{2,1,0:T(8,128)(2,1)S(1)}, bf16[2,288,512]{2,1,0:T(8,128)(2,1)S(1)}, u32[]{:S(2)}, u32[]{:S(2)}) collective-permute-start(bf16[2,288,512]{2,1,0:T(8,128)(2,1)S(1)} %pad_maximum_fusion.21), channel_id=1, source_target_pairs={{0,1},{1,0},{2,3},{3,2},{4,5},{5,4},{6,7},{7,6},{8,9},{9,8},{10,11... | collective-permute-start | bytes 1769480 | tf_op jit(solution)/shard_map/ppermute | solution.py:45
  86.7 30.9 %collective-permute-start.17 = (bf16[1152,512]{1,0:T(8,128)(2,1)S(1)}, bf16[1152,512]{1,0:T(8,128)(2,1)S(1)}, u32[]{:S(2)}, u32[]{:S(2)}) collective-permute-start(bf16[1152,512]{1,0:T(8,128)(2,1)S(1)} %bitcast.160), channel_id=1, source_target_pairs={{0,4},{4,0},{1,5},{5,1},{2,6},{6,2},{3,7},{7,3},{8,12},{12,8},{9,1... | collective-permute-start | bytes 3538952 | tf_op jit(solution)/shard_map/ppermute | solution.py:40
  90.4 27.2 %collective-permute-start.19 = (bf16[2,512,1024]{2,1,0:T(8,128)(2,1)S(1)}, bf16[2,512,1024]{2,1,0:T(8,128)(2,1)S(1)}, u32[]{:S(2)}, u32[]{:S(2)}) collective-permute-start(bf16[2,512,1024]{2,1,0:T(8,128)(2,1)S(1)} %pad_maximum_fusion.3), channel_id=1, source_target_pairs={{0,8},{8,0},{16,24},{24,16},{1,9},{9,1},{17,25},{25,17},{2,10},{10... | collective-permute-start | bytes 6291464 | tf_op jit(solution)/shard_map/ppermute | solution.py:28
  121.9 28.0 %collective-permute-start.25 = (bf16[1152,512]{1,0:T(8,128)(2,1)S(1)}, bf16[1152,512]{1,0:T(8,128)(2,1)S(1)}, u32[]{:S(2)}, u32[]{:S(2)}) collective-permute-start(bf16[1152,512]{1,0:T(8,128)(2,1)S(1)} %bitcast.163), channel_id=1, source_target_pairs={{0,4},{4,0},{1,5},{5,1},{2,6},{6,2},{3,7},{7,3},{8,12},{12,8},{9,1... | collective-permute-start | bytes 3538952 | tf_op jit(solution)/shard_map/ppermute | solution.py:40
  123.8 25.0 %collective-permute-start.23 = (bf16[512,1024]{1,0:T(8,128)(2,1)S(1)}, bf16[512,1024]{1,0:T(8,128)(2,1)S(1)}, u32[]{:S(2)}, u32[]{:S(2)}) collective-permute-start(bf16[512,1024]{1,0:T(8,128)(2,1)S(1)} %fusion.16), channel_id=1, source_target_pairs={{0,16},{8,24},{16,0},{24,8},{1,17},{9,25},{17,1},{25,9},{2,18},{10... | collective-permute-start | bytes 3145736 | tf_op jit(solution)/shard_map/ppermute | solution.py:28
  150.9 24.4 %collective-permute-start.27 = (bf16[512,1024]{1,0:T(8,128)(2,1)S(1)}, bf16[512,1024]{1,0:T(8,128)(2,1)S(1)}, u32[]{:S(2)}, u32[]{:S(2)}) collective-permute-start(bf16[512,1024]{1,0:T(8,128)(2,1)S(1)} %get-tuple-element.553), channel_id=1, source_target_pairs={{0,16},{8,24},{16,0},{24,8},{1,17},{9,25},{17,1},{25,9},{2,18},{10... | collective-permute-start | bytes 3145736 | tf_op jit(solution)/shard_map/ppermute | solution.py:28
  151.5 26.9 %collective-permute-start.26 = (bf16[1152,512]{1,0:T(8,128)(2,1)S(1)}, bf16[1152,512]{1,0:T(8,128)(2,1)S(1)}, u32[]{:S(2)}, u32[]{:S(2)}) collective-permute-start(bf16[1152,512]{1,0:T(8,128)(2,1)S(1)} %bitcast.166), channel_id=1, source_target_pairs={{0,4},{4,0},{1,5},{5,1},{2,6},{6,2},{3,7},{7,3},{8,12},{12,8},{9,1... | collective-permute-start | bytes 3538952 | tf_op jit(solution)/shard_map/ppermute | solution.py:40
  208.9 25.5 %collective-permute-start.30 = (bf16[512,1024]{1,0:T(8,128)(2,1)}, bf16[512,1024]{1,0:T(8,128)(2,1)}, u32[]{:S(2)}, u32[]{:S(2)}) collective-permute-start(bf16[512,1024]{1,0:T(8,128)(2,1)} %fusion.18), channel_id=1, source_target_pairs={{0,16},{8,24},{16,0},{24,8},{1,17},{9,25},{17,1},{25,9},{2,18},{10... | collective-permute-start | bytes 3145736 | tf_op jit(solution)/shard_map/ppermute | solution.py:28
  234.5 33.2 %collective-permute-start.35 = (bf16[512,1024]{1,0:T(8,128)(2,1)}, bf16[512,1024]{1,0:T(8,128)(2,1)}, u32[]{:S(2)}, u32[]{:S(2)}) collective-permute-start(bf16[512,1024]{1,0:T(8,128)(2,1)} %copy-done.43), channel_id=1, source_target_pairs={{0,8},{8,0},{16,24},{24,16},{1,9},{9,1},{17,25},{25,17},{2,10},{10... | collective-permute-start | bytes 3145736 | tf_op jit(solution)/shard_map/ppermute | solution.py:28
  235.1 32.7 %collective-permute-start.36 = (bf16[512,1024]{1,0:T(8,128)(2,1)S(1)}, bf16[512,1024]{1,0:T(8,128)(2,1)}, u32[]{:S(2)}, u32[]{:S(2)}) collective-permute-start(bf16[512,1024]{1,0:T(8,128)(2,1)S(1)} %get-tuple-element.375), channel_id=1, source_target_pairs={{0,8},{8,0},{16,24},{24,16},{1,9},{9,1},{17,25},{25,17},{2,10},{10... | collective-permute-start | bytes 3145736 | tf_op jit(solution)/shard_map/ppermute | solution.py:28
  239.1 28.6 %collective-permute-start.34 = (bf16[512,1024]{1,0:T(8,128)(2,1)}, bf16[512,1024]{1,0:T(8,128)(2,1)S(1)}, u32[]{:S(2)}, u32[]{:S(2)}) collective-permute-start(bf16[512,1024]{1,0:T(8,128)(2,1)} %fusion.19), channel_id=1, source_target_pairs={{0,16},{8,24},{16,0},{24,8},{1,17},{9,25},{17,1},{25,9},{2,18},{10... | collective-permute-start | bytes 3145736 | tf_op jit(solution)/shard_map/ppermute | solution.py:28
  251.0 34.9 %collective-permute-start.33 = (bf16[1,576,1024]{2,1,0:T(8,128)(2,1)}, bf16[1,576,1024]{2,1,0:T(8,128)(2,1)}, u32[]{:S(2)}, u32[]{:S(2)}) collective-permute-start(bf16[1,576,1024]{2,1,0:T(8,128)(2,1)} %slice_bitcast_fusion.3), channel_id=1, source_target_pairs={{0,1},{1,0},{2,3},{3,2},{4,5},{5,4},{6,7},{7,6},{8,9},{9,8},{10,11... | collective-permute-start | bytes 3538952 | tf_op jit(solution)/shard_map/ppermute | solution.py:45
  258.0 27.9 %collective-permute-start.32 = (bf16[1152,512]{1,0:T(8,128)(2,1)S(1)}, bf16[1152,512]{1,0:T(8,128)(2,1)}, u32[]{:S(2)}, u32[]{:S(2)}) collective-permute-start(bf16[1152,512]{1,0:T(8,128)(2,1)S(1)} %get-tuple-element.367), channel_id=1, source_target_pairs={{0,4},{4,0},{1,5},{5,1},{2,6},{6,2},{3,7},{7,3},{8,12},{12,8},{9,1... | collective-permute-start | bytes 3538952 | tf_op jit(solution)/shard_map/ppermute | solution.py:40
  306.6 31.8 %collective-permute-start.39 = (bf16[512,1024]{1,0:T(8,128)(2,1)}, bf16[512,1024]{1,0:T(8,128)(2,1)}, u32[]{:S(2)}, u32[]{:S(2)}) collective-permute-start(bf16[512,1024]{1,0:T(8,128)(2,1)} %get-tuple-element.406), channel_id=1, source_target_pairs={{0,8},{8,0},{16,24},{24,16},{1,9},{9,1},{17,25},{25,17},{2,10},{10... | collective-permute-start | bytes 3145736 | tf_op jit(solution)/shard_map/ppermute | solution.py:28
  306.6 31.6 %collective-permute-start.40 = (bf16[512,1024]{1,0:T(8,128)(2,1)}, bf16[512,1024]{1,0:T(8,128)(2,1)}, u32[]{:S(2)}, u32[]{:S(2)}) collective-permute-start(bf16[512,1024]{1,0:T(8,128)(2,1)} %add_convert_fusion.2), channel_id=1, source_target_pairs={{0,16},{8,24},{16,0},{24,8},{1,17},{9,25},{17,1},{25,9},{2,18},{10... | collective-permute-start | bytes 3145736 | tf_op jit(solution)/shard_map/ppermute | solution.py:28
  307.2 31.1 %collective-permute-start.41 = (bf16[1152,512]{1,0:T(8,128)(2,1)}, bf16[1152,512]{1,0:T(8,128)(2,1)}, u32[]{:S(2)}, u32[]{:S(2)}) collective-permute-start(bf16[1152,512]{1,0:T(8,128)(2,1)} %get-tuple-element.408), channel_id=1, source_target_pairs={{0,4},{4,0},{1,5},{5,1},{2,6},{6,2},{3,7},{7,3},{8,12},{12,8},{9,1... | collective-permute-start | bytes 3538952 | tf_op jit(solution)/shard_map/ppermute | solution.py:40
  308.7 27.1 %collective-permute-start.42 = (bf16[1,576,512]{2,1,0:T(8,128)(2,1)}, bf16[1,576,512]{2,1,0:T(8,128)(2,1)}, u32[]{:S(2)}, u32[]{:S(2)}) collective-permute-start(bf16[1,576,512]{2,1,0:T(8,128)(2,1)} %fusion.25), channel_id=1, source_target_pairs={{0,1},{1,0},{2,3},{3,2},{4,5},{5,4},{6,7},{7,6},{8,9},{9,8},{10,11... | collective-permute-start | bytes 1769480 | tf_op jit(solution)/shard_map/ppermute | solution.py:45
  309.5 28.8 %collective-permute-start.43 = (bf16[1,288,1024]{2,1,0:T(8,128)(2,1)}, bf16[1,288,1024]{2,1,0:T(8,128)(2,1)}, u32[]{:S(2)}, u32[]{:S(2)}) collective-permute-start(bf16[1,288,1024]{2,1,0:T(8,128)(2,1)} %slice.528), channel_id=1, source_target_pairs={{0,2},{1,3},{2,0},{3,1},{4,6},{5,7},{6,4},{7,5},{8,10},{9,11},{10,... | collective-permute-start | bytes 1769480 | tf_op jit(solution)/shard_map/ppermute | solution.py:45
  343.8 26.3 %collective-permute-start.46 = (bf16[512,1024]{1,0:T(8,128)(2,1)S(1)}, bf16[512,1024]{1,0:T(8,128)(2,1)S(1)}, u32[]{:S(2)}, u32[]{:S(2)}) collective-permute-start(bf16[512,1024]{1,0:T(8,128)(2,1)S(1)} %add_convert_fusion.1), channel_id=1, source_target_pairs={{0,16},{8,24},{16,0},{24,8},{1,17},{9,25},{17,1},{25,9},{2,18},{10... | collective-permute-start | bytes 3145736 | tf_op jit(solution)/shard_map/ppermute | solution.py:28
  345.3 24.7 %collective-permute-start.47 = (bf16[1024,512]{1,0:T(8,128)(2,1)}, bf16[1024,512]{1,0:T(8,128)(2,1)S(1)}, u32[]{:S(2)}, u32[]{:S(2)}) collective-permute-start(bf16[1024,512]{1,0:T(8,128)(2,1)} %pad_maximum_fusion.17), channel_id=1, source_target_pairs={{0,4},{4,0},{1,5},{5,1},{2,6},{6,2},{3,7},{7,3},{8,12},{12,8},{9,1... | collective-permute-start | bytes 3145736 | tf_op jit(solution)/shard_map/ppermute | solution.py:40
  (137 other events, 1261.3 us)

commit v7 on v6

--- a/solution.py
+++ b/solution.py
@@ -211,7 +211,7 @@
         in_specs=[row_tiles(normed), row_tiles(cotangent)] + [whole(one) for one in weights],
         out_specs=[row_tiles(wide_out)] * 3 + [own, sent] * 2,
         out_shape=[wide_out] * 3 + [part_out] * 4,
-        compiler_params=pltpu.CompilerParams(vmem_limit_bytes=36 * 2**20),
+        compiler_params=pltpu.CompilerParams(vmem_limit_bytes=32 * 2**20),
         cost_estimate=COST,
     )(normed, cotangent, *weights)
 
@@ -330,7 +330,7 @@
         in_specs=[left_spec, left_spec, whole(rights[0]), whole(rights[1])],
         out_specs=pl.BlockSpec((tile, width), lambda i: (i, 0)),
         out_shape=jax.ShapeDtypeStruct((columns, width), jnp.bfloat16),
-        compiler_params=pltpu.CompilerParams(vmem_limit_bytes=28 * 2**20),
+        compiler_params=pltpu.CompilerParams(vmem_limit_bytes=22 * 2**20),
         cost_estimate=COST,
     )(*lefts, *rights)
 
@@ -349,7 +349,7 @@
             jax.ShapeDtypeStruct((columns, half), jnp.float32),
             jax.ShapeDtypeStruct((columns, half), jnp.bfloat16),
         ],
-        compiler_params=pltpu.CompilerParams(vmem_limit_bytes=28 * 2**20),
+        compiler_params=pltpu.CompilerParams(vmem_limit_bytes=22 * 2**20),
         cost_estimate=COST,
     )(*lefts, *rights)
 

time: 437 us -> 433 us (level)
    unnamed x182 -> x186, local copies, waits for them, and re-layouts: 25.2 us -> 27.3 us
  transfers between devices with their start and end apart: 72 -> 72, of which waited for: 35 -> 35; matrix products, arithmetic and copies ran while one was open for 18% -> 17% of each run, Pallas kernels for 15% -> 15%
where the time goes in v7:
time: 433 us; the launch traced here: 427 us
  waiting for transfers between devices  154 us (36%)
  Pallas kernels  86.7 us (20%)
  starting transfers between devices  67.1 us (15%)
  other arithmetic  61.9 us (14%)
  local copies, waits for them, and re-layouts  51 us (12%)
    ppermute x18, waiting for transfers between devices, col_swap(): return lax.ppermute(values, 'col', [(i, i ^ distance) for i in range(size)])  73.9 us
    ppermute x37, waiting for transfers between devices, over_dp(): return lax.ppermute(values, 'dp', [(i, i ^ distance) for i in range(size)])  53.8 us
    pallas_call x2, Pallas kernels, gated_call(): pl.pallas_call(gated_kernel, grid=(steps,), in_specs=[row_tiles(normed),...  36.3 us
    ppermute x18, starting transfers between devices, col_swap(): return lax.ppermute(values, 'col', [(i, i ^ distance) for i in range(size)])  27.3 us
    unnamed x186, local copies, waits for them, and re-layouts  27.3 us
    ppermute x17, waiting for transfers between devices, over_row(): return lax.ppermute(values, 'row', [(0, 1), (1, 0)])  26.1 us
    ppermute x17, starting transfers between devices, over_row(): return lax.ppermute(values, 'row', [(0, 1), (1, 0)])  21.6 us
    pallas_call x4, Pallas kernels, weight_grads(): pl.pallas_call(weight_kernel, grid=(columns // tile,), in_specs=[left_spe...  18.5 us
  transfers between devices with their start and end apart: 72, of which 35 were waited for; matrix products, arithmetic and copies ran while one was open for 17% of the time, Pallas kernels for 15%

profile of v7, /device:TPU:0, one launch (start us, length us, event | category | flops | bytes accessed | tf_op | source)
XLA Modules:
  0.0 426.7 jit_solution(2186124321615690277)
XLA Ops:
  5.9 4.0 collective-permute-start
  33.9 11.4 %collective-permute-done.8 = bf16[288,512]{1,0:T(8,128)(2,1)S(1)} collective-permute-done((bf16[288,512]{1,0:T(8,128)(2,1)S(1)}, bf16[288,512]{1,0:T(8,128)(2,1)S(1)}, u32[]{:S(2)}, u32[]{:S(2)}) %collective-permute-start.8) | collective-permute-done | bytes 294944 | tf_op jit(solution)/shard_map/ppermute | solution.py:45
  69.2 10.9 %collective-permute-done.14 = bf16[288,512]{1,0:T(8,128)(2,1)} collective-permute-done((bf16[288,512]{1,0:T(8,128)(2,1)}, bf16[288,512]{1,0:T(8,128)(2,1)}, u32[]{:S(2)}, u32[]{:S(2)}) %collective-permute-start.14) | collective-permute-done | bytes 294944 | tf_op jit(solution)/shard_map/ppermute | solution.py:45
  108.7 5.3 %collective-permute-done.20 = f32[2,2,2,256]{3,2,1,0:T(2,128)S(1)} collective-permute-done((f32[2,2,2,256]{3,2,1,0:T(2,128)S(1)}, f32[2,2,2,256]{3,2,1,0:T(2,128)S(1)}, u32[]{:S(2)}, u32[]{:S(2)}) %collective-permute-start.20) | collective-permute-done | bytes 8224 | tf_op jit(solution)/shard_map/ppermute | solution.py:40
  124.1 14.5 %collective-permute-done.24 = bf16[2,288,512]{2,1,0:T(8,128)(2,1)S(1)} collective-permute-done((bf16[2,288,512]{2,1,0:T(8,128)(2,1)S(1)}, bf16[2,288,512]{2,1,0:T(8,128)(2,1)S(1)}, u32[]{:S(2)}, u32[]{:S(2)}) %collective-permute-start.24) | collective-permute-done | bytes 589856 | tf_op jit(solution)/shard_map/ppermute | solution.py:45
  138.6 9.6 %collective-permute-done.23 = bf16[512,1024]{1,0:T(8,128)(2,1)S(1)} collective-permute-done((bf16[512,1024]{1,0:T(8,128)(2,1)S(1)}, bf16[512,1024]{1,0:T(8,128)(2,1)S(1)}, u32[]{:S(2)}, u32[]{:S(2)}) %collective-permute-start.23) | collective-permute-done | bytes 1048608 | tf_op jit(solution)/shard_map/ppermute | solution.py:28
  152.6 22.1 %collective-permute-done.27 = bf16[512,1024]{1,0:T(8,128)(2,1)S(1)} collective-permute-done((bf16[512,1024]{1,0:T(8,128)(2,1)S(1)}, bf16[512,1024]{1,0:T(8,128)(2,1)S(1)}, u32[]{:S(2)}, u32[]{:S(2)}) %collective-permute-start.27) | collective-permute-done | bytes 1048608 | tf_op jit(solution)/shard_map/ppermute | solution.py:28
  178.0 4.1 collective-permute-done.28
  182.6 18.1 %shard_map.190 = (bf16[1024,1152]{1,0:T(8,128)(2,1)S(1)}, bf16[1024,1152]{1,0:T(8,128)(2,1)S(1)}, bf16[1024,1152]{1,0:T(8,128)(2,1)S(1)}, bf16[512,1024]{1,0:T(8...) custom-call(bf16[1024,1024]{1,0:T(8,128)(2,1)S(1)} %pad_maximum_fusion.7, ...), custom_call_target="tpu_custom_call" | custom-call | flops 1 | bytes 1 | tf_op jit(solution)/shard_map/pallas_call | solution.py:208
  209.0 18.2 %shard_map.191 = (bf16[1024,1152]{1,0:T(8,128)(2,1)S(1)}, bf16[1024,1152]{1,0:T(8,128)(2,1)S(1)}, bf16[1024,1152]{1,0:T(8,128)(2,1)S(1)}, bf16[512,1024]{1,0:T(8...) custom-call(bf16[1024,1024]{1,0:T(8,128)(2,1)S(1)} %pad_maximum_fusion.8, ...), custom_call_target="tpu_custom_call" | custom-call | flops 1 | bytes 1 | tf_op jit(solution)/shard_map/pallas_call | solution.py:208
  228.7 4.4 %collective-permute-done.30 = bf16[512,1024]{1,0:T(8,128)(2,1)} collective-permute-done((bf16[512,1024]{1,0:T(8,128)(2,1)}, bf16[512,1024]{1,0:T(8,128)(2,1)}, u32[]{:S(2)}, u32[]{:S(2)}) %collective-permute-start.30) | collective-permute-done | bytes 1048608 | tf_op jit(solution)/shard_map/ppermute | solution.py:28
  240.9 6.0 %shard_map.192 = bf16[1152,1024]{1,0:T(8,128)(2,1)S(1)} custom-call(bf16[1024,1152]{1,0:T(8,128)(2,1)S(1)} %copy-done.26, bf16[1024,1152]{1,0:T(8,128)(2,1)S(1)} %get-tuple-element.360.left_far, bf16[1024,1024]{1,0:T(8,128)(2,1)S(1)} %pad_maximum_fusion.4.cotangent.right_near, bf16[1024,1024]{1,0:T(8,128)(2,1)S(1)} %pad_maximum_fusion.5.cotangent.right_far), custom_call_target="tpu_custom_call" | custom-call | flops 1 | bytes 1 | tf_op jit(solution)/shard_map/pallas_call | solution.py:327
  248.6 6.0 %shard_map.193 = (f32[1152,512]{1,0:T(8,128)S(1)}, bf16[1152,512]{1,0:T(8,128)(2,1)S(1)}) custom-call(bf16[1024,1152]{1,0:T(8,128)(2,1)S(1)} %copy-done.24, bf16[1024,1152]{1,0:T(8,128)(2,1)S(1)} %get-tuple-element.366.left_far, bf16[1024,1024]{1,0:T(8,128)(2,1)S(1)} %pad_maximum_fusion.7.normed.right_near, ...), custom_call_target="tpu_custom_call" | custom-call | flops 1 | bytes 1 | tf_op jit(solution)/shard_map/pallas_call | solution.py:343
  256.3 6.8 %shard_map.194 = (f32[1152,512]{1,0:T(8,128)S(1)}, bf16[1152,512]{1,0:T(8,128)(2,1)}) custom-call(bf16[1024,1152]{1,0:T(8,128)(2,1)S(1)} %copy-done.22, bf16[1024,1152]{1,0:T(8,128)(2,1)S(1)} %copy-done.28, bf16[1024,1024]{1,0:T(8,128)(2,1)S(1)} %pad_maximum_fusion.7.normed.right_near, bf16[1024,1024]{1,0:T(8,128)(2,1)S(1)} %pad_maximum_fusion.8.normed.right_far), custom_call_target="tpu_custom_call" | custom-call | flops 1 | bytes 1 | tf_op jit(solution)/shard_map/pallas_call | solution.py:343
  268.6 4.5 %fusion.68 = (bf16[512,1024]{1,0:T(8,128)(2,1)S(1)}, f32[512,1024]{1,0:T(8,128)}, bf16[512,1024]{1,0:T(8,128)(2,1)S(1)}) fusion(f32[512]{0:T(512)S(1)} %get-tuple-element.533, f32[512,1024]{1,0:T(8,128)S(1)} %copy-done.43, f32[512]{0:T(512)S(1)} %get-tuple-element.597, f32[512]{0:T(512)S(1)} %get-tuple-element.598, f32[1024]{0:T(1024)S(1)} %bitcast.212, ...), kind=kLoop, calls=%fused_computation.249 | loop fusion | flops 13631488 | bytes 16793600 | tf_op jit(solution)/shard_map/convert_element_type | solution.py:49
  273.1 9.5 %collective-permute-done.32 = bf16[1152,512]{1,0:T(8,128)(2,1)} collective-permute-done((bf16[1152,512]{1,0:T(8,128)(2,1)S(1)}, bf16[1152,512]{1,0:T(8,128)(2,1)}, u32[]{:S(2)}, u32[]{:S(2)}) %collective-permute-start.32) | collective-permute-done | bytes 1179680 | tf_op jit(solution)/shard_map/ppermute | solution.py:40
  296.3 6.0 %shard_map.195 = (bf16[1024,768]{1,0:T(8,128)(2,1)S(1)}, f32[2,3,256]{2,1,0:T(4,128)S(1)}, bf16[512,1024]{1,0:T(8,128)(2,1)S(1)}, bf16[512,1024]{1,0:T(8,128)(2,1)}) custom-call(bf16[1024,1024]{1,0:T(8,128)(2,1)S(1)} %pad_maximum_fusion.11.grad_mixed.right_far, f32[1024,768]{1,0:T(8,128)S(1)} %copy-done.5, f32[1024,4]{1,0:T(8,128)S(1)} %bitcast.180, ...), custom_call_target="tpu_custom_call" | custom-call | flops 1 | bytes 1 | tf_op jit(solution)/shard_map/pallas_call | solution.py:301
  305.9 4.9 %shard_map.196 = (bf16[1024,768]{1,0:T(8,128)(2,1)S(1)}, f32[2,3,256]{2,1,0:T(4,128)S(1)}, bf16[512,1024]{1,0:T(8,128)(2,1)S(1)}, bf16[512,1024]{1,0:T(8,128)(2,1)S(1)}) custom-call(bf16[1024,1024]{1,0:T(8,128)(2,1)S(1)} %pad_maximum_fusion.10.grad_mixed.right_near, f32[1024,768]{1,0:T(8,128)S(1)} %copy-done.3, f32[1024,4]{1,0:T(8,128)S(1)} %bitcast.178, ...), custom_call_target="tpu_custom_call" | custom-call | flops 1 | bytes 1 | tf_op jit(solution)/shard_map/pallas_call | solution.py:301
  318.7 4.4 %shard_map.197 = (f32[768,512]{1,0:T(8,128)S(1)}, bf16[768,512]{1,0:T(8,128)(2,1)S(1)}) custom-call(bf16[1024,768]{1,0:T(8,128)(2,1)S(1)} %get-tuple-element.397.left_near, bf16[1024,768]{1,0:T(8,128)(2,1)S(1)} %get-tuple-element.398.left_far, bf16[1024,1024]{1,0:T(8,128)(2,1)S(1)} %copy-done.30, bf16[1024,1024]{1,0:T(8,128)(2,1)S(1)} %copy-done.32), custom_call_target="tpu_custom_call" | custom-call | flops 1 | bytes 1 | tf_op jit(solution)/shard_map/pallas_call | solution.py:343
  352.7 10.3 %collective-permute-done.50 = f32[2816]{0:T(1024)S(1)} collective-permute-done((f32[2816]{0:T(1024)S(1)}, f32[2816]{0:T(1024)S(1)}, u32[]{:S(2)}, u32[]{:S(2)}) %collective-permute-start.50) | collective-permute-done | bytes 11296 | tf_op jit(solution)/shard_map/ppermute | solution.py:45
  378.6 4.3 %collective-permute-done.52 = bf16[1,288,512]{2,1,0:T(8,128)(2,1)S(1)} collective-permute-done((bf16[1,288,512]{2,1,0:T(8,128)(2,1)S(1)}, bf16[1,288,512]{2,1,0:T(8,128)(2,1)S(1)}, u32[]{:S(2)}, u32[]{:S(2)}) %collective-permute-start.52) | collective-permute-done | bytes 294944 | tf_op jit(solution)/shard_map/ppermute | solution.py:45
  397.1 7.9 %collective-permute-done.57 = bf16[4,64,512]{2,1,0:T(8,128)(2,1)S(1)} collective-permute-done((bf16[4,64,512]{2,1,0:T(8,128)(2,1)S(1)}, bf16[4,64,512]{2,1,0:T(8,128)(2,1)S(1)}, u32[]{:S(2)}, u32[]{:S(2)}) %collective-permute-start.57) | collective-permute-done | bytes 262176 | tf_op jit(solution)/shard_map/ppermute | solution.py:45
  411.4 4.2 collective-permute-done.65
  417.4 5.1 %collective-permute-done.64 = bf16[512,512]{1,0:T(8,128)(2,1)S(1)} collective-permute-done((bf16[512,512]{1,0:T(8,128)(2,1)S(1)}, bf16[512,512]{1,0:T(8,128)(2,1)S(1)}, u32[]{:S(2)}, u32[]{:S(2)}) %collective-permute-start.64) | collective-permute-done | bytes 524320 | tf_op jit(solution)/shard_map/ppermute | solution.py:40
  (505 shorter events, 221.4 us)
Async XLA Ops:
  55.7 25.8 %collective-permute-start.11 = (bf16[784,512]{1,0:T(8,128)(2,1)}, bf16[784,512]{1,0:T(8,128)(2,1)}, u32[]{:S(2)}, u32[]{:S(2)}) collective-permute-start(bf16[784,512]{1,0:T(8,128)(2,1)} %pad_maximum_fusion.18), channel_id=1, source_target_pairs={{0,4},{4,0},{1,5},{5,1},{2,6},{6,2},{3,7},{7,3},{8,12},{12,8},{9,1... | collective-permute-start | bytes 2408456 | tf_op jit(solution)/shard_map/ppermute | solution.py:40
  56.8 24.7 %collective-permute-start.12 = (bf16[256,512]{1,0:T(8,128)(2,1)S(1)}, bf16[256,512]{1,0:T(8,128)(2,1)S(1)}, u32[]{:S(2)}, u32[]{:S(2)}) collective-permute-start(bf16[256,512]{1,0:T(8,128)(2,1)S(1)} %bitcast.169), channel_id=1, source_target_pairs={{0,4},{4,0},{1,5},{5,1},{2,6},{6,2},{3,7},{7,3},{8,12},{12,8},{9,1... | collective-permute-start | bytes 786440 | tf_op jit(solution)/shard_map/ppermute | solution.py:40
  57.8 23.7 %collective-permute-start.13 = (bf16[2,288,512]{2,1,0:T(8,128)(2,1)}, bf16[2,288,512]{2,1,0:T(8,128)(2,1)S(1)}, u32[]{:S(2)}, u32[]{:S(2)}) collective-permute-start(bf16[2,288,512]{2,1,0:T(8,128)(2,1)} %pad_maximum_fusion.20), channel_id=1, source_target_pairs={{0,1},{1,0},{2,3},{3,2},{4,5},{5,4},{6,7},{7,6},{8,9},{9,8},{10,11... | collective-permute-start | bytes 1769480 | tf_op jit(solution)/shard_map/ppermute | solution.py:45
  64.1 24.5 %collective-permute-start.18 = (bf16[512,1024]{1,0:T(8,128)(2,1)}, bf16[512,1024]{1,0:T(8,128)(2,1)}, u32[]{:S(2)}, u32[]{:S(2)}) collective-permute-start(bf16[512,1024]{1,0:T(8,128)(2,1)} %pad_maximum_fusion.16), channel_id=1, source_target_pairs={{0,16},{8,24},{16,0},{24,8},{1,17},{9,25},{17,1},{25,9},{2,18},{10... | collective-permute-start | bytes 3145736 | tf_op jit(solution)/shard_map/ppermute | solution.py:28
  83.4 33.6 %collective-permute-start.15 = (bf16[2,288,512]{2,1,0:T(8,128)(2,1)S(1)}, bf16[2,288,512]{2,1,0:T(8,128)(2,1)S(1)}, u32[]{:S(2)}, u32[]{:S(2)}) collective-permute-start(bf16[2,288,512]{2,1,0:T(8,128)(2,1)S(1)} %pad_maximum_fusion.21), channel_id=1, source_target_pairs={{0,1},{1,0},{2,3},{3,2},{4,5},{5,4},{6,7},{7,6},{8,9},{9,8},{10,11... | collective-permute-start | bytes 1769480 | tf_op jit(solution)/shard_map/ppermute | solution.py:45
  86.8 30.2 %collective-permute-start.17 = (bf16[1152,512]{1,0:T(8,128)(2,1)S(1)}, bf16[1152,512]{1,0:T(8,128)(2,1)S(1)}, u32[]{:S(2)}, u32[]{:S(2)}) collective-permute-start(bf16[1152,512]{1,0:T(8,128)(2,1)S(1)} %bitcast.160), channel_id=1, source_target_pairs={{0,4},{4,0},{1,5},{5,1},{2,6},{6,2},{3,7},{7,3},{8,12},{12,8},{9,1... | collective-permute-start | bytes 3538952 | tf_op jit(solution)/shard_map/ppermute | solution.py:40
  90.4 26.6 %collective-permute-start.19 = (bf16[2,512,1024]{2,1,0:T(8,128)(2,1)S(1)}, bf16[2,512,1024]{2,1,0:T(8,128)(2,1)S(1)}, u32[]{:S(2)}, u32[]{:S(2)}) collective-permute-start(bf16[2,512,1024]{2,1,0:T(8,128)(2,1)S(1)} %pad_maximum_fusion.3), channel_id=1, source_target_pairs={{0,8},{8,0},{16,24},{24,16},{1,9},{9,1},{17,25},{25,17},{2,10},{10... | collective-permute-start | bytes 6291464 | tf_op jit(solution)/shard_map/ppermute | solution.py:28
  121.2 28.0 %collective-permute-start.25 = (bf16[1152,512]{1,0:T(8,128)(2,1)S(1)}, bf16[1152,512]{1,0:T(8,128)(2,1)S(1)}, u32[]{:S(2)}, u32[]{:S(2)}) collective-permute-start(bf16[1152,512]{1,0:T(8,128)(2,1)S(1)} %bitcast.163), channel_id=1, source_target_pairs={{0,4},{4,0},{1,5},{5,1},{2,6},{6,2},{3,7},{7,3},{8,12},{12,8},{9,1... | collective-permute-start | bytes 3538952 | tf_op jit(solution)/shard_map/ppermute | solution.py:40
  123.2 25.0 %collective-permute-start.23 = (bf16[512,1024]{1,0:T(8,128)(2,1)S(1)}, bf16[512,1024]{1,0:T(8,128)(2,1)S(1)}, u32[]{:S(2)}, u32[]{:S(2)}) collective-permute-start(bf16[512,1024]{1,0:T(8,128)(2,1)S(1)} %fusion.16), channel_id=1, source_target_pairs={{0,16},{8,24},{16,0},{24,8},{1,17},{9,25},{17,1},{25,9},{2,18},{10... | collective-permute-start | bytes 3145736 | tf_op jit(solution)/shard_map/ppermute | solution.py:28
  150.3 24.4 %collective-permute-start.27 = (bf16[512,1024]{1,0:T(8,128)(2,1)S(1)}, bf16[512,1024]{1,0:T(8,128)(2,1)S(1)}, u32[]{:S(2)}, u32[]{:S(2)}) collective-permute-start(bf16[512,1024]{1,0:T(8,128)(2,1)S(1)} %get-tuple-element.553), channel_id=1, source_target_pairs={{0,16},{8,24},{16,0},{24,8},{1,17},{9,25},{17,1},{25,9},{2,18},{10... | collective-permute-start | bytes 3145736 | tf_op jit(solution)/shard_map/ppermute | solution.py:28
  150.8 26.9 %collective-permute-start.26 = (bf16[1152,512]{1,0:T(8,128)(2,1)S(1)}, bf16[1152,512]{1,0:T(8,128)(2,1)S(1)}, u32[]{:S(2)}, u32[]{:S(2)}) collective-permute-start(bf16[1152,512]{1,0:T(8,128)(2,1)S(1)} %bitcast.166), channel_id=1, source_target_pairs={{0,4},{4,0},{1,5},{5,1},{2,6},{6,2},{3,7},{7,3},{8,12},{12,8},{9,1... | collective-permute-start | bytes 3538952 | tf_op jit(solution)/shard_map/ppermute | solution.py:40
  207.5 25.5 %collective-permute-start.30 = (bf16[512,1024]{1,0:T(8,128)(2,1)}, bf16[512,1024]{1,0:T(8,128)(2,1)}, u32[]{:S(2)}, u32[]{:S(2)}) collective-permute-start(bf16[512,1024]{1,0:T(8,128)(2,1)} %fusion.18), channel_id=1, source_target_pairs={{0,16},{8,24},{16,0},{24,8},{1,17},{9,25},{17,1},{25,9},{2,18},{10... | collective-permute-start | bytes 3145736 | tf_op jit(solution)/shard_map/ppermute | solution.py:28
  233.1 31.4 %collective-permute-start.35 = (bf16[512,1024]{1,0:T(8,128)(2,1)S(1)}, bf16[512,1024]{1,0:T(8,128)(2,1)S(1)}, u32[]{:S(2)}, u32[]{:S(2)}) collective-permute-start(bf16[512,1024]{1,0:T(8,128)(2,1)S(1)} %get-tuple-element.374), channel_id=1, source_target_pairs={{0,8},{8,0},{16,24},{24,16},{1,9},{9,1},{17,25},{25,17},{2,10},{10... | collective-permute-start | bytes 3145736 | tf_op jit(solution)/shard_map/ppermute | solution.py:28
  233.7 30.8 %collective-permute-start.36 = (bf16[512,1024]{1,0:T(8,128)(2,1)S(1)}, bf16[512,1024]{1,0:T(8,128)(2,1)S(1)}, u32[]{:S(2)}, u32[]{:S(2)}) collective-permute-start(bf16[512,1024]{1,0:T(8,128)(2,1)S(1)} %get-tuple-element.375), channel_id=1, source_target_pairs={{0,8},{8,0},{16,24},{24,16},{1,9},{9,1},{17,25},{25,17},{2,10},{10... | collective-permute-start | bytes 3145736 | tf_op jit(solution)/shard_map/ppermute | solution.py:28
  236.1 28.3 %collective-permute-start.34 = (bf16[512,1024]{1,0:T(8,128)(2,1)S(1)}, bf16[512,1024]{1,0:T(8,128)(2,1)S(1)}, u32[]{:S(2)}, u32[]{:S(2)}) collective-permute-start(bf16[512,1024]{1,0:T(8,128)(2,1)S(1)} %fusion.19), channel_id=1, source_target_pairs={{0,16},{8,24},{16,0},{24,8},{1,17},{9,25},{17,1},{25,9},{2,18},{10... | collective-permute-start | bytes 3145736 | tf_op jit(solution)/shard_map/ppermute | solution.py:28
  247.1 35.5 %collective-permute-start.33 = (bf16[1,576,1024]{2,1,0:T(8,128)(2,1)S(1)}, bf16[1,576,1024]{2,1,0:T(8,128)(2,1)}, u32[]{:S(2)}, u32[]{:S(2)}) collective-permute-start(bf16[1,576,1024]{2,1,0:T(8,128)(2,1)S(1)} %slice_bitcast_fusion.3), channel_id=1, source_target_pairs={{0,1},{1,0},{2,3},{3,2},{4,5},{5,4},{6,7},{7,6},{8,9},{9,8},{10,11... | collective-permute-start | bytes 3538952 | tf_op jit(solution)/shard_map/ppermute | solution.py:45
  254.7 27.9 %collective-permute-start.32 = (bf16[1152,512]{1,0:T(8,128)(2,1)S(1)}, bf16[1152,512]{1,0:T(8,128)(2,1)}, u32[]{:S(2)}, u32[]{:S(2)}) collective-permute-start(bf16[1152,512]{1,0:T(8,128)(2,1)S(1)} %get-tuple-element.367), channel_id=1, source_target_pairs={{0,4},{4,0},{1,5},{5,1},{2,6},{6,2},{3,7},{7,3},{8,12},{12,8},{9,1... | collective-permute-start | bytes 3538952 | tf_op jit(solution)/shard_map/ppermute | solution.py:40
  302.3 31.4 %collective-permute-start.39 = (bf16[512,1024]{1,0:T(8,128)(2,1)}, bf16[512,1024]{1,0:T(8,128)(2,1)}, u32[]{:S(2)}, u32[]{:S(2)}) collective-permute-start(bf16[512,1024]{1,0:T(8,128)(2,1)} %get-tuple-element.406), channel_id=1, source_target_pairs={{0,8},{8,0},{16,24},{24,16},{1,9},{9,1},{17,25},{25,17},{2,10},{10... | collective-permute-start | bytes 3145736 | tf_op jit(solution)/shard_map/ppermute | solution.py:28
  302.3 31.2 %collective-permute-start.40 = (bf16[512,1024]{1,0:T(8,128)(2,1)}, bf16[512,1024]{1,0:T(8,128)(2,1)}, u32[]{:S(2)}, u32[]{:S(2)}) collective-permute-start(bf16[512,1024]{1,0:T(8,128)(2,1)} %add_convert_fusion.2), channel_id=1, source_target_pairs={{0,16},{8,24},{16,0},{24,8},{1,17},{9,25},{17,1},{25,9},{2,18},{10... | collective-permute-start | bytes 3145736 | tf_op jit(solution)/shard_map/ppermute | solution.py:28
  302.8 30.6 %collective-permute-start.41 = (bf16[1152,512]{1,0:T(8,128)(2,1)}, bf16[1152,512]{1,0:T(8,128)(2,1)}, u32[]{:S(2)}, u32[]{:S(2)}) collective-permute-start(bf16[1152,512]{1,0:T(8,128)(2,1)} %get-tuple-element.408), channel_id=1, source_target_pairs={{0,4},{4,0},{1,5},{5,1},{2,6},{6,2},{3,7},{7,3},{8,12},{12,8},{9,1... | collective-permute-start | bytes 3538952 | tf_op jit(solution)/shard_map/ppermute | solution.py:40
  304.3 27.6 %collective-permute-start.42 = (bf16[1,576,512]{2,1,0:T(8,128)(2,1)}, bf16[1,576,512]{2,1,0:T(8,128)(2,1)}, u32[]{:S(2)}, u32[]{:S(2)}) collective-permute-start(bf16[1,576,512]{2,1,0:T(8,128)(2,1)} %fusion.25), channel_id=1, source_target_pairs={{0,1},{1,0},{2,3},{3,2},{4,5},{5,4},{6,7},{7,6},{8,9},{9,8},{10,11... | collective-permute-start | bytes 1769480 | tf_op jit(solution)/shard_map/ppermute | solution.py:45
  304.6 28.8 %collective-permute-start.43 = (bf16[1,288,1024]{2,1,0:T(8,128)(2,1)}, bf16[1,288,1024]{2,1,0:T(8,128)(2,1)}, u32[]{:S(2)}, u32[]{:S(2)}) collective-permute-start(bf16[1,288,1024]{2,1,0:T(8,128)(2,1)} %slice.528), channel_id=1, source_target_pairs={{0,2},{1,3},{2,0},{3,1},{4,6},{5,7},{6,4},{7,5},{8,10},{9,11},{10,... | collective-permute-start | bytes 1769480 | tf_op jit(solution)/shard_map/ppermute | solution.py:45
  338.9 26.2 %collective-permute-start.46 = (bf16[512,1024]{1,0:T(8,128)(2,1)S(1)}, bf16[512,1024]{1,0:T(8,128)(2,1)S(1)}, u32[]{:S(2)}, u32[]{:S(2)}) collective-permute-start(bf16[512,1024]{1,0:T(8,128)(2,1)S(1)} %add_convert_fusion.1), channel_id=1, source_target_pairs={{0,16},{8,24},{16,0},{24,8},{1,17},{9,25},{17,1},{25,9},{2,18},{10... | collective-permute-start | bytes 3145736 | tf_op jit(solution)/shard_map/ppermute | solution.py:28
  340.5 24.7 %collective-permute-start.47 = (bf16[1024,512]{1,0:T(8,128)(2,1)}, bf16[1024,512]{1,0:T(8,128)(2,1)S(1)}, u32[]{:S(2)}, u32[]{:S(2)}) collective-permute-start(bf16[1024,512]{1,0:T(8,128)(2,1)} %pad_maximum_fusion.17), channel_id=1, source_target_pairs={{0,4},{4,0},{1,5},{5,1},{2,6},{6,2},{3,7},{7,3},{8,12},{12,8},{9,1... | collective-permute-start | bytes 3145736 | tf_op jit(solution)/shard_map/ppermute | solution.py:40
  (139 other events, 1389.7 us)
